TPU v7x, 256 devices: a whole 4x4x8 slice. The times are simulated.
256 devices in a mesh: dp: 16 (over z, y_hi), tensor: 16 (over x, y_lo, core).
Axes of the slice: x: 4, y: 4 (y_hi: 2, y_lo: 2; y = y_hi * 2 + y_lo), z: 8, core: 2. Of those that a mesh axis runs over, the one named last changes fastest.
Arguments:
- tokens: bfloat16 [8192, 16384], P('dp', 'tensor'), may hold values from -6 to 6
- queries: bfloat16 [8192, 16384], P('dp', 'tensor'), as said below
- out_grad: bfloat16 [8192, 16384], P('dp', 'tensor'), may hold values from -6 to 6
- key_weight: bfloat16 [16384, 1024], P('tensor'), may hold values from -0.0625 to 0.0625
- value_weight: bfloat16 [16384, 1024], P('tensor'), may hold values from -0.0625 to 0.0625
- key_scale: float32 [32, 1024], replicated, may hold values from 0.1 to 1.9
- value_scale: float32 [32, 1024], replicated, may hold values from 0.1 to 1.9
- segment_ids: int32 [16, 512], P('dp'), may hold values from 0 to 3, never falling along the last dimension, each value on 1 to 256 neighbouring positions
- tenant_ids: int32 [16, 4], P('dp'), may hold values from 0 to 31
Outputs:
- input_grad: bfloat16 [8192, 16384], P('dp', 'tensor')
- key_scale_grad: float32 [32, 1024], P(None, 'tensor')
- value_scale_grad: float32 [32, 1024], P(None, 'tensor')
Inputs may be any that keep to these rules, and one draw needn't show every extreme that they name: `segment_ids`: in each token group the sequence number never falls, all 4 sequences are present, and the longest holds exactly 256 tokens. `queries`: entries lie between -160 and 160.
All inputs are finite; a program needn't handle non-finite values.
Results may differ from a plain program's by a relative error of at most 0.034.
The roundings to bfloat16 on the way count: a program that leaves them out, or rounds other values in their place, can miss the bound.
Values may be sent and summed in bfloat16 or wider, within the bound.
No kernel may reach another device: no remote copies, remote signals or barrier semaphores. Data moves between devices by JAX's collectives and lax.ppermute only.
A program may use at most 128 MiB of HBM per device.

v0:
```python
import jax
import jax.numpy as jnp
from jax import lax
from jax.sharding import PartitionSpec as P

SEQS = 4
NT = 32


def swapped(array, axis, bit):
    return lax.ppermute(array, axis, [(i, i ^ 1 << bit) for i in range(lax.axis_size(axis))])


def tenant_rows(segments, tenants):
    seq_match = segments[:, None] == jnp.arange(SEQS, dtype=jnp.int32)[None, :]
    tenant_tok = jnp.sum(jnp.where(seq_match, tenants[None, :], 0), axis=1)
    return (tenant_tok[:, None] == jnp.arange(NT, dtype=jnp.int32)[None, :]).astype(jnp.float32)


def allowed_mask(segments):
    position = jnp.arange(segments.shape[0], dtype=jnp.int32)
    return (segments[:, None] == segments[None, :]) & (position[None, :] <= position[:, None])


def head_grads(query_head, out_head, key_tile, value_tile, allowed):
    score_scale = key_tile.shape[1] ** (-0.5)
    scores = (
        lax.dot_general(
            query_head, key_tile, (((1,), (1,)), ((), ())), preferred_element_type=jnp.float32
        )
        * score_scale
    )
    scores = jnp.where(allowed, scores, -1e30)
    row_peak = jnp.max(scores, axis=1, keepdims=True)
    exp_scores = jnp.exp(scores - row_peak)
    probs = exp_scores / jnp.sum(exp_scores, axis=1, keepdims=True)
    probs_low = probs.astype(jnp.bfloat16)
    attended = jnp.dot(probs_low, value_tile, preferred_element_type=jnp.float32)
    row_delta = jnp.sum(out_head.astype(jnp.float32) * attended, axis=1, keepdims=True)
    prob_grad = lax.dot_general(
        out_head, value_tile, (((1,), (1,)), ((), ())), preferred_element_type=jnp.float32
    )
    score_grad = (probs * (prob_grad - row_delta)).astype(jnp.bfloat16)
    value_grad = lax.dot_general(
        probs_low, out_head, (((0,), (0,)), ((), ())), preferred_element_type=jnp.float32
    )
    key_grad = (
        lax.dot_general(
            score_grad, query_head, (((0,), (0,)), ((), ())), preferred_element_type=jnp.float32
        )
        * score_scale
    )
    return (key_grad, value_grad)


def contract_rows(left, weight):
    return lax.dot_general(
        left, weight, (((1,), (1,)), ((), ())), preferred_element_type=jnp.float32
    )


def on_device(
    tokens,
    queries,
    out_grad,
    key_weight,
    value_weight,
    key_scale,
    value_scale,
    segment_ids,
    tenant_ids,
):
    tensor_size = lax.axis_size("tensor")
    tensor_rank = lax.axis_index("tensor")
    member_bit = tensor_rank % 2
    head_width = key_scale.shape[1] * 2 // tensor_size
    half_width = head_width // 2
    token_count = tokens.shape[0]
    heads_here = queries.shape[1] // head_width
    tenant_hot = tenant_rows(segment_ids[0], tenant_ids[0])
    key_factor = jnp.dot(tenant_hot, key_scale, precision=lax.Precision.HIGHEST)
    value_factor = jnp.dot(tenant_hot, value_scale, precision=lax.Precision.HIGHEST)
    own_start = tensor_rank * half_width
    key_own_factor = lax.dynamic_slice_in_dim(key_factor, own_start, half_width, 1)
    value_own_factor = lax.dynamic_slice_in_dim(value_factor, own_start, half_width, 1)
    key_partial_sum = jnp.dot(tokens, key_weight, preferred_element_type=jnp.float32)
    value_partial_sum = jnp.dot(tokens, value_weight, preferred_element_type=jnp.float32)
    key_base, value_base = (
        lax.psum_scatter(key_partial_sum, "tensor", scatter_dimension=1, tiled=True),
        lax.psum_scatter(value_partial_sum, "tensor", scatter_dimension=1, tiled=True),
    )
    key_mine = (key_base * key_own_factor).astype(jnp.bfloat16)
    value_mine = (value_base * value_own_factor).astype(jnp.bfloat16)
    key_partner, value_partner = swapped((key_mine, value_mine), "tensor", 0)
    key_tile = jnp.where(
        member_bit == 0,
        jnp.concatenate([key_mine, key_partner], 1),
        jnp.concatenate([key_partner, key_mine], 1),
    )
    value_tile = jnp.where(
        member_bit == 0,
        jnp.concatenate([value_mine, value_partner], 1),
        jnp.concatenate([value_partner, value_mine], 1),
    )
    allowed = allowed_mask(segment_ids[0])

    def one_head(head_index, totals):
        column = head_index * head_width
        query_head = lax.dynamic_slice_in_dim(queries, column, head_width, 1)
        out_head = lax.dynamic_slice_in_dim(out_grad, column, head_width, 1)
        key_part, value_part = head_grads(query_head, out_head, key_tile, value_tile, allowed)
        return (totals[0] + key_part, totals[1] + value_part)

    zeros_tile = jnp.zeros((token_count, head_width), jnp.float32)
    key_partial, value_partial = lax.fori_loop(0, heads_here, one_head, (zeros_tile, zeros_tile))
    partials = jnp.concatenate([key_partial, value_partial], axis=1)
    gathered = lax.all_gather(partials.astype(jnp.bfloat16), "tensor", axis=1, tiled=True).astype(
        partials.dtype
    )
    shaped = gathered.reshape(token_count, tensor_size // 2, 2, 2, head_width)
    summed = jnp.sum(shaped, axis=2)
    key_grad = summed[:, :, 0, :].reshape(token_count, key_scale.shape[1])
    value_grad = summed[:, :, 1, :].reshape(token_count, key_scale.shape[1])
    key_low = (key_grad * key_factor).astype(jnp.bfloat16)
    value_low = (value_grad * value_factor).astype(jnp.bfloat16)
    input_grad = contract_rows(key_low, key_weight) + contract_rows(value_low, value_weight)
    key_grad_own = lax.dynamic_slice_in_dim(key_grad, own_start, half_width, 1)
    value_grad_own = lax.dynamic_slice_in_dim(value_grad, own_start, half_width, 1)
    key_tenant = lax.dot_general(
        tenant_hot,
        key_grad_own * key_base,
        (((0,), (0,)), ((), ())),
        precision=lax.Precision.HIGHEST,
    )
    value_tenant = lax.dot_general(
        tenant_hot,
        value_grad_own * value_base,
        (((0,), (0,)), ((), ())),
        precision=lax.Precision.HIGHEST,
    )
    key_total, value_total = lax.psum((key_tenant, value_tenant), "dp")
    return (input_grad.astype(jnp.bfloat16), key_total, value_total)


def solution(mesh):
    return jax.shard_map(
        on_device,
        mesh=mesh,
        in_specs=(
            P("dp", "tensor"),
            P("dp", "tensor"),
            P("dp", "tensor"),
            P("tensor", None),
            P("tensor", None),
            P(),
            P(),
            P("dp", None),
            P("dp", None),
        ),
        out_specs=(P("dp", "tensor"), P(None, "tensor"), P(None, "tensor")),
        check_vma=False,
    )
```

profile of v0, /device:TPU:2, one launch (start us, length us, event | category | flops | bytes accessed | tf_op | source)
XLA Modules:
  0.0 408.8 jit_solution(9903915651289847543)
XLA Ops:
  7.2 4.7 %fusion.40 = f32[512,1024]{0,1:T(8,128)} fusion(bf16[512,1024]{1,0:T(8,128)(2,1)} %param.11, bf16[1024,1024]{1,0:T(8,128)(2,1)} %param.15), kind=kOutput, calls=%fused_computation.54 | convolution fusion | flops 1073741824 | bytes 5242880 | tf_op jit(solution)/shard_map/dot_general | solution.py:87
  12.0 1.1 copy-done.13
  13.1 2.6 fusion.39
  16.7 2.5 fusion.21
  19.1 2.4 fusion.22
  21.6 52.8 %reduce-scatter.5.cloned.1.call-done = f32[512,64]{0,1:T(8,128)} async-done(((f32[512,1024]{0,1:T(8,128)}), f32[512,64]{0,1:T(8,128)}) %reduce-scatter.5.cloned.1.call-update) | async-done | bytes 131088 | tf_op jit(solution)/shard_map/reduce_scatter | solution.py:90
  74.4 1.0 multiply_convert_fusion.4
  75.4 66.4 %reduce-scatter.3.cloned.1.call-done = f32[512,64]{0,1:T(8,128)} async-done(((f32[512,1024]{0,1:T(8,128)}), f32[512,64]{0,1:T(8,128)}) %reduce-scatter.3.cloned.1.call-update) | async-done | bytes 131088 | tf_op jit(solution)/shard_map/reduce_scatter | solution.py:89
  141.8 1.0 multiply_convert_fusion.5
  145.1 70.3 %while.16 = (s32[]{:T(128)}, f32[512,128]{1,0:T(8,128)}, f32[512,128]{1,0:T(8,128)S(1)}, bf16[512,1024]{1,0:T(8,128)(2,1)}, bf16[512,128]{1,0:T(8,128)(2,1)}, /*...) while((s32[]{:T(128)}, f32[512,128]{1,0:T(8,128)}, ...), condition=%wide.region_7.8_spmd.clone, body=%wide.region_3.7_spmd.clone.sunk | while | flops 340261376 | bytes 11557142 | solution.py:115
  145.1 0.9 constant_dynamic-slice_fusion.2
  146.8 1.4 fusion.77
  148.6 0.8 copy-done.1
  149.3 0.9 fusion.80
  150.2 2.2 fusion.81
  152.4 1.4 convolution_add_fusion.2
  153.8 0.9 constant_dynamic-slice_fusion.2
  155.5 1.4 fusion.77
  157.3 0.8 copy-done.1
  158.0 0.9 fusion.80
  158.9 2.3 fusion.81
  161.2 1.4 convolution_add_fusion.2
  162.6 0.9 constant_dynamic-slice_fusion.2
  164.3 1.4 fusion.77
  166.1 0.8 copy-done.1
  166.9 0.9 fusion.80
  167.7 2.3 fusion.81
  170.1 1.4 convolution_add_fusion.2
  171.4 0.9 constant_dynamic-slice_fusion.2
  173.1 1.4 fusion.77
  175.7 0.9 fusion.80
  176.5 2.3 fusion.81
  178.9 1.4 convolution_add_fusion.2
  180.3 0.9 constant_dynamic-slice_fusion.2
  181.9 1.4 fusion.77
  184.5 0.9 fusion.80
  185.3 2.3 fusion.81
  187.7 1.4 convolution_add_fusion.2
  189.1 0.9 constant_dynamic-slice_fusion.2
  190.7 1.4 fusion.77
  193.3 0.9 fusion.80
  194.1 2.3 fusion.81
  196.5 1.4 convolution_add_fusion.2
  197.9 0.9 constant_dynamic-slice_fusion.2
  199.6 1.4 fusion.77
  202.1 0.9 fusion.80
  203.0 2.3 fusion.81
  205.3 1.4 convolution_add_fusion.2
  206.7 0.9 constant_dynamic-slice_fusion.2
  208.4 1.4 fusion.77
  210.9 0.9 fusion.80
  211.8 2.3 fusion.81
  214.1 1.4 convolution_add_fusion.2
  215.5 1.0 convert.7
  217.2 53.3 %all-gather.2.cloned.1.call-done = bf16[512,4096]{1,0:T(8,128)(2,1)} async-done(((bf16[512,256]{1,0:T(8,128)(2,1)}), bf16[512,4096]{1,0:T(8,128)(2,1)}) %all-gather.2.cloned.1.call-update) | async-done | bytes 4194320 | tf_op jit(solution)/shard_map/all_gather | solution.py:117
  270.5 11.6 %reshape.20 = f32[512,8,2,2,128]{4,3,2,1,0:T(2,128)} reshape(bf16[512,4096]{1,0:T(8,128)(2,1)} %all-gather.2.cloned.1.call-done) | data formatting | bytes 12582912 | tf_op jit(solution)/shard_map/reshape | solution.py:120
  282.1 13.6 %reduce_sum.45 = f32[512,8,2,128]{3,2,1,0:T(2,128)} reduce(f32[512,8,2,2,128]{4,3,2,1,0:T(2,128)} %reshape.20, f32[]{:T(128)} %constant.72.clone.1), dimensions={2}, to_apply=%region_8.9 | reduce | flops 1048576 | bytes 12582916 | tf_op jit(solution)/shard_map/reduce_sum | solution.py:121
  295.7 9.0 %fusion.38 = (f32[512,8,1,128]{3,2,1,0:T(1,128)}, f32[512,8,1,128]{3,2,1,0:T(1,128)}) fusion(f32[512,8,2,128]{3,2,1,0:T(2,128)} %reduce_sum.45), kind=kLoop, calls=%fused_computation.52 | loop fusion | bytes 8388608 | tf_op jit(solution)/shard_map/slice | solution.py:123
  304.7 6.0 %copy.34 = f32[512,8,1,128]{0,3,1,2:T(8,128)} copy(f32[512,8,1,128]{3,2,1,0:T(1,128)} %get-tuple-element.219) | data formatting | bytes 4194304 | tf_op jit(solution)/shard_map/slice | solution.py:123
  310.7 6.0 %copy.32 = f32[512,8,1,128]{0,3,1,2:T(8,128)} copy(f32[512,8,1,128]{3,2,1,0:T(1,128)} %get-tuple-element.220) | data formatting | bytes 4194304 | tf_op jit(solution)/shard_map/slice | solution.py:122
  316.7 3.7 fusion.19
  320.9 2.3 add_convert_fusion
  323.6 1.3 fusion.25
  324.8 77.4 %all-reduce = (f32[32,64]{1,0:T(8,128)}, f32[32,64]{1,0:T(8,128)}) all-reduce(f32[32,64]{1,0:T(8,128)S(1)} %fusion.25, f32[32,64]{1,0:T(8,128)S(1)} %fusion.23), channel_id=1, replica_groups=mesh['dp'=16,'tensor'=16] {'dp'}, use_global_device_ids=true, to_apply=%region_9.10 | all-reduce | flops 4096 | bytes 32768 | tf_op jit(solution)/shard_map/psum | solution.py:141
  (110 shorter events, 17.9 us)
Async XLA Ops:
  7.2 4.8 %copy-start = (bf16[1024,1024]{1,0:T(8,128)(2,1)S(1)}, bf16[1024,1024]{1,0:T(8,128)(2,1)}, u32[]{:S(2)}) copy-start(bf16[1024,1024]{1,0:T(8,128)(2,1)} %param.14) | copy-start | bytes 6291460
  7.2 67.2 %reduce-scatter.5.cloned.1.call-start = ((), (), s32[]{:S(2)}) async-start(), calls=%async_computation.3 | async-start | bytes 2228224 | tf_op jit(solution)/shard_map/reduce_scatter | solution.py:90
  11.9 1.2 copy-start.13
  11.9 129.9 %reduce-scatter.3.cloned.1.call-start = ((), (), s32[]{:S(2)}) async-start(), calls=%async_computation.2 | async-start | bytes 2228224 | tf_op jit(solution)/shard_map/reduce_scatter | solution.py:89
  15.7 0.7 copy-start.11
  15.7 0.7 copy-start.12
  15.7 0.9 copy-start.8
  15.7 3.4 copy-start.9
  15.8 254.7 %all-gather.2.cloned.1.call-start = ((), (), s32[]{:S(2)}) async-start(), calls=%async_computation.4 | async-start | bytes 4456448 | tf_op jit(solution)/shard_map/all_gather | solution.py:117
  75.3 67.8 %collective-permute-start.1 = (bf16[512,64]{0,1:T(8,128)(2,1)S(1)}, bf16[512,64]{0,1:T(8,128)(2,1)S(1)}, u32[]{:S(2)}, u32[]{:S(2)}) collective-permute-start(bf16[512,64]{0,1:T(8,128)(2,1)S(1)} %multiply_convert_fusion.4), channel_id=1, source_target_pairs={{0,1},{1,0},{2,3},{3,2},{4,5},{5,4},{6,7},{7,6},{8,9},{9,8},{10,11... | collective-permute-start | bytes 196616 | tf_op jit(solution)/shard_map/ppermute | solution.py:11
  142.8 1.5 collective-permute-start
  146.8 2.5 copy-start.4
  146.8 2.5 copy-start.10
  148.5 0.8 copy-start.1
  155.5 2.5 copy-start.4
  155.5 2.5 copy-start.10
  157.2 0.8 copy-start.1
  164.3 2.5 copy-start.4
  164.3 2.5 copy-start.10
  166.1 0.8 copy-start.1
  173.1 2.5 copy-start.4
  173.1 2.5 copy-start.10
  174.9 0.8 copy-start.1
  181.9 2.5 copy-start.4
  181.9 2.5 copy-start.10
  183.7 0.8 copy-start.1
  190.7 2.5 copy-start.4
  190.7 2.5 copy-start.10
  192.5 0.8 copy-start.1
  199.6 2.5 copy-start.4
  199.6 2.5 copy-start.10
  201.3 0.8 copy-start.1
  208.4 2.5 copy-start.4
  208.4 2.5 copy-start.10
  210.1 0.8 copy-start.1
  316.7 3.7 copy-start.2
  316.7 3.7 copy-start.3
  316.7 4.1 %copy-start.5 = (bf16[1024,1024]{1,0:T(8,128)(2,1)S(1)}, bf16[1024,1024]{1,0:T(8,128)(2,1)}, u32[]{:S(2)}) copy-start(bf16[1024,1024]{1,0:T(8,128)(2,1)} %param.15) | copy-start | bytes 6291460
  320.9 2.3 copy-start.6
  320.9 2.7 copy-start.7
Sparse Core Ops, SparseCore 0:
  12.1 62.2 reduce-scatter.4
  76.9 64.9 reduce-scatter.2
  217.3 53.1 all-gather.1
where the time goes:
time: 411 us; the launch traced here: 409 us
  waiting for transfers between devices  173 us (42%)
  blocking collectives  77.4 us (19%)
  matrix products  67.1 us (16%)
  local copies, waits for them, and re-layouts  56.2 us (14%)
  other arithmetic  20.3 us (5%)
  between operations  13.9 us (3%)
    psum x1, blocking collectives, on_device(): key_total, value_total = lax.psum((key_tenant, value_tenant), 'dp')  77.4 us
    reduce_scatter x1, waiting for transfers between devices, on_device(): lax.psum_scatter(key_partial_sum, 'tensor', scatter_dimension=1, tiled=True)  66.4 us
    all_gather x1, waiting for transfers between devices, on_device(): lax.all_gather(partials.astype(jnp.bfloat16), 'tensor', axis=1, tiled=True)  53.3 us
    reduce_scatter x1, waiting for transfers between devices, on_device(): lax.psum_scatter(value_partial_sum, 'tensor', scatter_dimension=1, tiled=...  52.8 us
    dot_general x8, matrix products, head_grads(): lax.dot_general(score_grad, query_head, (((0,), (0,)), ((), ())), preferr...  18.6 us
    slice x2, local copies, waits for them, and re-layouts, on_device(): value_grad = summed[:, :, 1, :].reshape(token_count, key_scale.shape[1])  15.1 us
    reduce_sum x1, other arithmetic, on_device(): summed = jnp.sum(shaped, axis=2)  13.6 us
    dynamic_slice x16, local copies, waits for them, and re-layouts, one_head(): out_head = lax.dynamic_slice_in_dim(out_grad, column, head_width, 1)  13.4 us
  transfers between devices with their start and end apart: 5, of which 4 were waited for; matrix products, arithmetic and copies ran while one was open for 3% of the time, Pallas kernels for 0%

commit v1 on v0

v1 whole, which is shorter than its diff:
```python
import functools

import jax
import jax.numpy as jnp
from jax import lax
from jax.experimental import pallas as pl
from jax.experimental.pallas import tpu as pltpu
from jax.sharding import PartitionSpec as P

SEQS = 4
NT = 32
HEAD = 128
TOK = 512
HALF = 256
CHIPS = 8
BLOCK = 128
LOG2E = 1.4426950408889634
SCALE = HEAD**-0.5
BF = jnp.bfloat16
F32 = jnp.float32
VMEM_BYTES = 48 * 1024 * 1024


def params():
    return pltpu.CompilerParams(vmem_limit_bytes=VMEM_BYTES)


def device_index(x, y, core):
    return (x % 4 * 2 + y) * 2 + core


def tensor_pairs(step):
    places = [(x, y, core) for x in range(4) for y in range(2) for core in range(2)]
    return [(device_index(*place), device_index(*step(*place))) for place in places]


CORE_SWAP = tensor_pairs(lambda x, y, core: (x, y, core ^ 1))
SAME_CORE = [[chip * 2 + core for chip in range(CHIPS)] for core in range(2)]


def project_body(place, tok_send, tok_keep, kw, vw, send, keep, rows):
    @pl.when(pl.program_id(0) == 0)
    def _():
        rows[:HALF] = tok_send[...]
        rows[HALF:] = tok_keep[...]

    for part, weight in enumerate((kw, vw)):
        total = jnp.dot(rows[...], weight[...], preferred_element_type=F32)
        for head in range(2):
            block = total[:, head * HEAD : (head + 1) * HEAD]
            columns = slice(part * HEAD, (part + 1) * HEAD)
            send[head, :, columns] = block[:HALF]
            keep[head, :, columns] = block[HALF:]


def project(place, tokens, key_weight, value_weight):
    depth = tokens.shape[1]
    out = jax.ShapeDtypeStruct((CHIPS, HALF, 2 * HEAD), F32)
    return pl.pallas_call(
        project_body,
        grid_spec=pltpu.PrefetchScalarGridSpec(
            num_scalar_prefetch=1,
            grid=(CHIPS // 2,),
            in_specs=[
                pl.BlockSpec((HALF, depth), lambda i, place: (1 - place[0], 0)),
                pl.BlockSpec((HALF, depth), lambda i, place: (place[0], 0)),
                pl.BlockSpec((depth, 2 * HEAD), lambda i, place: (0, i)),
                pl.BlockSpec((depth, 2 * HEAD), lambda i, place: (0, i)),
            ],
            out_specs=[
                pl.BlockSpec((2, HALF, 2 * HEAD), lambda i, place: (i, 0, 0)),
                pl.BlockSpec((2, HALF, 2 * HEAD), lambda i, place: (i, 0, 0)),
            ],
            scratch_shapes=[pltpu.VMEM((TOK, depth), BF)],
        ),
        out_shape=(out, out),
        compiler_params=params(),
        name="project",
    )(place, tokens, tokens, key_weight, value_weight)


def pack_body(keep, recv, out):
    total = keep[...] + recv[...]
    key = total[:, :, :HEAD]
    high = key.astype(BF)
    out[:, :, :HEAD] = high
    out[:, :, HEAD : 2 * HEAD] = (key - high.astype(F32)).astype(BF)
    out[:, :, 2 * HEAD :] = total[:, :, HEAD:].astype(BF)


def pack(keep, recv):
    return pl.pallas_call(
        pack_body,
        grid=(CHIPS // 2,),
        in_specs=[pl.BlockSpec((2, HALF, 2 * HEAD), lambda i: (i, 0, 0))] * 2,
        out_specs=pl.BlockSpec((2, HALF, 3 * HEAD), lambda i: (i, 0, 0)),
        out_shape=jax.ShapeDtypeStruct((CHIPS, HALF, 3 * HEAD), BF),
        compiler_params=params(),
        name="pack",
    )(keep, recv)


def own_sequences(place):
    row = lax.broadcasted_iota(jnp.int32, (HALF, HEAD), 0) + place[0] * HALF
    found = [row >= place[1 + seq] for seq in range(1, SEQS)]
    return found


def token_factor(place, scale, sequences):
    rows = [scale[pl.ds(place[5 + seq], 1), :] for seq in range(SEQS)]
    factor = jnp.broadcast_to(rows[0], (HALF, HEAD))
    for seq in range(1, SEQS):
        factor = jnp.where(sequences[seq - 1], rows[seq], factor)
    return factor


def finish_body(place, parts, key_scale, value_scale, base, low):
    total = parts[0].astype(F32)
    for chip in range(1, CHIPS):
        total = total + parts[chip].astype(F32)
    sequences = own_sequences(place)
    key = total[:, :HEAD] + total[:, HEAD : 2 * HEAD]
    value = total[:, 2 * HEAD :]
    base[:, :HEAD] = key
    base[:, HEAD:] = value
    low[:, :HEAD] = (key * token_factor(place, key_scale, sequences)).astype(BF)
    low[:, HEAD:] = (value * token_factor(place, value_scale, sequences)).astype(BF)


def finish(place, parts, key_scale, value_scale):
    scale_spec = pl.BlockSpec((NT, HEAD), lambda i, place: (0, place[9]))
    whole = pl.BlockSpec((HALF, 2 * HEAD), lambda i, place: (0, 0))
    return pl.pallas_call(
        finish_body,
        grid_spec=pltpu.PrefetchScalarGridSpec(
            num_scalar_prefetch=1,
            grid=(1,),
            in_specs=[
                pl.BlockSpec((CHIPS, HALF, 3 * HEAD), lambda i, place: (0, 0, 0)),
                scale_spec,
                scale_spec,
            ],
            out_specs=[whole, whole],
        ),
        out_shape=(
            jax.ShapeDtypeStruct((HALF, 2 * HEAD), F32),
            jax.ShapeDtypeStruct((HALF, 2 * HEAD), BF),
        ),
        compiler_params=params(),
        name="finish",
    )(place, parts, key_scale, value_scale)


def contract_last(left, right):
    return lax.dot_general(left, right, (((1,), (1,)), ((), ())), preferred_element_type=F32)


def attention_body(place, mine, other, queries, out_grad, send, keep, tile, grads):
    core = place[0]
    own_rows = pl.ds(pl.multiple_of(core * HALF, HALF), HALF)
    other_rows = pl.ds(pl.multiple_of((1 - core) * HALF, HALF), HALF)
    tile[own_rows, :] = mine[...]
    tile[other_rows, :] = other[...]
    grads[...] = jnp.zeros_like(grads)
    heads = queries.shape[1] // HEAD
    for block in range(TOK // BLOCK):
        first = max(0, block - 2) * BLOCK
        reach = (block + 1) * BLOCK - first
        rows = slice(block * BLOCK, (block + 1) * BLOCK)
        visible = slice(first, first + reach)
        key_row = lax.broadcasted_iota(jnp.int32, (reach, BLOCK), 0) + first
        query_row = lax.broadcasted_iota(jnp.int32, (reach, BLOCK), 1) + block * BLOCK
        start = jnp.zeros((reach, BLOCK), jnp.int32)
        for seq in range(1, SEQS):
            start = jnp.where(query_row >= place[1 + seq], place[1 + seq], start)
        allowed = (key_row >= start) & (key_row <= query_row)
        bias = jnp.where(allowed, 0.0, -1e30).astype(F32)
        bias = jnp.concatenate([bias, bias], axis=1)
        key_tile = tile[visible, :HEAD]
        value_tile = tile[visible, HEAD:]
        key_total = jnp.zeros((reach, HEAD), F32)
        value_total = jnp.zeros((reach, HEAD), F32)
        for pair in range(heads // 2):
            columns = [slice(h * HEAD, (h + 1) * HEAD) for h in (2 * pair, 2 * pair + 1)]
            query = jnp.concatenate([queries[rows, c] for c in columns], axis=0)
            out = jnp.concatenate([out_grad[rows, c] for c in columns], axis=0)
            scores = contract_last(key_tile, query) + bias
            peak = jnp.max(scores, axis=0, keepdims=True)
            exps = jnp.exp2((scores - peak) * (SCALE * LOG2E))
            probs = exps * (1.0 / jnp.sum(exps, axis=0, keepdims=True))
            probs_low = probs.astype(BF)
            prob_grad = contract_last(value_tile, out)
            delta = jnp.sum(probs_low.astype(F32) * prob_grad, axis=0, keepdims=True)
            score_grad = (probs * (prob_grad - delta)).astype(BF)
            value_total += jnp.dot(probs_low, out, preferred_element_type=F32)
            key_total += jnp.dot(score_grad, query, preferred_element_type=F32)
        grads[visible, :HEAD] += key_total
        grads[visible, HEAD:] += value_total
    for rows, target in ((other_rows, send), (own_rows, keep)):
        target[:, :HEAD] = grads[rows, :HEAD] * SCALE
        target[:, HEAD:] = grads[rows, HEAD:]


def attention(place, mine, other, queries, out_grad):
    out = jax.ShapeDtypeStruct((HALF, 2 * HEAD), F32)
    vmem = pl.BlockSpec(memory_space=pltpu.VMEM)
    return pl.pallas_call(
        attention_body,
        in_specs=[pl.BlockSpec(memory_space=pltpu.SMEM)] + [vmem] * 4,
        out_specs=[vmem, vmem],
        out_shape=(out, out),
        scratch_shapes=[pltpu.VMEM((TOK, 2 * HEAD), BF), pltpu.VMEM((TOK, 2 * HEAD), F32)],
        compiler_params=params(),
        name="attention",
    )(place, mine, other, queries, out_grad)


def scale_body(place, keep, recv, base, key_scale, value_scale, low, sums):
    sequences = own_sequences(place)
    for part, scale in enumerate((key_scale, value_scale)):
        columns = slice(part * HEAD, (part + 1) * HEAD)
        grad = keep[:, columns] + recv[:, columns]
        low[:, columns] = (grad * token_factor(place, scale, sequences)).astype(BF)
        product = grad * base[:, columns]
        later = [jnp.sum(product, axis=0, keepdims=True)]
        for seq in range(1, SEQS):
            later.append(jnp.sum(jnp.where(sequences[seq - 1], product, 0.0), axis=0, keepdims=True))
        later.append(jnp.zeros_like(later[0]))
        row = lax.broadcasted_iota(jnp.int32, (NT, HEAD), 0)
        table = jnp.zeros((NT, HEAD), F32)
        for seq in range(SEQS):
            table = table + jnp.where(row == place[5 + seq], later[seq] - later[seq + 1], 0.0)
        sums[:, columns] = table


def scale_grads(place, keep, recv, base, key_scale, value_scale):
    scale_spec = pl.BlockSpec((NT, HEAD), lambda i, place: (0, place[9]))
    whole = pl.BlockSpec((HALF, 2 * HEAD), lambda i, place: (0, 0))
    return pl.pallas_call(
        scale_body,
        grid_spec=pltpu.PrefetchScalarGridSpec(
            num_scalar_prefetch=1,
            grid=(1,),
            in_specs=[whole, whole, whole, scale_spec, scale_spec],
            out_specs=[whole, pl.BlockSpec((NT, 2 * HEAD), lambda i, place: (0, 0))],
        ),
        out_shape=(
            jax.ShapeDtypeStruct((HALF, 2 * HEAD), BF),
            jax.ShapeDtypeStruct((NT, 2 * HEAD), F32),
        ),
        compiler_params=params(),
        name="scale_grads",
    )(place, keep, recv, base, key_scale, value_scale)


def input_body(place, mine, other, kw, vw, out):
    core = place[0]
    for index, source in ((core, mine), (1 - core, other)):
        total = jnp.zeros((HALF, out.shape[1]), F32)
        for part, weight in enumerate((kw, vw)):
            left = jnp.concatenate(
                [source[chip, :, part * HEAD : (part + 1) * HEAD] for chip in range(CHIPS)], axis=1
            )
            total += contract_last(left, weight[...])
        out[pl.ds(pl.multiple_of(index * HALF, HALF), HALF), :] = total.astype(BF)


def input_grads(place, mine, other, key_weight, value_weight):
    features = key_weight.shape[0]
    width = features // 4
    gathered = pl.BlockSpec((CHIPS, HALF, 2 * HEAD), lambda i, place: (0, 0, 0))
    weight = pl.BlockSpec((width, CHIPS * HEAD), lambda i, place: (i, 0))
    return pl.pallas_call(
        input_body,
        grid_spec=pltpu.PrefetchScalarGridSpec(
            num_scalar_prefetch=1,
            grid=(4,),
            in_specs=[gathered, gathered, weight, weight],
            out_specs=pl.BlockSpec((TOK, width), lambda i, place: (0, i)),
        ),
        out_shape=jax.ShapeDtypeStruct((TOK, features), BF),
        compiler_params=params(),
        name="input_grads",
    )(place, mine, other, key_weight, value_weight)


def core_swap(array):
    return lax.ppermute(array, "tensor", CORE_SWAP)


def chip_exchange(array):
    return lax.all_to_all(array, "tensor", 0, 0, axis_index_groups=SAME_CORE, tiled=True)


def on_device(
    tokens,
    queries,
    out_grad,
    key_weight,
    value_weight,
    key_scale,
    value_scale,
    segment_ids,
    tenant_ids,
):
    rank = lax.axis_index("tensor")
    core, chip = rank % 2, rank // 2
    before = segment_ids[0][None, :] < jnp.arange(SEQS, dtype=jnp.int32)[:, None]
    starts = jnp.sum(before.astype(jnp.int32), axis=1)
    place = jnp.concatenate(
        [core.reshape(1), starts, tenant_ids[0], chip.reshape(1)]
    ).astype(jnp.int32)
    send, keep = project(place, tokens, key_weight, value_weight)
    packed = pack(keep, core_swap(send))
    base, low = finish(place, chip_exchange(packed), key_scale, value_scale)
    send, keep = attention(place, low, core_swap(low), queries, out_grad)
    grad_low, sums = scale_grads(place, keep, core_swap(send), base, key_scale, value_scale)
    spread = jnp.broadcast_to(grad_low[None], (CHIPS,) + grad_low.shape)
    gathered = chip_exchange(spread)
    input_grad = input_grads(place, gathered, core_swap(gathered), key_weight, value_weight)
    quarter = HEAD // 2
    halves = [lax.dynamic_slice_in_dim(sums, p * HEAD + core * quarter, quarter, 1) for p in (0, 1)]
    gives = [
        lax.dynamic_slice_in_dim(sums, p * HEAD + (1 - core) * quarter, quarter, 1) for p in (0, 1)
    ]
    own = jnp.concatenate(halves, axis=1) + core_swap(jnp.concatenate(gives, axis=1))
    for bit in range(4):
        own = own + lax.ppermute(own, "dp", [(i, i ^ 1 << bit) for i in range(16)])
    return input_grad, own[:, :quarter], own[:, quarter:]


def solution(mesh):
    return jax.shard_map(
        on_device,
        mesh=mesh,
        in_specs=(
            P("dp", "tensor"),
            P("dp", "tensor"),
            P("dp", "tensor"),
            P("tensor", None),
            P("tensor", None),
            P(),
            P(),
            P("dp", None),
            P("dp", None),
        ),
        out_specs=(P("dp", "tensor"), P(None, "tensor"), P(None, "tensor")),
        check_vma=False,
    )
```

time: 411 us -> 102 us (0.25)
  the two profiles are of different devices: /device:TPU:2 before, /device:TPU:16 now
where the time goes in v1:
time: 102 us; the launch traced here: 101 us
  blocking collectives  44.9 us (44%)
  Pallas kernels  19.6 us (19%)
  waiting for transfers between devices  18.7 us (18%)
  starting transfers between devices  13.6 us (13%)
  local copies, waits for them, and re-layouts  2.1 us (2%)
  other arithmetic  1.7 us (2%)
    all_to_all x2, blocking collectives, chip_exchange(): lax.all_to_all(array, 'tensor', 0, 0, axis_index_groups=SAME_CORE, tiled=...  44.9 us
    ppermute x4, starting transfers between devices, on_device(): own = own + lax.ppermute(own, 'dp', [(i, i ^ 1 << bit) for i in range(16)])  12.7 us
    ppermute x4, waiting for transfers between devices, on_device(): own = own + lax.ppermute(own, 'dp', [(i, i ^ 1 << bit) for i in range(16)])  9.87 us
    ppermute x5, waiting for transfers between devices, core_swap(): return lax.ppermute(array, 'tensor', CORE_SWAP)  8.84 us
    pallas_call x1, Pallas kernels, attention(): pl.pallas_call(attention_body, in_specs=[pl.BlockSpec(memory_space=pltpu....  6.16 us
    pallas_call x1, Pallas kernels, input_grads(): pl.pallas_call(input_body, grid_spec=pltpu.PrefetchScalarGridSpec(num_sca...  6.11 us
    pallas_call x1, Pallas kernels, project(): pl.pallas_call(project_body, grid_spec=pltpu.PrefetchScalarGridSpec(num_s...  5.28 us
  transfers between devices with their start and end apart: 9, of which 8 were waited for; matrix products, arithmetic and copies ran while one was open for 1% of the time, Pallas kernels for 0%

profile of v1, /device:TPU:16, one launch (start us, length us, event | category | flops | bytes accessed | tf_op | source)
XLA Modules:
  0.0 101.5 jit_solution(9568246165433940718)
XLA Ops:
  0.6 0.8 convert_reduce_fusion
  1.5 0.7 pad_add_fusion.place
  2.2 0.0 copy-start.1
  2.2 1.2 %copy-done.1 = bf16[512,1024]{1,0:T(8,128)(2,1)S(1)} copy-done((bf16[512,1024]{1,0:T(8,128)(2,1)S(1)}, bf16[512,1024]{1,0:T(8,128)(2,1)}, u32[]{:S(2)}) %copy-start.1) | copy-done | bytes 1048600
  3.4 5.3 %project.1 = (f32[8,256,256]{2,1,0:T(8,128)S(1)}, f32[8,256,256]{2,1,0:T(8,128)S(1)}) custom-call(s32[10]{0:T(128)S(1)} %pad_add_fusion.place, bf16[512,1024]{1,0:T(8,128)(2,1)S(1)} %copy-done.1, bf16[512,1024]{1,0:T(8,128)(2,1)S(1)} %copy-done.1, bf16[1024,1024]{1,0:T(8,128)(2,1)} %kw.3, bf16[1024,1024]{1,0:T(8,128)(2,1)} %vw.3), custom_call_target="tpu_custom_call" | custom-call | tf_op jit(solution)/shard_map/project/pallas_call | solution.py:59
  8.7 0.1 collective-permute-start
  8.8 4.1 %collective-permute-done.recv = f32[8,256,256]{2,1,0:T(8,128)S(1)} collective-permute-done((f32[8,256,256]{2,1,0:T(8,128)S(1)}, f32[8,256,256]{2,1,0:T(8,128)S(1)}, u32[]{:S(2)}, u32[]{:S(2)}) %collective-permute-start) | collective-permute-done | bytes 2097184 | tf_op jit(solution)/shard_map/ppermute | solution.py:288
  12.9 0.4 pack.1
  13.3 0.0 copy-start.4
  13.3 0.0 copy-start.5
  13.3 0.0 copy-start.2
  13.4 0.0 copy-start.3
  13.4 26.2 %all_to_all.10.parts = bf16[8,256,384]{2,1,0:T(8,128)(2,1)S(1)} all-to-all(bf16[8,256,384]{2,1,0:T(8,128)(2,1)S(1)} %pack.1), channel_id=1, replica_groups={{0,2,4,6,8,10,12,14},{1,3,5,7,9,11,13,15},{16,18,20,22,24,26,28,30},{17..., dimensions={0} | all-to-all | bytes 3145728 | tf_op jit(solution)/shard_map/all_to_all | solution.py:292
  39.6 0.0 copy-done.4
  39.6 0.0 copy-done.5
  39.6 0.9 finish.1
  40.5 0.1 collective-permute-start.1
  40.6 1.3 %collective-permute-done.1.other = bf16[256,256]{1,0:T(8,128)(2,1)S(1)} collective-permute-done((bf16[256,256]{1,0:T(8,128)(2,1)S(1)}, bf16[256,256]{1,0:T(8,128)(2,1)S(1)}, u32[]{:S(2)}, u32[]{:S(2)}) %collective-permute-start.1) | collective-permute-done | bytes 131104 | tf_op jit(solution)/shard_map/ppermute | solution.py:288
  42.0 0.0 copy-done.2
  42.0 0.0 copy-done.3
  42.0 6.2 %attention.1 = (f32[256,256]{1,0:T(8,128)S(1)}, f32[256,256]{1,0:T(8,128)S(1)}) custom-call(s32[10]{0:T(128)S(1)} %pad_add_fusion.place, bf16[256,256]{1,0:T(8,128)(2,1)S(1)} %get-tuple-element.13.mine, bf16[256,256]{1,0:T(8,128)(2,1)S(1)} %collective-permute-done.1.other, bf16[512,1024]{1,0:T(8,128)(2,1)S(1)} %copy-done.2, bf16[512,1024]{1,0:T(8,128)(2,1)S(1)} %copy-done.3), custom_call_target="tpu_custom_call" | custom-call | tf_op jit(solution)/shard_map/attention/pallas_call | solution.py:207
  48.1 0.2 collective-permute-start.2
  48.4 1.4 %collective-permute-done.2.recv = f32[256,256]{1,0:T(8,128)S(1)} collective-permute-done((f32[256,256]{1,0:T(8,128)S(1)}, f32[256,256]{1,0:T(8,128)S(1)}, u32[]{:S(2)}, u32[]{:S(2)}) %collective-permute-start.2) | collective-permute-done | bytes 262176 | tf_op jit(solution)/shard_map/ppermute | solution.py:288
  49.8 0.8 scale_grads.1
  50.6 0.0 copy-start
  50.6 0.1 broadcast_in_dim.2
  50.6 18.7 %all_to_all.11.mine = bf16[8,256,256]{2,1,0:T(8,128)(2,1)S(1)} all-to-all(bf16[8,256,256]{2,1,0:T(8,128)(2,1)S(1)} %broadcast_in_dim.2), channel_id=1, replica_groups={{0,2,4,6,8,10,12,14},{1,3,5,7,9,11,13,15},{16,18,20,22,24,26,28,30},{17..., dimensions={0} | all-to-all | bytes 2097152 | tf_op jit(solution)/shard_map/all_to_all | solution.py:292
  69.3 0.0 collective-permute-start.3
  69.3 0.1 constant_dynamic-slice_fusion.3
  69.4 0.1 pad_maximum_fusion
  69.5 0.5 collective-permute-start.4
  70.0 2.0 %collective-permute-done.4 = f32[32,128]{1,0:T(8,128)S(1)} collective-permute-done((f32[32,128]{1,0:T(8,128)S(1)}, f32[32,128]{1,0:T(8,128)S(1)}, u32[]{:S(2)}, u32[]{:S(2)}) %collective-permute-start.4) | collective-permute-done | bytes 16416 | tf_op jit(solution)/shard_map/ppermute | solution.py:288
  72.0 0.1 maximum_add_fusion
  72.1 0.7 collective-permute-start.5
  72.7 4.6 %collective-permute-done.5 = f32[32,128]{1,0:T(8,128)S(1)} collective-permute-done((f32[32,128]{1,0:T(8,128)S(1)}, f32[32,128]{1,0:T(8,128)S(1)}, u32[]{:S(2)}, u32[]{:S(2)}) %collective-permute-start.5) | collective-permute-done | bytes 16416 | tf_op jit(solution)/shard_map/ppermute | solution.py:328
  77.4 1.9 %collective-permute-start.6 = (f32[32,128]{1,0:T(8,128)S(1)}, f32[32,128]{1,0:T(8,128)S(1)}, u32[]{:S(2)}, u32[]{:S(2)}) collective-permute-start(f32[32,128]{1,0:T(8,128)S(1)} %add.50), channel_id=1, source_target_pairs={{0,32},{16,48},{32,0},{48,16},{64,96},{80,112},{96,64},{112,80},{1... | collective-permute-start | bytes 49160 | tf_op jit(solution)/shard_map/ppermute | solution.py:328
  79.3 1.8 %collective-permute-done.6 = f32[32,128]{1,0:T(8,128)S(1)} collective-permute-done((f32[32,128]{1,0:T(8,128)S(1)}, f32[32,128]{1,0:T(8,128)S(1)}, u32[]{:S(2)}, u32[]{:S(2)}) %collective-permute-start.6) | collective-permute-done | bytes 16416 | tf_op jit(solution)/shard_map/ppermute | solution.py:328
  81.1 3.3 %collective-permute-start.7 = (f32[32,128]{1,0:T(8,128)S(1)}, f32[32,128]{1,0:T(8,128)S(1)}, u32[]{:S(2)}, u32[]{:S(2)}) collective-permute-start(f32[32,128]{1,0:T(8,128)S(1)} %add.51), channel_id=1, source_target_pairs={{0,64},{16,80},{32,96},{48,112},{64,0},{80,16},{96,32},{112,48},{1... | collective-permute-start | bytes 49160 | tf_op jit(solution)/shard_map/ppermute | solution.py:328
  84.4 1.7 %collective-permute-done.7 = f32[32,128]{1,0:T(8,128)S(1)} collective-permute-done((f32[32,128]{1,0:T(8,128)S(1)}, f32[32,128]{1,0:T(8,128)S(1)}, u32[]{:S(2)}, u32[]{:S(2)}) %collective-permute-start.7) | collective-permute-done | bytes 16416 | tf_op jit(solution)/shard_map/ppermute | solution.py:328
  86.1 6.8 %collective-permute-start.8 = (f32[32,128]{1,0:T(8,128)S(1)}, f32[32,128]{1,0:T(8,128)S(1)}, u32[]{:S(2)}, u32[]{:S(2)}) collective-permute-start(f32[32,128]{1,0:T(8,128)S(1)} %add.52), channel_id=1, source_target_pairs={{0,128},{16,144},{32,160},{48,176},{64,192},{80,208},{96,224},{112... | collective-permute-start | bytes 49160 | tf_op jit(solution)/shard_map/ppermute | solution.py:328
  92.9 1.7 %collective-permute-done.8 = f32[32,128]{1,0:T(8,128)S(1)} collective-permute-done((f32[32,128]{1,0:T(8,128)S(1)}, f32[32,128]{1,0:T(8,128)S(1)}, u32[]{:S(2)}, u32[]{:S(2)}) %collective-permute-start.8) | collective-permute-done | bytes 16416 | tf_op jit(solution)/shard_map/ppermute | solution.py:328
  94.7 0.7 fusion
  95.3 0.0 collective-permute-done.3.other
  95.3 0.0 copy-done
  95.3 6.1 %input_grads.1 = bf16[512,1024]{1,0:T(8,128)(2,1)} custom-call(s32[10]{0:T(128)S(1)} %pad_add_fusion.place, bf16[8,256,256]{2,1,0:T(8,128)(2,1)S(1)} %all_to_all.11.mine, bf16[8,256,256]{2,1,0:T(8,128)(2,1)} %collective-permute-done.3.other, bf16[1024,1024]{1,0:T(8,128)(2,1)S(1)} %copy-done, bf16[1024,1024]{1,0:T(8,128)(2,1)} %vw.3), custom_call_target="tpu_custom_call" | custom-call | tf_op jit(solution)/shard_map/input_grads/pallas_call | solution.py:273
  (4 shorter events, 0.0 us)
Async XLA Ops:
  2.2 1.2 %copy-start.1 = (bf16[512,1024]{1,0:T(8,128)(2,1)S(1)}, bf16[512,1024]{1,0:T(8,128)(2,1)}, u32[]{:S(2)}) copy-start(bf16[512,1024]{1,0:T(8,128)(2,1)} %tok_keep.1) | copy-start | bytes 3145732
  8.7 4.2 %collective-permute-start = (f32[8,256,256]{2,1,0:T(8,128)S(1)}, f32[8,256,256]{2,1,0:T(8,128)S(1)}, u32[]{:S(2)}, u32[]{:S(2)}) collective-permute-start(f32[8,256,256]{2,1,0:T(8,128)S(1)} %get-tuple-element.12), channel_id=1, source_target_pairs={{0,1},{1,0},{2,3},{3,2},{4,5},{5,4},{6,7},{7,6},{8,9},{9,8},{10,11... | collective-permute-start | bytes 6291464 | tf_op jit(solution)/shard_map/ppermute | solution.py:288
  13.3 26.3 %copy-start.4 = (f32[32,1024]{1,0:T(8,128)S(1)}, f32[32,1024]{1,0:T(8,128)}, u32[]{:S(2)}) copy-start(f32[32,1024]{1,0:T(8,128)} %key_scale.3) | copy-start | bytes 393220
  13.3 26.3 %copy-start.5 = (f32[32,1024]{1,0:T(8,128)S(1)}, f32[32,1024]{1,0:T(8,128)}, u32[]{:S(2)}) copy-start(f32[32,1024]{1,0:T(8,128)} %value_scale.3) | copy-start | bytes 393220
  13.3 28.6 %copy-start.2 = (bf16[512,1024]{1,0:T(8,128)(2,1)S(1)}, bf16[512,1024]{1,0:T(8,128)(2,1)}, u32[]{:S(2)}) copy-start(bf16[512,1024]{1,0:T(8,128)(2,1)} %queries.1) | copy-start | bytes 3145732
  13.4 28.6 %copy-start.3 = (bf16[512,1024]{1,0:T(8,128)(2,1)S(1)}, bf16[512,1024]{1,0:T(8,128)(2,1)}, u32[]{:S(2)}) copy-start(bf16[512,1024]{1,0:T(8,128)(2,1)} %out_grad.1) | copy-start | bytes 3145732
  40.5 1.4 %collective-permute-start.1 = (bf16[256,256]{1,0:T(8,128)(2,1)S(1)}, bf16[256,256]{1,0:T(8,128)(2,1)S(1)}, u32[]{:S(2)}, u32[]{:S(2)}) collective-permute-start(bf16[256,256]{1,0:T(8,128)(2,1)S(1)} %get-tuple-element.13.mine), channel_id=1, source_target_pairs={{0,1},{1,0},{2,3},{3,2},{4,5},{5,4},{6,7},{7,6},{8,9},{9,8},{10,11... | collective-permute-start | bytes 393224 | tf_op jit(solution)/shard_map/ppermute | solution.py:288
  48.1 1.6 %collective-permute-start.2 = (f32[256,256]{1,0:T(8,128)S(1)}, f32[256,256]{1,0:T(8,128)S(1)}, u32[]{:S(2)}, u32[]{:S(2)}) collective-permute-start(f32[256,256]{1,0:T(8,128)S(1)} %get-tuple-element.15), channel_id=1, source_target_pairs={{0,1},{1,0},{2,3},{3,2},{4,5},{5,4},{6,7},{7,6},{8,9},{9,8},{10,11... | collective-permute-start | bytes 786440 | tf_op jit(solution)/shard_map/ppermute | solution.py:288
  50.6 44.8 %copy-start = (bf16[1024,1024]{1,0:T(8,128)(2,1)S(1)}, bf16[1024,1024]{1,0:T(8,128)(2,1)}, u32[]{:S(2)}) copy-start(bf16[1024,1024]{1,0:T(8,128)(2,1)} %kw.3) | copy-start | bytes 6291460
  69.3 26.0 %collective-permute-start.3 = (bf16[8,256,256]{2,1,0:T(8,128)(2,1)S(1)}, bf16[8,256,256]{2,1,0:T(8,128)(2,1)}, u32[]{:S(2)}, u32[]{:S(2)}) collective-permute-start(bf16[8,256,256]{2,1,0:T(8,128)(2,1)S(1)} %all_to_all.11.mine), channel_id=1, source_target_pairs={{0,1},{1,0},{2,3},{3,2},{4,5},{5,4},{6,7},{7,6},{8,9},{9,8},{10,11... | collective-permute-start | bytes 3145736 | tf_op jit(solution)/shard_map/ppermute | solution.py:288
  69.5 2.5 %collective-permute-start.4 = (f32[32,128]{1,0:T(8,128)S(1)}, f32[32,128]{1,0:T(8,128)S(1)}, u32[]{:S(2)}, u32[]{:S(2)}) collective-permute-start(f32[32,128]{1,0:T(8,128)S(1)} %pad_maximum_fusion), channel_id=1, source_target_pairs={{0,1},{1,0},{2,3},{3,2},{4,5},{5,4},{6,7},{7,6},{8,9},{9,8},{10,11... | collective-permute-start | bytes 49160 | tf_op jit(solution)/shard_map/ppermute | solution.py:288
  72.1 5.3 %collective-permute-start.5 = (f32[32,128]{1,0:T(8,128)S(1)}, f32[32,128]{1,0:T(8,128)S(1)}, u32[]{:S(2)}, u32[]{:S(2)}) collective-permute-start(f32[32,128]{1,0:T(8,128)S(1)} %maximum_add_fusion), channel_id=1, source_target_pairs={{0,16},{16,0},{32,48},{48,32},{64,80},{80,64},{96,112},{112,96},{1... | collective-permute-start | bytes 49160 | tf_op jit(solution)/shard_map/ppermute | solution.py:328
  77.4 3.7 %collective-permute-start.6 = (f32[32,128]{1,0:T(8,128)S(1)}, f32[32,128]{1,0:T(8,128)S(1)}, u32[]{:S(2)}, u32[]{:S(2)}) collective-permute-start(f32[32,128]{1,0:T(8,128)S(1)} %add.50), channel_id=1, source_target_pairs={{0,32},{16,48},{32,0},{48,16},{64,96},{80,112},{96,64},{112,80},{1... | collective-permute-start | bytes 49160 | tf_op jit(solution)/shard_map/ppermute | solution.py:328
  81.1 5.0 %collective-permute-start.7 = (f32[32,128]{1,0:T(8,128)S(1)}, f32[32,128]{1,0:T(8,128)S(1)}, u32[]{:S(2)}, u32[]{:S(2)}) collective-permute-start(f32[32,128]{1,0:T(8,128)S(1)} %add.51), channel_id=1, source_target_pairs={{0,64},{16,80},{32,96},{48,112},{64,0},{80,16},{96,32},{112,48},{1... | collective-permute-start | bytes 49160 | tf_op jit(solution)/shard_map/ppermute | solution.py:328
  86.1 8.6 %collective-permute-start.8 = (f32[32,128]{1,0:T(8,128)S(1)}, f32[32,128]{1,0:T(8,128)S(1)}, u32[]{:S(2)}, u32[]{:S(2)}) collective-permute-start(f32[32,128]{1,0:T(8,128)S(1)} %add.52), channel_id=1, source_target_pairs={{0,128},{16,144},{32,160},{48,176},{64,192},{80,208},{96,224},{112... | collective-permute-start | bytes 49160 | tf_op jit(solution)/shard_map/ppermute | solution.py:328

commit v2 on v1

v2 whole, which is shorter than its diff:
```python
import functools

import jax
import jax.numpy as jnp
from jax import lax
from jax.experimental import pallas as pl
from jax.experimental.pallas import tpu as pltpu
from jax.sharding import PartitionSpec as P

SEQS = 4
NT = 32
HEAD = 128
TOK = 512
HALF = 256
CHIPS = 8
BLOCK = 128
LOG2E = 1.4426950408889634
SCALE = HEAD**-0.5
BF = jnp.bfloat16
F32 = jnp.float32
MIB = 1024 * 1024


def call(name, body, outs, args, scratch=(), mib=16, flops=0, out_space=pltpu.VMEM):
    spaces = [pltpu.SMEM if array.ndim == 1 else pltpu.VMEM for array in args]
    placed = [
        array if space is pltpu.SMEM else pltpu.with_memory_space_constraint(array, space)
        for array, space in zip(args, spaces)
    ]
    nbytes = sum(array.size * array.dtype.itemsize for array in args)
    return pl.pallas_call(
        body,
        in_specs=[pl.BlockSpec(memory_space=space) for space in spaces],
        out_specs=[pl.BlockSpec(memory_space=out_space)] * len(outs),
        out_shape=[out_space(*out) for out in outs],
        scratch_shapes=list(scratch),
        compiler_params=pltpu.CompilerParams(vmem_limit_bytes=mib * MIB),
        cost_estimate=pl.CostEstimate(flops=flops, bytes_accessed=nbytes, transcendentals=0),
        name=name,
    )(*placed)


def device_index(x, y, core):
    return (x % 4 * 2 + y) * 2 + core


def tensor_pairs(step):
    places = [(x, y, core) for x in range(4) for y in range(2) for core in range(2)]
    return [(device_index(*place), device_index(*step(*place))) for place in places]


CORE_SWAP = tensor_pairs(lambda x, y, core: (x, y, core ^ 1))
ROW_SWAP = tensor_pairs(lambda x, y, core: (x, y ^ 1, core))


def chip_shift(across, row):
    return tensor_pairs(lambda x, y, core: (x + across, y ^ row, core))


X_FROM = [tensor_pairs(lambda x, y, core, step=step: (x - step, y, core)) for step in range(4)]
SAME_CORE = [[chip * 2 + core for chip in range(CHIPS)] for core in range(2)]


def home_of(chip, across, row):
    home = lax.rem(chip + 2 * across, CHIPS)
    return home + row * (1 - 2 * lax.rem(home, 2))


def project_body(flip, count, tokens, *refs):
    weights, outs = refs[:count], refs[count:]
    core = lax.rem(lax.axis_index("tensor"), 2)
    half = 1 - core if flip else core
    rows = pl.ds(pl.multiple_of(half * HALF, HALF), HALF)
    for weight, out in zip(weights, outs):
        out[...] = jnp.dot(tokens[rows, :], weight[...], preferred_element_type=F32).astype(out.dtype)


def project(name, flip, tokens, weights, dtypes):
    depth, columns = weights[0].shape
    count = len(weights)
    return call(
        name,
        functools.partial(project_body, flip, count),
        [((HALF, columns), dtype) for dtype in dtypes],
        [tokens, *weights],
        flops=2 * count * HALF * depth * columns,
    )


def pack_body(key_keep, value_keep, key_recv, value_recv, out):
    for chip in range(CHIPS):
        columns = slice(chip * HEAD, (chip + 1) * HEAD)
        key = key_keep[:, columns] + key_recv[:, columns]
        high = key.astype(BF)
        out[chip, :, :HEAD] = high
        out[chip, :, HEAD : 2 * HEAD] = (key - high.astype(F32)).astype(BF)
        value = value_keep[:, columns] + value_recv[:, columns].astype(F32)
        out[chip, :, 2 * HEAD :] = value.astype(BF)


def pack(*parts):
    return call("pack", pack_body, [((CHIPS, HALF, 3 * HEAD), BF)], parts)[0]


def place_body(segments, tenants, place):
    rank = lax.axis_index("tensor")
    place[0] = lax.rem(rank, 2)
    for seq in range(SEQS):
        place[1 + seq] = jnp.sum((segments[...] < seq).astype(jnp.int32))
        place[5 + seq] = tenants[0, seq]
    place[9] = lax.div(rank, 2)


def find_place(segment_ids, tenant_ids):
    smem = pl.BlockSpec(memory_space=pltpu.SMEM)
    return pl.pallas_call(
        place_body,
        in_specs=[pl.BlockSpec(memory_space=pltpu.VMEM), smem],
        out_specs=smem,
        out_shape=jax.ShapeDtypeStruct((10,), jnp.int32),
        compiler_params=pltpu.CompilerParams(vmem_limit_bytes=4 * MIB),
        name="place",
    )(segment_ids, tenant_ids)


def own_sequences(place):
    row = lax.broadcasted_iota(jnp.int32, (HALF, HEAD), 0) + place[0] * HALF
    found = [row >= place[1 + seq] for seq in range(1, SEQS)]
    return found


def token_factor(place, scale, sequences):
    columns = pl.ds(pl.multiple_of(place[9] * HEAD, HEAD), HEAD)
    table = scale[:, columns]
    tenant = lax.broadcasted_iota(jnp.int32, table.shape, 0)
    rows = [
        jnp.sum(jnp.where(tenant == place[5 + seq], table, 0.0), axis=0, keepdims=True)
        for seq in range(SEQS)
    ]
    factor = jnp.broadcast_to(rows[0], (HALF, HEAD))
    for seq in range(1, SEQS):
        factor = jnp.where(sequences[seq - 1], rows[seq], factor)
    return factor


def finish_body(place, parts, key_scale, value_scale, base, low):
    total = parts[0].astype(F32)
    for chip in range(1, CHIPS):
        total = total + parts[chip].astype(F32)
    sequences = own_sequences(place)
    key = total[:, :HEAD] + total[:, HEAD : 2 * HEAD]
    value = total[:, 2 * HEAD :]
    base[:, :HEAD] = key
    base[:, HEAD:] = value
    low[:, :HEAD] = (key * token_factor(place, key_scale, sequences)).astype(BF)
    low[:, HEAD:] = (value * token_factor(place, value_scale, sequences)).astype(BF)


def finish(*args):
    return call("finish", finish_body, [((HALF, 2 * HEAD), F32), ((HALF, 2 * HEAD), BF)], args)


def contract_last(left, right):
    return lax.dot_general(left, right, (((1,), (1,)), ((), ())), preferred_element_type=F32)


def attention_body(place, mine, other, queries, out_grad, send, keep, tile, grads):
    core = place[0]
    own_rows = pl.ds(pl.multiple_of(core * HALF, HALF), HALF)
    other_rows = pl.ds(pl.multiple_of((1 - core) * HALF, HALF), HALF)
    tile[own_rows, :] = mine[...]
    tile[other_rows, :] = other[...]
    grads[...] = jnp.zeros_like(grads)
    heads = queries.shape[1] // HEAD
    for block in range(TOK // BLOCK):
        first = max(0, block - 2) * BLOCK
        reach = (block + 1) * BLOCK - first
        rows = slice(block * BLOCK, (block + 1) * BLOCK)
        visible = slice(first, first + reach)
        key_row = lax.broadcasted_iota(jnp.int32, (reach, BLOCK), 0) + first
        query_row = lax.broadcasted_iota(jnp.int32, (reach, BLOCK), 1) + block * BLOCK
        start = jnp.zeros((reach, BLOCK), jnp.int32)
        for seq in range(1, SEQS):
            start = jnp.where(query_row >= place[1 + seq], place[1 + seq], start)
        allowed = (key_row >= start) & (key_row <= query_row)
        bias = jnp.where(allowed, 0.0, -1e30).astype(F32)
        bias = jnp.concatenate([bias, bias], axis=1)
        key_tile = tile[visible, :HEAD]
        value_tile = tile[visible, HEAD:]
        key_total = jnp.zeros((reach, HEAD), F32)
        value_total = jnp.zeros((reach, HEAD), F32)
        for pair in range(heads // 2):
            columns = [slice(h * HEAD, (h + 1) * HEAD) for h in (2 * pair, 2 * pair + 1)]
            query = jnp.concatenate([queries[rows, c] for c in columns], axis=0)
            out = jnp.concatenate([out_grad[rows, c] for c in columns], axis=0)
            scores = contract_last(key_tile, query) + bias
            peak = jnp.max(scores, axis=0, keepdims=True)
            exps = jnp.exp2((scores - peak) * (SCALE * LOG2E))
            probs = exps * (1.0 / jnp.sum(exps, axis=0, keepdims=True))
            probs_low = probs.astype(BF)
            prob_grad = contract_last(value_tile, out)
            delta = jnp.sum(probs_low.astype(F32) * prob_grad, axis=0, keepdims=True)
            score_grad = (probs * (prob_grad - delta)).astype(BF)
            value_total += jnp.dot(probs_low, out, preferred_element_type=F32)
            key_total += jnp.dot(score_grad, query, preferred_element_type=F32)
        grads[visible, :HEAD] += key_total
        grads[visible, HEAD:] += value_total
    for rows, target in ((other_rows, send), (own_rows, keep)):
        target[:, :HEAD] = grads[rows, :HEAD] * SCALE
        target[:, HEAD:] = grads[rows, HEAD:]


def attention(*args):
    return call(
        "attention",
        attention_body,
        [((HALF, 2 * HEAD), F32)] * 2,
        args,
        scratch=[pltpu.VMEM((TOK, 2 * HEAD), BF), pltpu.VMEM((TOK, 2 * HEAD), F32)],
        mib=24,
    )


def scale_body(place, keep, recv, base, key_scale, value_scale, low, sums):
    sequences = own_sequences(place)
    tables = []
    for part, scale in enumerate((key_scale, value_scale)):
        columns = slice(part * HEAD, (part + 1) * HEAD)
        grad = keep[:, columns] + recv[:, columns]
        low[:, columns] = (grad * token_factor(place, scale, sequences)).astype(BF)
        product = grad * base[:, columns]
        later = [jnp.sum(product, axis=0, keepdims=True)]
        for seq in range(1, SEQS):
            later.append(jnp.sum(jnp.where(sequences[seq - 1], product, 0.0), axis=0, keepdims=True))
        later.append(jnp.zeros_like(later[0]))
        row = lax.broadcasted_iota(jnp.int32, (NT, HEAD), 0)
        table = jnp.zeros((NT, HEAD), F32)
        for seq in range(SEQS):
            table = table + jnp.where(row == place[5 + seq], later[seq] - later[seq + 1], 0.0)
        tables.append(table)
    key, value = tables
    lower = lax.broadcasted_iota(jnp.int32, (NT, HEAD), 1) < HEAD // 2
    first = jnp.where(lower, key, pltpu.roll(value, HEAD // 2, 1))
    second = jnp.where(lower, pltpu.roll(key, HEAD // 2, 1), value)
    sums[0] = jnp.where(place[0] == 0, first, second)
    sums[1] = jnp.where(place[0] == 0, second, first)


def scale_grads(*args):
    outs = [((HALF, 2 * HEAD), BF), ((2, NT, HEAD), F32)]
    return call("scale_grads", scale_body, outs, args)


def input_body(place, *refs):
    mine, other = refs[: CHIPS // 2], refs[CHIPS // 2 : CHIPS]
    key_weight, value_weight, out, left_key, left_value, totals, sems = refs[CHIPS:]
    core, chip = place[0], place[9]
    for half, pieces in ((core, mine), (1 - core, other)):
        rows = pl.ds(pl.multiple_of(half * HALF, HALF), HALF)
        for step, piece in enumerate(pieces):
            for row in range(2):
                columns = pl.ds(pl.multiple_of(home_of(chip, step, row) * HEAD, HEAD), HEAD)
                left_key[rows, columns] = piece[row, :, :HEAD]
                left_value[rows, columns] = piece[row, :, HEAD:]
    writes = []
    steps, width = totals.shape[0], totals.shape[2]
    for step in range(steps):
        columns = pl.ds(step * width, width)
        total = contract_last(left_key[...], key_weight[columns, :])
        total += contract_last(left_value[...], value_weight[columns, :])
        totals[step] = total.astype(BF)
        writes.append(pltpu.make_async_copy(totals.at[step], out.at[:, columns], sems.at[step]))
        writes[-1].start()
    for write in writes:
        write.wait()


def input_grads(place, mine, other, key_weight, value_weight):
    features, depth = key_weight.shape
    steps = 4
    scratch = [
        pltpu.VMEM((TOK, depth), BF),
        pltpu.VMEM((TOK, depth), BF),
        pltpu.VMEM((steps, TOK, features // steps), BF),
        pltpu.SemaphoreType.DMA((steps,)),
    ]
    outs = [((TOK, features), BF)]
    args = [place, *mine, *other, key_weight, value_weight]
    flops = 4 * TOK * features * depth
    return call("input_grads", input_body, outs, args, scratch, 20, flops, out_space=pltpu.HBM)[0]


def pair_body(mine, other, out):
    out[0] = mine[...]
    out[1] = other[...]


def pair_up(mine, other):
    return call("pair", pair_body, [((2,) + mine.shape, BF)], [mine, other])[0]


def add_body(*refs):
    total = refs[0][...]
    for ref in refs[1:-1]:
        total = total + ref[...]
    refs[-1][...] = total


def add_up(*parts):
    return call("add_up", add_body, [(parts[0].shape, F32)], parts, mib=4)[0]


def ring_body(below, here, above, three, two):
    two[...] = here[...] + above[...]
    three[...] = two[...] + below[...]


def ring_sums(*parts):
    return call("ring_sums", ring_body, [(parts[0].shape, F32)] * 2, parts, mib=4)


def split_body(first, second, third, own, give):
    total = first[...] + second[...] + third[...]
    own[...] = total[0]
    give[...] = total[1]


def split_sums(*parts):
    return call("split_sums", split_body, [((NT, HEAD), F32)] * 2, parts, mib=4)


def total_body(own, recv, key, value):
    total = own[...] + recv[...]
    key[...] = total[:, : HEAD // 2]
    value[...] = total[:, HEAD // 2 :]


def tenant_totals(own, recv):
    return pl.pallas_call(
        total_body,
        out_shape=[jax.ShapeDtypeStruct((NT, HEAD // 2), F32)] * 2,
        compiler_params=pltpu.CompilerParams(vmem_limit_bytes=4 * MIB),
        name="tenant_totals",
    )(own, recv)


def core_swap(array):
    return lax.ppermute(array, "tensor", CORE_SWAP)


def depth_from(array, step):
    pairs = [((z + step) % 8 * 2 + row, z * 2 + row) for z in range(8) for row in range(2)]
    return lax.ppermute(array, "dp", pairs)


def on_device(
    tokens,
    queries,
    out_grad,
    key_weight,
    value_weight,
    key_scale,
    value_scale,
    segment_ids,
    tenant_ids,
):
    place = find_place(segment_ids, tenant_ids)
    key_send = project("project_key", True, tokens, [key_weight], [F32])[0]
    key_recv = core_swap(key_send)
    value_send = project("project_value", True, tokens, [value_weight], [BF])[0]
    value_recv = core_swap(value_send)
    weights = [key_weight, value_weight]
    key_keep, value_keep = project("project_keep", False, tokens, weights, [F32, F32])
    packed = pack(key_keep, value_keep, key_recv, value_recv)
    packed, place = lax.optimization_barrier((packed, place))
    parts = lax.all_to_all(packed, "tensor", 0, 0, axis_index_groups=SAME_CORE, tiled=True)
    base, low = finish(place, parts, key_scale, value_scale)
    send, keep = attention(place, low, core_swap(low), queries, out_grad)
    grad_low, sums = scale_grads(place, keep, core_swap(send), base, key_scale, value_scale)
    sums = add_up(sums, lax.ppermute(sums, "dp", [(i, i ^ 1) for i in range(16)]))
    pair = pair_up(grad_low, lax.ppermute(grad_low, "tensor", ROW_SWAP))
    pair, sums = lax.optimization_barrier((pair, sums))
    near = [lax.ppermute(pair, "tensor", X_FROM[step]) for step in (2, 1, 3)]
    three, two = ring_sums(depth_from(sums, -1), sums, depth_from(sums, 1))
    own, give = split_sums(three, depth_from(three, 3), depth_from(two, -3))
    near, own, give = lax.optimization_barrier((near, own, give))
    mine = [pair, near[1], near[0], near[2]]
    other = [core_swap(piece) for piece in mine]
    input_grad = input_grads(place, mine, other, key_weight, value_weight)
    key_total, value_total = tenant_totals(own, core_swap(give))
    return input_grad, key_total, value_total


def solution(mesh):
    return jax.shard_map(
        on_device,
        mesh=mesh,
        in_specs=(
            P("dp", "tensor"),
            P("dp", "tensor"),
            P("dp", "tensor"),
            P("tensor", None),
            P("tensor", None),
            P(),
            P(),
            P("dp", None),
            P("dp", None),
        ),
        out_specs=(P("dp", "tensor"), P(None, "tensor"), P(None, "tensor")),
        check_vma=False,
    )
```

time: 102 us -> 86.4 us (0.85)
  the two profiles are of different devices: /device:TPU:16 before, /device:TPU:1 now
where the time goes in v2:
time: 86.4 us; the launch traced here: 86 us
  starting transfers between devices  28.3 us (33%)
  blocking collectives  24 us (28%)
  Pallas kernels  17.1 us (20%)
  waiting for transfers between devices  12.8 us (15%)
  local copies, waits for them, and re-layouts  2.86 us (3%)
  between operations  1.01 us (1%)
    all_to_all x1, blocking collectives, on_device(): lax.all_to_all(packed, 'tensor', 0, 0, axis_index_groups=SAME_CORE, tiled...  24 us
    pallas_call x12, Pallas kernels, call(): pl.pallas_call(body, in_specs=[pl.BlockSpec(memory_space=space) for space...  15.2 us
    ppermute x9, starting transfers between devices, core_swap(): return lax.ppermute(array, 'tensor', CORE_SWAP)  12.7 us
    ppermute x4, starting transfers between devices, depth_from(): return lax.ppermute(array, 'dp', pairs)  8.94 us
    ppermute x4, waiting for transfers between devices, depth_from(): return lax.ppermute(array, 'dp', pairs)  5.58 us
    ppermute x1, waiting for transfers between devices, on_device(): lax.ppermute(sums, 'dp', [(i, i ^ 1) for i in range(16)])  3.66 us
    ppermute x9, waiting for transfers between devices, core_swap(): return lax.ppermute(array, 'tensor', CORE_SWAP)  3.5 us
    ppermute x3, starting transfers between devices, on_device(): near = [lax.ppermute(pair, 'tensor', X_FROM[step]) for step in (2, 1, 3)]  2.95 us
  transfers between devices with their start and end apart: 18, of which 7 were waited for; matrix products, arithmetic and copies ran while one was open for 0% of the time, Pallas kernels for 5%

profile of v2, /device:TPU:1, one launch (start us, length us, event | category | flops | bytes accessed | tf_op | source)
XLA Modules:
  0.0 86.0 jit_solution(12772752500162146617)
XLA Ops:
  0.6 0.0 copy-start
  0.6 1.2 %copy-done = bf16[512,1024]{1,0:T(8,128)(2,1)S(1)} copy-done((bf16[512,1024]{1,0:T(8,128)(2,1)S(1)}, bf16[512,1024]{1,0:T(8,128)(2,1)}, u32[]{:S(2)}) %copy-start) | copy-done | bytes 1048600
  1.9 1.6 %copy-done.2 = bf16[1024,1024]{1,0:T(8,128)(2,1)S(1)} copy-done((bf16[1024,1024]{1,0:T(8,128)(2,1)S(1)}, bf16[1024,1024]{1,0:T(8,128)(2,1)}, u32[]{:S(2)}) %copy-start.2) | copy-done | bytes 2097176
  3.4 0.7 project_key.1
  4.2 0.0 copy-start.8
  4.2 0.0 copy-start.9
  4.2 3.3 %collective-permute-start = (f32[256,1024]{1,0:T(8,128)S(1)}, f32[256,1024]{1,0:T(8,128)S(1)}, u32[]{:S(2)}, u32[]{:S(2)}) collective-permute-start(f32[256,1024]{1,0:T(8,128)S(1)} %project_key.1), channel_id=1, source_target_pairs={{0,1},{1,0},{2,3},{3,2},{4,5},{5,4},{6,7},{7,6},{8,9},{9,8},{10,11... | collective-permute-start | bytes 3145736 | tf_op jit(solution)/shard_map/ppermute | solution.py:348
  7.5 0.0 copy-done.1
  7.5 0.7 project_value.1
  8.2 0.9 collective-permute-start.1
  9.1 0.0 copy-done.8
  9.1 0.0 copy-done.9
  9.1 1.3 %place.1 = s32[10]{0:T(128)S(1)} custom-call(s32[1,512]{1,0:T(1,128)S(1)} %copy-done.8, s32[1,4]{1,0:T(1,128)S(1)} %copy-done.9), custom_call_target="tpu_custom_call" | custom-call | tf_op jit(solution)/shard_map/place/pallas_call | solution.py:116
  10.4 1.3 %project_keep.1 = (f32[256,1024]{1,0:T(8,128)S(1)}, f32[256,1024]{1,0:T(8,128)S(1)}) custom-call(bf16[512,1024]{1,0:T(8,128)(2,1)S(1)} %copy-done, bf16[1024,1024]{1,0:T(8,128)(2,1)S(1)} %copy-done.2, bf16[1024,1024]{1,0:T(8,128)(2,1)S(1)} %copy-done.1), custom_call_target="tpu_custom_call" | custom-call | flops 1073741824 | bytes 5242880 | tf_op jit(solution)/shard_map/project_keep/pallas_call | solution.py:31
  11.6 0.0 collective-permute-done.1.value_recv
  11.7 0.0 collective-permute-done.key_recv
  11.7 0.4 pack.1
  12.1 0.0 copy-start.6
  12.1 0.0 copy-start.7
  12.1 0.0 copy-start.4
  12.2 0.0 copy-start.5
  12.2 24.0 %all_to_all.5.parts = bf16[8,256,384]{2,1,0:T(8,128)(2,1)S(1)} all-to-all(bf16[8,256,384]{2,1,0:T(8,128)(2,1)S(1)} %pack.1), channel_id=1, replica_groups={{0,2,4,6,8,10,12,14},{1,3,5,7,9,11,13,15},{16,18,20,22,24,26,28,30},{17..., dimensions={0} | all-to-all | bytes 3145728 | tf_op jit(solution)/shard_map/all_to_all | solution.py:376
  36.2 0.0 copy-done.6
  36.2 0.0 copy-done.7
  36.2 0.8 finish.1
  37.0 0.0 copy-start.3
  37.1 1.2 %collective-permute-start.2 = (bf16[256,256]{1,0:T(8,128)(2,1)S(1)}, bf16[256,256]{1,0:T(8,128)(2,1)S(1)}, u32[]{:S(2)}, u32[]{:S(2)}) collective-permute-start(bf16[256,256]{1,0:T(8,128)(2,1)S(1)} %get-tuple-element.30.mine), channel_id=1, source_target_pairs={{0,1},{1,0},{2,3},{3,2},{4,5},{5,4},{6,7},{7,6},{8,9},{9,8},{10,11... | collective-permute-start | bytes 393224 | tf_op jit(solution)/shard_map/ppermute | solution.py:348
  38.3 1.0 %collective-permute-done.2.other = bf16[256,256]{1,0:T(8,128)(2,1)S(1)} collective-permute-done((bf16[256,256]{1,0:T(8,128)(2,1)S(1)}, bf16[256,256]{1,0:T(8,128)(2,1)S(1)}, u32[]{:S(2)}, u32[]{:S(2)}) %collective-permute-start.2) | collective-permute-done | bytes 131104 | tf_op jit(solution)/shard_map/ppermute | solution.py:348
  39.2 0.0 copy-done.4
  39.3 0.0 copy-done.5
  39.3 6.2 %attention.1 = (f32[256,256]{1,0:T(8,128)S(1)}, f32[256,256]{1,0:T(8,128)S(1)}) custom-call(s32[10]{0:T(128)S(1)} %place.1, bf16[256,256]{1,0:T(8,128)(2,1)S(1)} %get-tuple-element.30.mine, bf16[256,256]{1,0:T(8,128)(2,1)S(1)} %collective-permute-done.2.other, bf16[512,1024]{1,0:T(8,128)(2,1)S(1)} %copy-done.4, bf16[512,1024]{1,0:T(8,128)(2,1)S(1)} %copy-done.5), custom_call_target="tpu_custom_call" | custom-call | bytes 2359336 | tf_op jit(solution)/shard_map/attention/pallas_call | solution.py:31
  45.4 0.4 collective-permute-start.3
  45.9 1.2 %collective-permute-done.3.recv = f32[256,256]{1,0:T(8,128)S(1)} collective-permute-done((f32[256,256]{1,0:T(8,128)S(1)}, f32[256,256]{1,0:T(8,128)S(1)}, u32[]{:S(2)}, u32[]{:S(2)}) %collective-permute-start.3) | collective-permute-done | bytes 262176 | tf_op jit(solution)/shard_map/ppermute | solution.py:348
  47.1 0.8 scale_grads.1
  47.8 1.0 %collective-permute-start.4 = (bf16[256,256]{1,0:T(8,128)(2,1)S(1)}, bf16[256,256]{1,0:T(8,128)(2,1)S(1)}, u32[]{:S(2)}, u32[]{:S(2)}) collective-permute-start(bf16[256,256]{1,0:T(8,128)(2,1)S(1)} %get-tuple-element.34.mine), channel_id=1, source_target_pairs={{0,2},{1,3},{2,0},{3,1},{4,6},{5,7},{6,4},{7,5},{8,10},{9,11},{10,... | collective-permute-start | bytes 393224 | tf_op jit(solution)/shard_map/ppermute | solution.py:381
  48.9 2.6 %collective-permute-start.5 = (f32[2,32,128]{2,1,0:T(8,128)S(1)}, f32[2,32,128]{2,1,0:T(8,128)S(1)}, u32[]{:S(2)}, u32[]{:S(2)}) collective-permute-start(f32[2,32,128]{2,1,0:T(8,128)S(1)} %get-tuple-element.35.refs_0_), channel_id=1, source_target_pairs={{0,16},{16,0},{32,48},{48,32},{64,80},{80,64},{96,112},{112,96},{1... | collective-permute-start | bytes 98312 | tf_op jit(solution)/shard_map/ppermute | solution.py:380
  51.5 3.7 %collective-permute-done.5.refs_1_ = f32[2,32,128]{2,1,0:T(8,128)S(1)} collective-permute-done((f32[2,32,128]{2,1,0:T(8,128)S(1)}, f32[2,32,128]{2,1,0:T(8,128)S(1)}, u32[]{:S(2)}, u32[]{:S(2)}) %collective-permute-start.5) | collective-permute-done | bytes 32800 | tf_op jit(solution)/shard_map/ppermute | solution.py:380
  55.1 0.0 collective-permute-done.4.other
  55.2 0.5 collective-permute-start.6
  55.7 2.4 %collective-permute-start.7 = (bf16[2,256,256]{2,1,0:T(8,128)(2,1)S(1)}, bf16[2,256,256]{2,1,0:T(8,128)(2,1)S(1)}, u32[]{:S(2)}, u32[]{:S(2)}) collective-permute-start(bf16[2,256,256]{2,1,0:T(8,128)(2,1)S(1)} %pair.1.refs_0_), channel_id=1, source_target_pairs={{0,12},{1,13},{2,14},{3,15},{4,0},{5,1},{6,2},{7,3},{8,4},{9,5},{1... | collective-permute-start | bytes 786440 | tf_op jit(solution)/shard_map/ppermute | solution.py:383
  58.1 0.0 collective-permute-start.8
  58.1 5.6 %collective-permute-start.10 = (f32[2,32,128]{2,1,0:T(8,128)S(1)}, f32[2,32,128]{2,1,0:T(8,128)S(1)}, u32[]{:S(2)}, u32[]{:S(2)}) collective-permute-start(f32[2,32,128]{2,1,0:T(8,128)S(1)} %add_up.1.here), channel_id=1, source_target_pairs={{32,0},{48,16},{64,32},{80,48},{96,64},{112,80},{128,96},{144,112}... | collective-permute-start | bytes 98312 | tf_op jit(solution)/shard_map/ppermute | solution.py:353
  63.7 0.0 collective-permute-start.9
  63.7 1.0 %collective-permute-done.10.above = f32[2,32,128]{2,1,0:T(8,128)S(1)} collective-permute-done((f32[2,32,128]{2,1,0:T(8,128)S(1)}, f32[2,32,128]{2,1,0:T(8,128)S(1)}, u32[]{:S(2)}, u32[]{:S(2)}) %collective-permute-start.10) | collective-permute-done | bytes 32800 | tf_op jit(solution)/shard_map/ppermute | solution.py:353
  64.7 3.2 %collective-permute-done.9.below = f32[2,32,128]{2,1,0:T(8,128)S(1)} collective-permute-done((f32[2,32,128]{2,1,0:T(8,128)S(1)}, f32[2,32,128]{2,1,0:T(8,128)S(1)}, u32[]{:S(2)}, u32[]{:S(2)}) %collective-permute-start.9) | collective-permute-done | bytes 32800 | tf_op jit(solution)/shard_map/ppermute | solution.py:353
  68.0 0.5 collective-permute-start.11
  68.5 2.9 %collective-permute-start.12 = (f32[2,32,128]{2,1,0:T(8,128)S(1)}, f32[2,32,128]{2,1,0:T(8,128)S(1)}, u32[]{:S(2)}, u32[]{:S(2)}) collective-permute-start(f32[2,32,128]{2,1,0:T(8,128)S(1)} %get-tuple-element.39), channel_id=1, source_target_pairs={{160,0},{176,16},{192,32},{208,48},{224,64},{240,80},{0,96},{16,11... | collective-permute-start | bytes 98312 | tf_op jit(solution)/shard_map/ppermute | solution.py:353
  71.3 1.3 %collective-permute-done.11.second = f32[2,32,128]{2,1,0:T(8,128)S(1)} collective-permute-done((f32[2,32,128]{2,1,0:T(8,128)S(1)}, f32[2,32,128]{2,1,0:T(8,128)S(1)}, u32[]{:S(2)}, u32[]{:S(2)}) %collective-permute-start.11) | collective-permute-done | bytes 32800 | tf_op jit(solution)/shard_map/ppermute | solution.py:353
  72.7 4.4 %collective-permute-start.13 = (bf16[2,256,256]{2,1,0:T(8,128)(2,1)S(1)}, bf16[2,256,256]{2,1,0:T(8,128)(2,1)S(1)}, u32[]{:S(2)}, u32[]{:S(2)}) collective-permute-start(bf16[2,256,256]{2,1,0:T(8,128)(2,1)S(1)} %pair.1.refs_0_), channel_id=1, source_target_pairs={{0,1},{1,0},{2,3},{3,2},{4,5},{5,4},{6,7},{7,6},{8,9},{9,8},{10,11... | collective-permute-start | bytes 786440 | tf_op jit(solution)/shard_map/ppermute | solution.py:348
  77.1 0.0 collective-permute-done.12.third
  77.1 0.0 collective-permute-done.6.refs_2_
  77.1 0.0 collective-permute-done.7.refs_1_
  77.1 0.0 collective-permute-done.8.refs_3_
  77.1 1.9 %collective-permute-start.14 = (bf16[2,256,256]{2,1,0:T(8,128)(2,1)S(1)}, bf16[2,256,256]{2,1,0:T(8,128)(2,1)S(1)}, u32[]{:S(2)}, u32[]{:S(2)}) collective-permute-start(bf16[2,256,256]{2,1,0:T(8,128)(2,1)S(1)} %collective-permute-done.7.refs_1_), channel_id=1, source_target_pairs={{0,1},{1,0},{2,3},{3,2},{4,5},{5,4},{6,7},{7,6},{8,9},{9,8},{10,11... | collective-permute-start | bytes 786440 | tf_op jit(solution)/shard_map/ppermute | solution.py:348
  79.0 0.1 collective-permute-start.15
  79.1 0.4 collective-permute-start.16
  79.5 0.1 collective-permute-start.17
  79.6 1.3 %collective-permute-done.17.recv = f32[32,128]{1,0:T(8,128)S(1)} collective-permute-done((f32[32,128]{1,0:T(8,128)S(1)}, f32[32,128]{1,0:T(8,128)S(1)}, u32[]{:S(2)}, u32[]{:S(2)}) %collective-permute-start.17) | collective-permute-done | bytes 16416 | tf_op jit(solution)/shard_map/ppermute | solution.py:348
  80.9 0.7 tenant_totals.1
  81.6 0.0 collective-permute-done.13.refs_4_
  81.6 0.0 collective-permute-done.14.refs_5_
  81.6 0.0 collective-permute-done.15.refs_6_
  81.6 0.0 collective-permute-done.16.refs_7_
  81.6 4.2 %input_grads.1 = bf16[512,1024]{1,0:T(8,128)(2,1)} custom-call(s32[10]{0:T(128)S(1)} %place.1, bf16[2,256,256]{2,1,0:T(8,128)(2,1)S(1)} %pair.1.refs_0_, bf16[2,256,256]{2,1,0:T(8,128)(2,1)S(1)} %collective-permute-done.7.refs_1_, bf16[2,256,256]{2,1,0:T(8,128)(2,1)S(1)} %collective-permute-done.6.refs_2_, ...), custom_call_target="tpu_custom_call" | custom-call | flops 2147483648 | bytes 6291496 | tf_op jit(solution)/shard_map/input_grads/pallas_call | solution.py:31
  (7 shorter events, 0.0 us)
Async XLA Ops:
  0.6 1.2 %copy-start = (bf16[512,1024]{1,0:T(8,128)(2,1)S(1)}, bf16[512,1024]{1,0:T(8,128)(2,1)}, u32[]{:S(2)}) copy-start(bf16[512,1024]{1,0:T(8,128)(2,1)} %tokens.5) | copy-start | bytes 3145732
  1.9 1.6 %copy-start.2 = (bf16[1024,1024]{1,0:T(8,128)(2,1)S(1)}, bf16[1024,1024]{1,0:T(8,128)(2,1)}, u32[]{:S(2)}) copy-start(bf16[1024,1024]{1,0:T(8,128)(2,1)} %refs_8_.1) | copy-start | bytes 6291460
  3.4 4.1 %copy-start.1 = (bf16[1024,1024]{1,0:T(8,128)(2,1)S(1)}, bf16[1024,1024]{1,0:T(8,128)(2,1)}, u32[]{:S(2)}) copy-start(bf16[1024,1024]{1,0:T(8,128)(2,1)} %refs_9_.1) | copy-start | bytes 6291460
  4.2 4.9 %copy-start.8 = (s32[1,512]{1,0:T(1,128)S(1)}, s32[1,512]{1,0:T(1,128)}, u32[]{:S(2)}) copy-start(s32[1,512]{1,0:T(1,128)} %segments.1) | copy-start | bytes 6148
  4.2 4.9 %copy-start.9 = (s32[1,4]{1,0:T(1,128)S(1)}, s32[1,4]{1,0:T(1,128)}, u32[]{:S(2)}) copy-start(s32[1,4]{1,0:T(1,128)} %tenants.1) | copy-start | bytes 52
  4.2 7.5 %collective-permute-start = (f32[256,1024]{1,0:T(8,128)S(1)}, f32[256,1024]{1,0:T(8,128)S(1)}, u32[]{:S(2)}, u32[]{:S(2)}) collective-permute-start(f32[256,1024]{1,0:T(8,128)S(1)} %project_key.1), channel_id=1, source_target_pairs={{0,1},{1,0},{2,3},{3,2},{4,5},{5,4},{6,7},{7,6},{8,9},{9,8},{10,11... | collective-permute-start | bytes 3145736 | tf_op jit(solution)/shard_map/ppermute | solution.py:348
  8.2 3.4 %collective-permute-start.1 = (bf16[256,1024]{1,0:T(8,128)(2,1)S(1)}, bf16[256,1024]{1,0:T(8,128)(2,1)S(1)}, u32[]{:S(2)}, u32[]{:S(2)}) collective-permute-start(bf16[256,1024]{1,0:T(8,128)(2,1)S(1)} %project_value.1), channel_id=1, source_target_pairs={{0,1},{1,0},{2,3},{3,2},{4,5},{5,4},{6,7},{7,6},{8,9},{9,8},{10,11... | collective-permute-start | bytes 1572872 | tf_op jit(solution)/shard_map/ppermute | solution.py:348
  12.1 24.1 %copy-start.6 = (f32[32,1024]{1,0:T(8,128)S(1)}, f32[32,1024]{1,0:T(8,128)}, u32[]{:S(2)}) copy-start(f32[32,1024]{1,0:T(8,128)} %key_scale.3) | copy-start | bytes 393220
  12.1 24.1 %copy-start.7 = (f32[32,1024]{1,0:T(8,128)S(1)}, f32[32,1024]{1,0:T(8,128)}, u32[]{:S(2)}) copy-start(f32[32,1024]{1,0:T(8,128)} %value_scale.3) | copy-start | bytes 393220
  12.1 27.1 %copy-start.4 = (bf16[512,1024]{1,0:T(8,128)(2,1)S(1)}, bf16[512,1024]{1,0:T(8,128)(2,1)}, u32[]{:S(2)}) copy-start(bf16[512,1024]{1,0:T(8,128)(2,1)} %queries.1) | copy-start | bytes 3145732
  12.2 27.1 %copy-start.5 = (bf16[512,1024]{1,0:T(8,128)(2,1)S(1)}, bf16[512,1024]{1,0:T(8,128)(2,1)}, u32[]{:S(2)}) copy-start(bf16[512,1024]{1,0:T(8,128)(2,1)} %out_grad.1) | copy-start | bytes 3145732
  37.0 44.6 %copy-start.3 = (bf16[1024,1024]{1,0:T(8,128)(2,1)S(1)}, bf16[1024,1024]{1,0:T(8,128)(2,1)}, u32[]{:S(2)}) copy-start(bf16[1024,1024]{1,0:T(8,128)(2,1)} %refs_8_.1) | copy-start | bytes 6291460
  37.1 2.2 %collective-permute-start.2 = (bf16[256,256]{1,0:T(8,128)(2,1)S(1)}, bf16[256,256]{1,0:T(8,128)(2,1)S(1)}, u32[]{:S(2)}, u32[]{:S(2)}) collective-permute-start(bf16[256,256]{1,0:T(8,128)(2,1)S(1)} %get-tuple-element.30.mine), channel_id=1, source_target_pairs={{0,1},{1,0},{2,3},{3,2},{4,5},{5,4},{6,7},{7,6},{8,9},{9,8},{10,11... | collective-permute-start | bytes 393224 | tf_op jit(solution)/shard_map/ppermute | solution.py:348
  45.4 1.6 %collective-permute-start.3 = (f32[256,256]{1,0:T(8,128)S(1)}, f32[256,256]{1,0:T(8,128)S(1)}, u32[]{:S(2)}, u32[]{:S(2)}) collective-permute-start(f32[256,256]{1,0:T(8,128)S(1)} %get-tuple-element.32), channel_id=1, source_target_pairs={{0,1},{1,0},{2,3},{3,2},{4,5},{5,4},{6,7},{7,6},{8,9},{9,8},{10,11... | collective-permute-start | bytes 786440 | tf_op jit(solution)/shard_map/ppermute | solution.py:348
  47.8 7.3 %collective-permute-start.4 = (bf16[256,256]{1,0:T(8,128)(2,1)S(1)}, bf16[256,256]{1,0:T(8,128)(2,1)S(1)}, u32[]{:S(2)}, u32[]{:S(2)}) collective-permute-start(bf16[256,256]{1,0:T(8,128)(2,1)S(1)} %get-tuple-element.34.mine), channel_id=1, source_target_pairs={{0,2},{1,3},{2,0},{3,1},{4,6},{5,7},{6,4},{7,5},{8,10},{9,11},{10,... | collective-permute-start | bytes 393224 | tf_op jit(solution)/shard_map/ppermute | solution.py:381
  48.9 6.3 %collective-permute-start.5 = (f32[2,32,128]{2,1,0:T(8,128)S(1)}, f32[2,32,128]{2,1,0:T(8,128)S(1)}, u32[]{:S(2)}, u32[]{:S(2)}) collective-permute-start(f32[2,32,128]{2,1,0:T(8,128)S(1)} %get-tuple-element.35.refs_0_), channel_id=1, source_target_pairs={{0,16},{16,0},{32,48},{48,32},{64,80},{80,64},{96,112},{112,96},{1... | collective-permute-start | bytes 98312 | tf_op jit(solution)/shard_map/ppermute | solution.py:380
  55.2 21.9 %collective-permute-start.6 = (bf16[2,256,256]{2,1,0:T(8,128)(2,1)S(1)}, bf16[2,256,256]{2,1,0:T(8,128)(2,1)S(1)}, u32[]{:S(2)}, u32[]{:S(2)}) collective-permute-start(bf16[2,256,256]{2,1,0:T(8,128)(2,1)S(1)} %pair.1.refs_0_), channel_id=1, source_target_pairs={{0,8},{1,9},{2,10},{3,11},{4,12},{5,13},{6,14},{7,15},{8,0},{9,1},... | collective-permute-start | bytes 786440 | tf_op jit(solution)/shard_map/ppermute | solution.py:383
  55.7 21.4 %collective-permute-start.7 = (bf16[2,256,256]{2,1,0:T(8,128)(2,1)S(1)}, bf16[2,256,256]{2,1,0:T(8,128)(2,1)S(1)}, u32[]{:S(2)}, u32[]{:S(2)}) collective-permute-start(bf16[2,256,256]{2,1,0:T(8,128)(2,1)S(1)} %pair.1.refs_0_), channel_id=1, source_target_pairs={{0,12},{1,13},{2,14},{3,15},{4,0},{5,1},{6,2},{7,3},{8,4},{9,5},{1... | collective-permute-start | bytes 786440 | tf_op jit(solution)/shard_map/ppermute | solution.py:383
  58.1 19.0 %collective-permute-start.8 = (bf16[2,256,256]{2,1,0:T(8,128)(2,1)S(1)}, bf16[2,256,256]{2,1,0:T(8,128)(2,1)S(1)}, u32[]{:S(2)}, u32[]{:S(2)}) collective-permute-start(bf16[2,256,256]{2,1,0:T(8,128)(2,1)S(1)} %pair.1.refs_0_), channel_id=1, source_target_pairs={{0,4},{1,5},{2,6},{3,7},{4,8},{5,9},{6,10},{7,11},{8,12},{9,13},{1... | collective-permute-start | bytes 786440 | tf_op jit(solution)/shard_map/ppermute | solution.py:383
  58.1 6.6 %collective-permute-start.10 = (f32[2,32,128]{2,1,0:T(8,128)S(1)}, f32[2,32,128]{2,1,0:T(8,128)S(1)}, u32[]{:S(2)}, u32[]{:S(2)}) collective-permute-start(f32[2,32,128]{2,1,0:T(8,128)S(1)} %add_up.1.here), channel_id=1, source_target_pairs={{32,0},{48,16},{64,32},{80,48},{96,64},{112,80},{128,96},{144,112}... | collective-permute-start | bytes 98312 | tf_op jit(solution)/shard_map/ppermute | solution.py:353
  63.7 4.3 %collective-permute-start.9 = (f32[2,32,128]{2,1,0:T(8,128)S(1)}, f32[2,32,128]{2,1,0:T(8,128)S(1)}, u32[]{:S(2)}, u32[]{:S(2)}) collective-permute-start(f32[2,32,128]{2,1,0:T(8,128)S(1)} %add_up.1.here), channel_id=1, source_target_pairs={{224,0},{240,16},{0,32},{16,48},{32,64},{48,80},{64,96},{80,112},{... | collective-permute-start | bytes 98312 | tf_op jit(solution)/shard_map/ppermute | solution.py:353
  68.0 4.7 %collective-permute-start.11 = (f32[2,32,128]{2,1,0:T(8,128)S(1)}, f32[2,32,128]{2,1,0:T(8,128)S(1)}, u32[]{:S(2)}, u32[]{:S(2)}) collective-permute-start(f32[2,32,128]{2,1,0:T(8,128)S(1)} %get-tuple-element.38.first), channel_id=1, source_target_pairs={{96,0},{112,16},{128,32},{144,48},{160,64},{176,80},{192,96},{208,... | collective-permute-start | bytes 98312 | tf_op jit(solution)/shard_map/ppermute | solution.py:353
  68.5 8.6 %collective-permute-start.12 = (f32[2,32,128]{2,1,0:T(8,128)S(1)}, f32[2,32,128]{2,1,0:T(8,128)S(1)}, u32[]{:S(2)}, u32[]{:S(2)}) collective-permute-start(f32[2,32,128]{2,1,0:T(8,128)S(1)} %get-tuple-element.39), channel_id=1, source_target_pairs={{160,0},{176,16},{192,32},{208,48},{224,64},{240,80},{0,96},{16,11... | collective-permute-start | bytes 98312 | tf_op jit(solution)/shard_map/ppermute | solution.py:353
  72.7 9.0 %collective-permute-start.13 = (bf16[2,256,256]{2,1,0:T(8,128)(2,1)S(1)}, bf16[2,256,256]{2,1,0:T(8,128)(2,1)S(1)}, u32[]{:S(2)}, u32[]{:S(2)}) collective-permute-start(bf16[2,256,256]{2,1,0:T(8,128)(2,1)S(1)} %pair.1.refs_0_), channel_id=1, source_target_pairs={{0,1},{1,0},{2,3},{3,2},{4,5},{5,4},{6,7},{7,6},{8,9},{9,8},{10,11... | collective-permute-start | bytes 786440 | tf_op jit(solution)/shard_map/ppermute | solution.py:348
  77.1 4.5 %collective-permute-start.14 = (bf16[2,256,256]{2,1,0:T(8,128)(2,1)S(1)}, bf16[2,256,256]{2,1,0:T(8,128)(2,1)S(1)}, u32[]{:S(2)}, u32[]{:S(2)}) collective-permute-start(bf16[2,256,256]{2,1,0:T(8,128)(2,1)S(1)} %collective-permute-done.7.refs_1_), channel_id=1, source_target_pairs={{0,1},{1,0},{2,3},{3,2},{4,5},{5,4},{6,7},{7,6},{8,9},{9,8},{10,11... | collective-permute-start | bytes 786440 | tf_op jit(solution)/shard_map/ppermute | solution.py:348
  79.0 2.6 %collective-permute-start.15 = (bf16[2,256,256]{2,1,0:T(8,128)(2,1)S(1)}, bf16[2,256,256]{2,1,0:T(8,128)(2,1)S(1)}, u32[]{:S(2)}, u32[]{:S(2)}) collective-permute-start(bf16[2,256,256]{2,1,0:T(8,128)(2,1)S(1)} %collective-permute-done.6.refs_2_), channel_id=1, source_target_pairs={{0,1},{1,0},{2,3},{3,2},{4,5},{5,4},{6,7},{7,6},{8,9},{9,8},{10,11... | collective-permute-start | bytes 786440 | tf_op jit(solution)/shard_map/ppermute | solution.py:348
  79.1 2.5 %collective-permute-start.16 = (bf16[2,256,256]{2,1,0:T(8,128)(2,1)S(1)}, bf16[2,256,256]{2,1,0:T(8,128)(2,1)S(1)}, u32[]{:S(2)}, u32[]{:S(2)}) collective-permute-start(bf16[2,256,256]{2,1,0:T(8,128)(2,1)S(1)} %collective-permute-done.8.refs_3_), channel_id=1, source_target_pairs={{0,1},{1,0},{2,3},{3,2},{4,5},{5,4},{6,7},{7,6},{8,9},{9,8},{10,11... | collective-permute-start | bytes 786440 | tf_op jit(solution)/shard_map/ppermute | solution.py:348
  79.5 1.4 %collective-permute-start.17 = (f32[32,128]{1,0:T(8,128)S(1)}, f32[32,128]{1,0:T(8,128)S(1)}, u32[]{:S(2)}, u32[]{:S(2)}) collective-permute-start(f32[32,128]{1,0:T(8,128)S(1)} %get-tuple-element.46), channel_id=1, source_target_pairs={{0,1},{1,0},{2,3},{3,2},{4,5},{5,4},{6,7},{7,6},{8,9},{9,8},{10,11... | collective-permute-start | bytes 49160 | tf_op jit(solution)/shard_map/ppermute | solution.py:348

commit v3 on v2

--- a/solution.py
+++ b/solution.py
@@ -50,15 +50,9 @@
 
 
 CORE_SWAP = tensor_pairs(lambda x, y, core: (x, y, core ^ 1))
-ROW_SWAP = tensor_pairs(lambda x, y, core: (x, y ^ 1, core))
-
-
-def chip_shift(across, row):
-    return tensor_pairs(lambda x, y, core: (x + across, y ^ row, core))
-
-
-X_FROM = [tensor_pairs(lambda x, y, core, step=step: (x - step, y, core)) for step in range(4)]
-SAME_CORE = [[chip * 2 + core for chip in range(CHIPS)] for core in range(2)]
+X_ORDER = [0, 2, 1, 3]
+SENT = [(2, 1), (1, 1), (3, 1), (1, 0), (3, 0)]
+KEPT = [(2, 0), (0, 1), (0, 0)]
 
 
 def home_of(chip, across, row):
@@ -87,19 +81,45 @@
     )
 
 
-def pack_body(key_keep, value_keep, key_recv, value_recv, out):
-    for chip in range(CHIPS):
-        columns = slice(chip * HEAD, (chip + 1) * HEAD)
+def encode(total, out):
+    high = total[:, :HEAD].astype(BF)
+    out[:, :HEAD] = high
+    out[:, HEAD : 2 * HEAD] = (total[:, :HEAD] - high.astype(F32)).astype(BF)
+    out[:, 2 * HEAD :] = total[:, HEAD:].astype(BF)
+
+
+def decode(part):
+    key = part[:, :HEAD].astype(F32) + part[:, HEAD : 2 * HEAD].astype(F32)
+    return jnp.concatenate([key, part[:, 2 * HEAD :].astype(F32)], axis=1)
+
+
+def pack_body(key_keep, value_keep, key_recv, value_recv, *outs):
+    chip = lax.div(lax.axis_index("tensor"), 2)
+    for (across, row), out in zip(SENT + KEPT, outs):
+        columns = pl.ds(pl.multiple_of(home_of(chip, across, row) * HEAD, HEAD), HEAD)
         key = key_keep[:, columns] + key_recv[:, columns]
-        high = key.astype(BF)
-        out[chip, :, :HEAD] = high
-        out[chip, :, HEAD : 2 * HEAD] = (key - high.astype(F32)).astype(BF)
         value = value_keep[:, columns] + value_recv[:, columns].astype(F32)
-        out[chip, :, 2 * HEAD :] = value.astype(BF)
+        total = jnp.concatenate([key, value], axis=1)
+        if (across, row) in KEPT:
+            out[...] = total
+        else:
+            encode(total, out)
 
 
 def pack(*parts):
-    return call("pack", pack_body, [((CHIPS, HALF, 3 * HEAD), BF)], parts)[0]
+    outs = [((HALF, 3 * HEAD), BF)] * len(SENT) + [((HALF, 2 * HEAD), F32)] * len(KEPT)
+    return call("pack", pack_body, outs, parts)
+
+
+def relay_body(kept, *refs):
+    total = kept[...]
+    for part in refs[:-1]:
+        total = total + decode(part[...])
+    encode(total, refs[-1])
+
+
+def relay(*parts):
+    return call("relay", relay_body, [((HALF, 3 * HEAD), BF)], parts, mib=8)[0]
 
 
 def place_body(segments, tenants, place):
@@ -143,13 +163,14 @@
     return factor
 
 
-def finish_body(place, parts, key_scale, value_scale, base, low):
-    total = parts[0].astype(F32)
-    for chip in range(1, CHIPS):
-        total = total + parts[chip].astype(F32)
+def finish_body(place, kept, *refs):
+    parts, (key_scale, value_scale, base, low) = refs[:-4], refs[-4:]
+    total = kept[...]
+    for part in parts:
+        total = total + decode(part[...])
     sequences = own_sequences(place)
-    key = total[:, :HEAD] + total[:, HEAD : 2 * HEAD]
-    value = total[:, 2 * HEAD :]
+    key = total[:, :HEAD]
+    value = total[:, HEAD:]
     base[:, :HEAD] = key
     base[:, HEAD:] = value
     low[:, :HEAD] = (key * token_factor(place, key_scale, sequences)).astype(BF)
@@ -221,7 +242,7 @@
     )
 
 
-def scale_body(place, keep, recv, base, key_scale, value_scale, low, sums):
+def scale_body(place, keep, recv, base, key_scale, value_scale, low, own, give):
     sequences = own_sequences(place)
     tables = []
     for part, scale in enumerate((key_scale, value_scale)):
@@ -242,12 +263,12 @@
     lower = lax.broadcasted_iota(jnp.int32, (NT, HEAD), 1) < HEAD // 2
     first = jnp.where(lower, key, pltpu.roll(value, HEAD // 2, 1))
     second = jnp.where(lower, pltpu.roll(key, HEAD // 2, 1), value)
-    sums[0] = jnp.where(place[0] == 0, first, second)
-    sums[1] = jnp.where(place[0] == 0, second, first)
+    own[...] = jnp.where(place[0] == 0, first, second)
+    give[...] = jnp.where(place[0] == 0, second, first)
 
 
 def scale_grads(*args):
-    outs = [((HALF, 2 * HEAD), BF), ((2, NT, HEAD), F32)]
+    outs = [((HALF, 2 * HEAD), BF), ((NT, HEAD), F32), ((NT, HEAD), F32)]
     return call("scale_grads", scale_body, outs, args)
 
 
@@ -257,9 +278,9 @@
     core, chip = place[0], place[9]
     for half, pieces in ((core, mine), (1 - core, other)):
         rows = pl.ds(pl.multiple_of(half * HALF, HALF), HALF)
-        for step, piece in enumerate(pieces):
+        for across, piece in zip(X_ORDER, pieces):
             for row in range(2):
-                columns = pl.ds(pl.multiple_of(home_of(chip, step, row) * HEAD, HEAD), HEAD)
+                columns = pl.ds(pl.multiple_of(home_of(chip, across, row) * HEAD, HEAD), HEAD)
                 left_key[rows, columns] = piece[row, :, :HEAD]
                 left_value[rows, columns] = piece[row, :, HEAD:]
     writes = []
@@ -290,15 +311,6 @@
     return call("input_grads", input_body, outs, args, scratch, 20, flops, out_space=pltpu.HBM)[0]
 
 
-def pair_body(mine, other, out):
-    out[0] = mine[...]
-    out[1] = other[...]
-
-
-def pair_up(mine, other):
-    return call("pair", pair_body, [((2,) + mine.shape, BF)], [mine, other])[0]
-
-
 def add_body(*refs):
     total = refs[0][...]
     for ref in refs[1:-1]:
@@ -310,42 +322,42 @@
     return call("add_up", add_body, [(parts[0].shape, F32)], parts, mib=4)[0]
 
 
-def ring_body(below, here, above, three, two):
+def pair_body(mine, other, here, below, above, out, three, two):
+    out[0] = mine[...]
+    out[1] = other[...]
     two[...] = here[...] + above[...]
     three[...] = two[...] + below[...]
 
 
-def ring_sums(*parts):
-    return call("ring_sums", ring_body, [(parts[0].shape, F32)] * 2, parts, mib=4)
-
-
-def split_body(first, second, third, own, give):
-    total = first[...] + second[...] + third[...]
-    own[...] = total[0]
-    give[...] = total[1]
-
-
-def split_sums(*parts):
-    return call("split_sums", split_body, [((NT, HEAD), F32)] * 2, parts, mib=4)
-
-
-def total_body(own, recv, key, value):
-    total = own[...] + recv[...]
+def pair_up(*args):
+    outs = [((2,) + args[0].shape, BF), (args[2].shape, F32), (args[2].shape, F32)]
+    return call("pair", pair_body, outs, args, mib=4)
+
+
+def total_body(here, recv, key, value):
+    total = here[...] + recv[...]
     key[...] = total[:, : HEAD // 2]
     value[...] = total[:, HEAD // 2 :]
 
 
-def tenant_totals(own, recv):
+def tenant_totals(here, recv):
     return pl.pallas_call(
         total_body,
         out_shape=[jax.ShapeDtypeStruct((NT, HEAD // 2), F32)] * 2,
         compiler_params=pltpu.CompilerParams(vmem_limit_bytes=4 * MIB),
         name="tenant_totals",
-    )(own, recv)
+    )(here, recv)
 
 
 def core_swap(array):
     return lax.ppermute(array, "tensor", CORE_SWAP)
+
+
+def chip_from(array, across, row):
+    if across == row == 0:
+        return array
+    pairs = tensor_pairs(lambda x, y, core: (x - across, y ^ row, core))
+    return lax.ppermute(array, "tensor", pairs)
 
 
 def depth_from(array, step):
@@ -372,22 +384,33 @@
     weights = [key_weight, value_weight]
     key_keep, value_keep = project("project_keep", False, tokens, weights, [F32, F32])
     packed = pack(key_keep, value_keep, key_recv, value_recv)
-    packed, place = lax.optimization_barrier((packed, place))
-    parts = lax.all_to_all(packed, "tensor", 0, 0, axis_index_groups=SAME_CORE, tiled=True)
-    base, low = finish(place, parts, key_scale, value_scale)
+    part_21, part_11, part_31, part_10, part_30, kept_20, kept_01, kept_00 = packed
+    part_20 = relay(kept_20, chip_from(part_21, 0, 1))
+    part_01 = relay(kept_01, chip_from(part_11, -1, 0), chip_from(part_31, 1, 0))
+    parts = [
+        chip_from(part_10, -1, 0),
+        chip_from(part_30, 1, 0),
+        chip_from(part_20, 2, 0),
+        chip_from(part_01, 0, 1),
+    ]
+    base, low = finish(place, kept_00, *parts, key_scale, value_scale)
     send, keep = attention(place, low, core_swap(low), queries, out_grad)
-    grad_low, sums = scale_grads(place, keep, core_swap(send), base, key_scale, value_scale)
-    sums = add_up(sums, lax.ppermute(sums, "dp", [(i, i ^ 1) for i in range(16)]))
-    pair = pair_up(grad_low, lax.ppermute(grad_low, "tensor", ROW_SWAP))
-    pair, sums = lax.optimization_barrier((pair, sums))
-    near = [lax.ppermute(pair, "tensor", X_FROM[step]) for step in (2, 1, 3)]
-    three, two = ring_sums(depth_from(sums, -1), sums, depth_from(sums, 1))
-    own, give = split_sums(three, depth_from(three, 3), depth_from(two, -3))
-    near, own, give = lax.optimization_barrier((near, own, give))
-    mine = [pair, near[1], near[0], near[2]]
+    grad_low, own, give = scale_grads(place, keep, core_swap(send), base, key_scale, value_scale)
+    sums = add_up(own, core_swap(give))
+    arrived = lax.optimization_barrier(
+        (chip_from(grad_low, 0, 1), sums, depth_from(sums, -1), depth_from(sums, 1))
+    )
+    pair, three, two = pair_up(grad_low, *arrived)
+    near = [chip_from(pair, across, 0) for across in X_ORDER[1:]]
+    far = [depth_from(three, 3), depth_from(two, -3)]
+    near, far = lax.optimization_barrier((near, far))
+    sums = add_up(three, *far)
+    sums_other = lax.ppermute(sums, "dp", [(i, i ^ 1) for i in range(16)])
+    mine = [pair] + near
     other = [core_swap(piece) for piece in mine]
     input_grad = input_grads(place, mine, other, key_weight, value_weight)
-    key_total, value_total = tenant_totals(own, core_swap(give))
+    input_grad, sums_other = lax.optimization_barrier((input_grad, sums_other))
+    key_total, value_total = tenant_totals(sums, sums_other)
     return input_grad, key_total, value_total
 
 

time: 86.4 us -> 73 us (0.84)
  blocking collectives: 24 us -> 0 us
  starting transfers between devices: 28.3 us -> 37.5 us
  waiting for transfers between devices: 12.8 us -> 14.3 us
    all_to_all x1 -> x0, blocking collectives: 24 us -> none  [on_device(): lax.all_to_all(packed, 'tensor', 0, 0, axis_index_groups=SAME_CORE, tiled...]
    ppermute x5 -> x12, starting transfers between devices: 6.58 us -> 14.6 us  [the longest x11 11.7 us: chip_from(): return lax.ppermute(array, 'tensor', pairs)]
    ppermute x5 -> x12, waiting for transfers between devices: 3.67 us -> 8.43 us  [the longest x11 8.42 us: chip_from(): return lax.ppermute(array, 'tensor', pairs)]
    ppermute x4, waiting for transfers between devices: 5.58 us -> 2.6 us  [depth_from(): return lax.ppermute(array, 'dp', pairs)]
    ppermute x9, starting transfers between devices: 12.7 us -> 14.1 us  [core_swap(): return lax.ppermute(array, 'tensor', CORE_SWAP)]
    pallas_call x12 -> x13, Pallas kernels: 15.2 us -> 15.3 us  [call(): pl.pallas_call(body, in_specs=[pl.BlockSpec(memory_space=space) for space...]
  transfers between devices with their start and end apart: 18 -> 25, of which waited for: 7 -> 14; matrix products, arithmetic and copies ran while one was open for 0% -> 0% of each run, Pallas kernels for 5% -> 10%
where the time goes in v3:
time: 73 us; the launch traced here: 72.8 us
  starting transfers between devices  37.5 us (51%)
  Pallas kernels  17.3 us (24%)
  waiting for transfers between devices  14.3 us (20%)
  local copies, waits for them, and re-layouts  2.85 us (4%)
  between operations  0.83 us (1%)
    pallas_call x13, Pallas kernels, call(): pl.pallas_call(body, in_specs=[pl.BlockSpec(memory_space=space) for space...  15.3 us
    ppermute x9, starting transfers between devices, core_swap(): return lax.ppermute(array, 'tensor', CORE_SWAP)  14.1 us
    ppermute x11, starting transfers between devices, chip_from(): return lax.ppermute(array, 'tensor', pairs)  11.7 us
    ppermute x4, starting transfers between devices, depth_from(): return lax.ppermute(array, 'dp', pairs)  8.83 us
    ppermute x11, waiting for transfers between devices, chip_from(): return lax.ppermute(array, 'tensor', pairs)  8.42 us
    ppermute x9, waiting for transfers between devices, core_swap(): return lax.ppermute(array, 'tensor', CORE_SWAP)  3.28 us
    ppermute x1, starting transfers between devices, on_device(): sums_other = lax.ppermute(sums, 'dp', [(i, i ^ 1) for i in range(16)])  2.93 us
    unnamed x20, local copies, waits for them, and re-layouts  2.85 us
  transfers between devices with their start and end apart: 25, of which 14 were waited for; matrix products, arithmetic and copies ran while one was open for 0% of the time, Pallas kernels for 10%

profile of v3, /device:TPU:1, one launch (start us, length us, event | category | flops | bytes accessed | tf_op | source)
XLA Modules:
  0.0 72.8 jit_solution(15997471757259960998)
XLA Ops:
  0.6 1.2 %copy-done = bf16[512,1024]{1,0:T(8,128)(2,1)S(1)} copy-done((bf16[512,1024]{1,0:T(8,128)(2,1)S(1)}, bf16[512,1024]{1,0:T(8,128)(2,1)}, u32[]{:S(2)}) %copy-start) | copy-done | bytes 1048600
  1.9 1.6 %copy-done.2 = bf16[1024,1024]{1,0:T(8,128)(2,1)S(1)} copy-done((bf16[1024,1024]{1,0:T(8,128)(2,1)S(1)}, bf16[1024,1024]{1,0:T(8,128)(2,1)}, u32[]{:S(2)}) %copy-start.2) | copy-done | bytes 2097176
  3.4 0.7 project_key.1
  4.2 3.3 %collective-permute-start = (f32[256,1024]{1,0:T(8,128)S(1)}, f32[256,1024]{1,0:T(8,128)S(1)}, u32[]{:S(2)}, u32[]{:S(2)}) collective-permute-start(f32[256,1024]{1,0:T(8,128)S(1)} %project_key.1), channel_id=1, source_target_pairs={{0,1},{1,0},{2,3},{3,2},{4,5},{5,4},{6,7},{7,6},{8,9},{9,8},{10,11... | collective-permute-start | bytes 3145736 | tf_op jit(solution)/shard_map/ppermute | solution.py:353
  7.5 0.7 project_value.1
  8.2 0.9 %collective-permute-start.1 = (bf16[256,1024]{1,0:T(8,128)(2,1)S(1)}, bf16[256,1024]{1,0:T(8,128)(2,1)S(1)}, u32[]{:S(2)}, u32[]{:S(2)}) collective-permute-start(bf16[256,1024]{1,0:T(8,128)(2,1)S(1)} %project_value.1), channel_id=1, source_target_pairs={{0,1},{1,0},{2,3},{3,2},{4,5},{5,4},{6,7},{7,6},{8,9},{9,8},{10,11... | collective-permute-start | bytes 1572872 | tf_op jit(solution)/shard_map/ppermute | solution.py:353
  9.1 1.3 %project_keep.1 = (f32[256,1024]{1,0:T(8,128)S(1)}, f32[256,1024]{1,0:T(8,128)S(1)}) custom-call(bf16[512,1024]{1,0:T(8,128)(2,1)S(1)} %copy-done, bf16[1024,1024]{1,0:T(8,128)(2,1)S(1)} %copy-done.2, bf16[1024,1024]{1,0:T(8,128)(2,1)S(1)} %copy-done.1), custom_call_target="tpu_custom_call" | custom-call | flops 1073741824 | bytes 5242880 | tf_op jit(solution)/shard_map/project_keep/pallas_call | solution.py:31
  10.4 0.3 collective-permute-done.1.value_recv
  10.6 0.0 collective-permute-done.key_recv
  10.6 0.0 copy-start.7
  10.7 0.6 pack.1
  11.2 0.0 copy-start.4
  11.3 0.0 copy-start.5
  11.3 0.1 collective-permute-start.6
  11.4 2.7 %collective-permute-start.7 = (bf16[256,384]{1,0:T(8,128)(2,1)S(1)}, bf16[256,384]{1,0:T(8,128)(2,1)S(1)}, u32[]{:S(2)}, u32[]{:S(2)}) collective-permute-start(bf16[256,384]{1,0:T(8,128)(2,1)S(1)} %get-tuple-element.45), channel_id=1, source_target_pairs={{0,12},{1,13},{2,14},{3,15},{4,0},{5,1},{6,2},{7,3},{8,4},{9,5},{1... | collective-permute-start | bytes 589832 | tf_op jit(solution)/shard_map/ppermute | solution.py:360
  14.0 0.0 collective-permute-start.4
  14.0 0.0 collective-permute-start.2
  14.0 2.7 %collective-permute-start.3 = (bf16[256,384]{1,0:T(8,128)(2,1)S(1)}, bf16[256,384]{1,0:T(8,128)(2,1)S(1)}, u32[]{:S(2)}, u32[]{:S(2)}) collective-permute-start(bf16[256,384]{1,0:T(8,128)(2,1)S(1)} %get-tuple-element.40), channel_id=1, source_target_pairs={{0,12},{1,13},{2,14},{3,15},{4,0},{5,1},{6,2},{7,3},{8,4},{9,5},{1... | collective-permute-start | bytes 589832 | tf_op jit(solution)/shard_map/ppermute | solution.py:360
  16.7 2.0 %collective-permute-done.6.refs_0_ = bf16[256,384]{1,0:T(8,128)(2,1)S(1)} collective-permute-done((bf16[256,384]{1,0:T(8,128)(2,1)S(1)}, bf16[256,384]{1,0:T(8,128)(2,1)S(1)}, u32[]{:S(2)}, u32[]{:S(2)}) %collective-permute-start.6) | collective-permute-done | bytes 196640 | tf_op jit(solution)/shard_map/ppermute | solution.py:360
  18.7 0.0 collective-permute-done.7.refs_1_
  18.7 0.1 relay.3
  18.8 0.1 collective-permute-start.8
  18.9 0.6 collective-permute-done.4.refs_0_
  19.5 0.1 relay.2
  19.5 1.1 %collective-permute-start.5 = (bf16[256,384]{1,0:T(8,128)(2,1)S(1)}, bf16[256,384]{1,0:T(8,128)(2,1)S(1)}, u32[]{:S(2)}, u32[]{:S(2)}) collective-permute-start(bf16[256,384]{1,0:T(8,128)(2,1)S(1)} %relay.2), channel_id=1, source_target_pairs={{0,8},{1,9},{2,10},{3,11},{4,12},{5,13},{6,14},{7,15},{8,0},{9,1},... | collective-permute-start | bytes 589832 | tf_op jit(solution)/shard_map/ppermute | solution.py:360
  20.7 1.3 %place.1 = s32[10]{0:T(128)S(1)} custom-call(s32[1,512]{1,0:T(1,128)S(1)} %copy-done.8, s32[1,4]{1,0:T(1,128)S(1)} %copy-done.9), custom_call_target="tpu_custom_call" | custom-call | tf_op jit(solution)/shard_map/place/pallas_call | solution.py:136
  22.0 0.9 %collective-permute-done.2.refs_0_ = bf16[256,384]{1,0:T(8,128)(2,1)S(1)} collective-permute-done((bf16[256,384]{1,0:T(8,128)(2,1)S(1)}, bf16[256,384]{1,0:T(8,128)(2,1)S(1)}, u32[]{:S(2)}, u32[]{:S(2)}) %collective-permute-start.2) | collective-permute-done | bytes 196640 | tf_op jit(solution)/shard_map/ppermute | solution.py:360
  22.9 0.0 collective-permute-done.3.refs_1_
  22.9 0.8 %collective-permute-done.8.refs_3_ = bf16[256,384]{1,0:T(8,128)(2,1)S(1)} collective-permute-done((bf16[256,384]{1,0:T(8,128)(2,1)S(1)}, bf16[256,384]{1,0:T(8,128)(2,1)S(1)}, u32[]{:S(2)}, u32[]{:S(2)}) %collective-permute-start.8) | collective-permute-done | bytes 196640 | tf_op jit(solution)/shard_map/ppermute | solution.py:360
  23.7 2.0 %collective-permute-done.5.refs_2_ = bf16[256,384]{1,0:T(8,128)(2,1)S(1)} collective-permute-done((bf16[256,384]{1,0:T(8,128)(2,1)S(1)}, bf16[256,384]{1,0:T(8,128)(2,1)S(1)}, u32[]{:S(2)}, u32[]{:S(2)}) %collective-permute-start.5) | collective-permute-done | bytes 196640 | tf_op jit(solution)/shard_map/ppermute | solution.py:360
  25.7 0.7 %finish.1 = (f32[256,256]{1,0:T(8,128)S(1)}, bf16[256,256]{1,0:T(8,128)(2,1)S(1)}) custom-call(s32[10]{0:T(128)S(1)} %place.1, f32[256,256]{1,0:T(8,128)S(1)} %get-tuple-element.38.kept, bf16[256,384]{1,0:T(8,128)(2,1)S(1)} %collective-permute-done.2.refs_0_, bf16[256,384]{1,0:T(8,128)(2,1)S(1)} %collective-permute-done.3.refs_1_, ...), custom_call_target="tpu_custom_call" | custom-call | bytes 1310760 | tf_op jit(solution)/shard_map/finish/pallas_call | solution.py:31
  26.4 0.0 copy-start.3
  26.4 3.3 %collective-permute-start.9 = (bf16[256,256]{1,0:T(8,128)(2,1)S(1)}, bf16[256,256]{1,0:T(8,128)(2,1)S(1)}, u32[]{:S(2)}, u32[]{:S(2)}) collective-permute-start(bf16[256,256]{1,0:T(8,128)(2,1)S(1)} %get-tuple-element.46.mine), channel_id=1, source_target_pairs={{0,1},{1,0},{2,3},{3,2},{4,5},{5,4},{6,7},{7,6},{8,9},{9,8},{10,11... | collective-permute-start | bytes 393224 | tf_op jit(solution)/shard_map/ppermute | solution.py:353
  29.7 1.0 %collective-permute-done.9.other = bf16[256,256]{1,0:T(8,128)(2,1)S(1)} collective-permute-done((bf16[256,256]{1,0:T(8,128)(2,1)S(1)}, bf16[256,256]{1,0:T(8,128)(2,1)S(1)}, u32[]{:S(2)}, u32[]{:S(2)}) %collective-permute-start.9) | collective-permute-done | bytes 131104 | tf_op jit(solution)/shard_map/ppermute | solution.py:353
  30.7 6.2 %attention.1 = (f32[256,256]{1,0:T(8,128)S(1)}, f32[256,256]{1,0:T(8,128)S(1)}) custom-call(s32[10]{0:T(128)S(1)} %place.1, bf16[256,256]{1,0:T(8,128)(2,1)S(1)} %get-tuple-element.46.mine, bf16[256,256]{1,0:T(8,128)(2,1)S(1)} %collective-permute-done.9.other, bf16[512,1024]{1,0:T(8,128)(2,1)S(1)} %copy-done.4, bf16[512,1024]{1,0:T(8,128)(2,1)S(1)} %copy-done.5), custom_call_target="tpu_custom_call" | custom-call | bytes 2359336 | tf_op jit(solution)/shard_map/attention/pallas_call | solution.py:31
  36.9 0.4 collective-permute-start.10
  37.3 1.2 %collective-permute-done.10.recv = f32[256,256]{1,0:T(8,128)S(1)} collective-permute-done((f32[256,256]{1,0:T(8,128)S(1)}, f32[256,256]{1,0:T(8,128)S(1)}, u32[]{:S(2)}, u32[]{:S(2)}) %collective-permute-start.10) | collective-permute-done | bytes 262176 | tf_op jit(solution)/shard_map/ppermute | solution.py:353
  38.5 0.8 %scale_grads.1 = (bf16[256,256]{1,0:T(8,128)(2,1)S(1)}, f32[32,128]{1,0:T(8,128)S(1)}, f32[32,128]{1,0:T(8,128)S(1)}) custom-call(s32[10]{0:T(128)S(1)} %place.1, f32[256,256]{1,0:T(8,128)S(1)} %get-tuple-element.47.keep, f32[256,256]{1,0:T(8,128)S(1)} %collective-permute-done.10.recv, f32[256,256]{1,0:T(8,128)S(1)} %get-tuple-element.49.base, ...), custom_call_target="tpu_custom_call" | custom-call | bytes 1048616 | tf_op jit(solution)/shard_map/scale_grads/pallas_call | solution.py:31
  39.3 1.4 %collective-permute-start.11 = (bf16[256,256]{1,0:T(8,128)(2,1)S(1)}, bf16[256,256]{1,0:T(8,128)(2,1)S(1)}, u32[]{:S(2)}, u32[]{:S(2)}) collective-permute-start(bf16[256,256]{1,0:T(8,128)(2,1)S(1)} %get-tuple-element.50.mine), channel_id=1, source_target_pairs={{0,2},{1,3},{2,0},{3,1},{4,6},{5,7},{6,4},{7,5},{8,10},{9,11},{10,... | collective-permute-start | bytes 393224 | tf_op jit(solution)/shard_map/ppermute | solution.py:360
  40.6 0.6 collective-permute-start.12
  41.3 0.8 %collective-permute-done.12.refs_1_ = f32[32,128]{1,0:T(8,128)S(1)} collective-permute-done((f32[32,128]{1,0:T(8,128)S(1)}, f32[32,128]{1,0:T(8,128)S(1)}, u32[]{:S(2)}, u32[]{:S(2)}) %collective-permute-start.12) | collective-permute-done | bytes 16416 | tf_op jit(solution)/shard_map/ppermute | solution.py:353
  42.1 0.6 collective-permute-start.13
  42.7 4.0 %collective-permute-start.14 = (f32[32,128]{1,0:T(8,128)S(1)}, f32[32,128]{1,0:T(8,128)S(1)}, u32[]{:S(2)}, u32[]{:S(2)}) collective-permute-start(f32[32,128]{1,0:T(8,128)S(1)} %add_up.2.here), channel_id=1, source_target_pairs={{32,0},{48,16},{64,32},{80,48},{96,64},{112,80},{128,96},{144,112}... | collective-permute-start | bytes 49160 | tf_op jit(solution)/shard_map/ppermute | solution.py:365
  46.6 1.1 %collective-permute-done.13.below = f32[32,128]{1,0:T(8,128)S(1)} collective-permute-done((f32[32,128]{1,0:T(8,128)S(1)}, f32[32,128]{1,0:T(8,128)S(1)}, u32[]{:S(2)}, u32[]{:S(2)}) %collective-permute-start.13) | collective-permute-done | bytes 16416 | tf_op jit(solution)/shard_map/ppermute | solution.py:365
  47.7 0.0 collective-permute-done.14.above
  47.7 0.0 collective-permute-done.11.other
  47.8 2.2 %collective-permute-start.15 = (bf16[2,256,256]{2,1,0:T(8,128)(2,1)S(1)}, bf16[2,256,256]{2,1,0:T(8,128)(2,1)S(1)}, u32[]{:S(2)}, u32[]{:S(2)}) collective-permute-start(bf16[2,256,256]{2,1,0:T(8,128)(2,1)S(1)} %get-tuple-element.57.refs_0_), channel_id=1, source_target_pairs={{0,8},{1,9},{2,10},{3,11},{4,12},{5,13},{6,14},{7,15},{8,0},{9,1},... | collective-permute-start | bytes 786440 | tf_op jit(solution)/shard_map/ppermute | solution.py:360
  50.0 1.2 %collective-permute-start.16 = (bf16[2,256,256]{2,1,0:T(8,128)(2,1)S(1)}, bf16[2,256,256]{2,1,0:T(8,128)(2,1)S(1)}, u32[]{:S(2)}, u32[]{:S(2)}) collective-permute-start(bf16[2,256,256]{2,1,0:T(8,128)(2,1)S(1)} %get-tuple-element.57.refs_0_), channel_id=1, source_target_pairs={{0,12},{1,13},{2,14},{3,15},{4,0},{5,1},{6,2},{7,3},{8,4},{9,5},{1... | collective-permute-start | bytes 786440 | tf_op jit(solution)/shard_map/ppermute | solution.py:360
  51.1 0.3 collective-permute-start.17
  51.4 3.4 %collective-permute-start.18 = (f32[32,128]{1,0:T(8,128)S(1)}, f32[32,128]{1,0:T(8,128)S(1)}, u32[]{:S(2)}, u32[]{:S(2)}) collective-permute-start(f32[32,128]{1,0:T(8,128)S(1)} %get-tuple-element.58.refs_0_), channel_id=1, source_target_pairs={{96,0},{112,16},{128,32},{144,48},{160,64},{176,80},{192,96},{208,... | collective-permute-start | bytes 49160 | tf_op jit(solution)/shard_map/ppermute | solution.py:365
  54.8 0.9 %collective-permute-start.19 = (f32[32,128]{1,0:T(8,128)S(1)}, f32[32,128]{1,0:T(8,128)S(1)}, u32[]{:S(2)}, u32[]{:S(2)}) collective-permute-start(f32[32,128]{1,0:T(8,128)S(1)} %get-tuple-element.59), channel_id=1, source_target_pairs={{160,0},{176,16},{192,32},{208,48},{224,64},{240,80},{0,96},{16,11... | collective-permute-start | bytes 49160 | tf_op jit(solution)/shard_map/ppermute | solution.py:365
  55.7 1.4 %collective-permute-done.18.refs_1_ = f32[32,128]{1,0:T(8,128)S(1)} collective-permute-done((f32[32,128]{1,0:T(8,128)S(1)}, f32[32,128]{1,0:T(8,128)S(1)}, u32[]{:S(2)}, u32[]{:S(2)}) %collective-permute-start.18) | collective-permute-done | bytes 16416 | tf_op jit(solution)/shard_map/ppermute | solution.py:365
  57.1 3.2 %collective-permute-start.20 = (bf16[2,256,256]{2,1,0:T(8,128)(2,1)S(1)}, bf16[2,256,256]{2,1,0:T(8,128)(2,1)S(1)}, u32[]{:S(2)}, u32[]{:S(2)}) collective-permute-start(bf16[2,256,256]{2,1,0:T(8,128)(2,1)S(1)} %get-tuple-element.57.refs_0_), channel_id=1, source_target_pairs={{0,1},{1,0},{2,3},{3,2},{4,5},{5,4},{6,7},{7,6},{8,9},{9,8},{10,11... | collective-permute-start | bytes 786440 | tf_op jit(solution)/shard_map/ppermute | solution.py:353
  60.3 0.1 collective-permute-done.19.refs_2_
  60.4 0.0 collective-permute-done.15.refs_1_
  60.4 1.4 %collective-permute-done.16.refs_2_ = bf16[2,256,256]{2,1,0:T(8,128)(2,1)S(1)} collective-permute-done((bf16[2,256,256]{2,1,0:T(8,128)(2,1)S(1)}, bf16[2,256,256]{2,1,0:T(8,128)(2,1)S(1)}, u32[]{:S(2)}, u32[]{:S(2)}) %collective-permute-start.16) | collective-permute-done | bytes 262176 | tf_op jit(solution)/shard_map/ppermute | solution.py:360
  61.8 0.8 %collective-permute-done.17.refs_3_ = bf16[2,256,256]{2,1,0:T(8,128)(2,1)S(1)} collective-permute-done((bf16[2,256,256]{2,1,0:T(8,128)(2,1)S(1)}, bf16[2,256,256]{2,1,0:T(8,128)(2,1)S(1)}, u32[]{:S(2)}, u32[]{:S(2)}) %collective-permute-start.17) | collective-permute-done | bytes 262176 | tf_op jit(solution)/shard_map/ppermute | solution.py:360
  62.6 1.8 %collective-permute-start.21 = (bf16[2,256,256]{2,1,0:T(8,128)(2,1)S(1)}, bf16[2,256,256]{2,1,0:T(8,128)(2,1)S(1)}, u32[]{:S(2)}, u32[]{:S(2)}) collective-permute-start(bf16[2,256,256]{2,1,0:T(8,128)(2,1)S(1)} %collective-permute-done.15.refs_1_), channel_id=1, source_target_pairs={{0,1},{1,0},{2,3},{3,2},{4,5},{5,4},{6,7},{7,6},{8,9},{9,8},{10,11... | collective-permute-start | bytes 786440 | tf_op jit(solution)/shard_map/ppermute | solution.py:353
  64.4 0.1 collective-permute-start.22
  64.5 0.4 collective-permute-start.23
  64.9 2.9 %collective-permute-start.24 = (f32[32,128]{1,0:T(8,128)S(1)}, f32[32,128]{1,0:T(8,128)S(1)}, u32[]{:S(2)}, u32[]{:S(2)}) collective-permute-start(f32[32,128]{1,0:T(8,128)S(1)} %add_up.3.here), channel_id=1, source_target_pairs={{0,16},{16,0},{32,48},{48,32},{64,80},{80,64},{96,112},{112,96},{1... | collective-permute-start | bytes 49160 | tf_op jit(solution)/shard_map/ppermute | solution.py:408
  67.9 0.0 collective-permute-done.23.refs_7_
  67.9 4.2 %input_grads.1 = bf16[512,1024]{1,0:T(8,128)(2,1)} custom-call(s32[10]{0:T(128)S(1)} %place.1, bf16[2,256,256]{2,1,0:T(8,128)(2,1)S(1)} %get-tuple-element.57.refs_0_, bf16[2,256,256]{2,1,0:T(8,128)(2,1)S(1)} %collective-permute-done.15.refs_1_, bf16[2,256,256]{2,1,0:T(8,128)(2,1)S(1)} %collective-permute-done.16.refs_2_, ...), custom_call_target="tpu_custom_call" | custom-call | flops 2147483648 | bytes 6291496 | tf_op jit(solution)/shard_map/input_grads/pallas_call | solution.py:31
  72.1 0.7 tenant_totals.1
  (21 shorter events, 0.1 us)
Async XLA Ops:
  0.6 1.2 %copy-start = (bf16[512,1024]{1,0:T(8,128)(2,1)S(1)}, bf16[512,1024]{1,0:T(8,128)(2,1)}, u32[]{:S(2)}) copy-start(bf16[512,1024]{1,0:T(8,128)(2,1)} %tokens.5) | copy-start | bytes 3145732
  1.9 1.6 %copy-start.2 = (bf16[1024,1024]{1,0:T(8,128)(2,1)S(1)}, bf16[1024,1024]{1,0:T(8,128)(2,1)}, u32[]{:S(2)}) copy-start(bf16[1024,1024]{1,0:T(8,128)(2,1)} %refs_8_.1) | copy-start | bytes 6291460
  3.4 4.0 %copy-start.1 = (bf16[1024,1024]{1,0:T(8,128)(2,1)S(1)}, bf16[1024,1024]{1,0:T(8,128)(2,1)}, u32[]{:S(2)}) copy-start(bf16[1024,1024]{1,0:T(8,128)(2,1)} %refs_9_.1) | copy-start | bytes 6291460
  4.2 6.5 %collective-permute-start = (f32[256,1024]{1,0:T(8,128)S(1)}, f32[256,1024]{1,0:T(8,128)S(1)}, u32[]{:S(2)}, u32[]{:S(2)}) collective-permute-start(f32[256,1024]{1,0:T(8,128)S(1)} %project_key.1), channel_id=1, source_target_pairs={{0,1},{1,0},{2,3},{3,2},{4,5},{5,4},{6,7},{7,6},{8,9},{9,8},{10,11... | collective-permute-start | bytes 3145736 | tf_op jit(solution)/shard_map/ppermute | solution.py:353
  8.2 2.4 %collective-permute-start.1 = (bf16[256,1024]{1,0:T(8,128)(2,1)S(1)}, bf16[256,1024]{1,0:T(8,128)(2,1)S(1)}, u32[]{:S(2)}, u32[]{:S(2)}) collective-permute-start(bf16[256,1024]{1,0:T(8,128)(2,1)S(1)} %project_value.1), channel_id=1, source_target_pairs={{0,1},{1,0},{2,3},{3,2},{4,5},{5,4},{6,7},{7,6},{8,9},{9,8},{10,11... | collective-permute-start | bytes 1572872 | tf_op jit(solution)/shard_map/ppermute | solution.py:353
  10.6 10.0 %copy-start.8 = (s32[1,512]{1,0:T(1,128)S(1)}, s32[1,512]{1,0:T(1,128)}, u32[]{:S(2)}) copy-start(s32[1,512]{1,0:T(1,128)} %segments.1) | copy-start | bytes 6148
  10.6 10.0 %copy-start.9 = (s32[1,4]{1,0:T(1,128)S(1)}, s32[1,4]{1,0:T(1,128)}, u32[]{:S(2)}) copy-start(s32[1,4]{1,0:T(1,128)} %tenants.1) | copy-start | bytes 52
  10.6 15.0 %copy-start.6 = (f32[32,1024]{1,0:T(8,128)S(1)}, f32[32,1024]{1,0:T(8,128)}, u32[]{:S(2)}) copy-start(f32[32,1024]{1,0:T(8,128)} %key_scale.1) | copy-start | bytes 393220
  10.6 15.0 %copy-start.7 = (f32[32,1024]{1,0:T(8,128)S(1)}, f32[32,1024]{1,0:T(8,128)}, u32[]{:S(2)}) copy-start(f32[32,1024]{1,0:T(8,128)} %value_scale.1) | copy-start | bytes 393220
  11.2 19.4 %copy-start.4 = (bf16[512,1024]{1,0:T(8,128)(2,1)S(1)}, bf16[512,1024]{1,0:T(8,128)(2,1)}, u32[]{:S(2)}) copy-start(bf16[512,1024]{1,0:T(8,128)(2,1)} %queries.1) | copy-start | bytes 3145732
  11.3 19.4 %copy-start.5 = (bf16[512,1024]{1,0:T(8,128)(2,1)S(1)}, bf16[512,1024]{1,0:T(8,128)(2,1)}, u32[]{:S(2)}) copy-start(bf16[512,1024]{1,0:T(8,128)(2,1)} %out_grad.1) | copy-start | bytes 3145732
  11.3 7.4 %collective-permute-start.6 = (bf16[256,384]{1,0:T(8,128)(2,1)S(1)}, bf16[256,384]{1,0:T(8,128)(2,1)S(1)}, u32[]{:S(2)}, u32[]{:S(2)}) collective-permute-start(bf16[256,384]{1,0:T(8,128)(2,1)S(1)} %get-tuple-element.44), channel_id=1, source_target_pairs={{0,4},{1,5},{2,6},{3,7},{4,8},{5,9},{6,10},{7,11},{8,12},{9,13},{1... | collective-permute-start | bytes 589832 | tf_op jit(solution)/shard_map/ppermute | solution.py:360
  11.4 7.3 %collective-permute-start.7 = (bf16[256,384]{1,0:T(8,128)(2,1)S(1)}, bf16[256,384]{1,0:T(8,128)(2,1)S(1)}, u32[]{:S(2)}, u32[]{:S(2)}) collective-permute-start(bf16[256,384]{1,0:T(8,128)(2,1)S(1)} %get-tuple-element.45), channel_id=1, source_target_pairs={{0,12},{1,13},{2,14},{3,15},{4,0},{5,1},{6,2},{7,3},{8,4},{9,5},{1... | collective-permute-start | bytes 589832 | tf_op jit(solution)/shard_map/ppermute | solution.py:360
  14.0 5.5 %collective-permute-start.4 = (bf16[256,384]{1,0:T(8,128)(2,1)S(1)}, bf16[256,384]{1,0:T(8,128)(2,1)S(1)}, u32[]{:S(2)}, u32[]{:S(2)}) collective-permute-start(bf16[256,384]{1,0:T(8,128)(2,1)S(1)} %get-tuple-element.42), channel_id=1, source_target_pairs={{0,2},{1,3},{2,0},{3,1},{4,6},{5,7},{6,4},{7,5},{8,10},{9,11},{10,... | collective-permute-start | bytes 589832 | tf_op jit(solution)/shard_map/ppermute | solution.py:360
  14.0 8.9 %collective-permute-start.2 = (bf16[256,384]{1,0:T(8,128)(2,1)S(1)}, bf16[256,384]{1,0:T(8,128)(2,1)S(1)}, u32[]{:S(2)}, u32[]{:S(2)}) collective-permute-start(bf16[256,384]{1,0:T(8,128)(2,1)S(1)} %get-tuple-element.39), channel_id=1, source_target_pairs={{0,4},{1,5},{2,6},{3,7},{4,8},{5,9},{6,10},{7,11},{8,12},{9,13},{1... | collective-permute-start | bytes 589832 | tf_op jit(solution)/shard_map/ppermute | solution.py:360
  14.0 8.9 %collective-permute-start.3 = (bf16[256,384]{1,0:T(8,128)(2,1)S(1)}, bf16[256,384]{1,0:T(8,128)(2,1)S(1)}, u32[]{:S(2)}, u32[]{:S(2)}) collective-permute-start(bf16[256,384]{1,0:T(8,128)(2,1)S(1)} %get-tuple-element.40), channel_id=1, source_target_pairs={{0,12},{1,13},{2,14},{3,15},{4,0},{5,1},{6,2},{7,3},{8,4},{9,5},{1... | collective-permute-start | bytes 589832 | tf_op jit(solution)/shard_map/ppermute | solution.py:360
  18.8 4.9 %collective-permute-start.8 = (bf16[256,384]{1,0:T(8,128)(2,1)S(1)}, bf16[256,384]{1,0:T(8,128)(2,1)S(1)}, u32[]{:S(2)}, u32[]{:S(2)}) collective-permute-start(bf16[256,384]{1,0:T(8,128)(2,1)S(1)} %relay.3), channel_id=1, source_target_pairs={{0,2},{1,3},{2,0},{3,1},{4,6},{5,7},{6,4},{7,5},{8,10},{9,11},{10,... | collective-permute-start | bytes 589832 | tf_op jit(solution)/shard_map/ppermute | solution.py:360
  19.5 6.1 %collective-permute-start.5 = (bf16[256,384]{1,0:T(8,128)(2,1)S(1)}, bf16[256,384]{1,0:T(8,128)(2,1)S(1)}, u32[]{:S(2)}, u32[]{:S(2)}) collective-permute-start(bf16[256,384]{1,0:T(8,128)(2,1)S(1)} %relay.2), channel_id=1, source_target_pairs={{0,8},{1,9},{2,10},{3,11},{4,12},{5,13},{6,14},{7,15},{8,0},{9,1},... | collective-permute-start | bytes 589832 | tf_op jit(solution)/shard_map/ppermute | solution.py:360
  26.4 41.5 %copy-start.3 = (bf16[1024,1024]{1,0:T(8,128)(2,1)S(1)}, bf16[1024,1024]{1,0:T(8,128)(2,1)}, u32[]{:S(2)}) copy-start(bf16[1024,1024]{1,0:T(8,128)(2,1)} %refs_8_.1) | copy-start | bytes 6291460
  26.4 4.3 %collective-permute-start.9 = (bf16[256,256]{1,0:T(8,128)(2,1)S(1)}, bf16[256,256]{1,0:T(8,128)(2,1)S(1)}, u32[]{:S(2)}, u32[]{:S(2)}) collective-permute-start(bf16[256,256]{1,0:T(8,128)(2,1)S(1)} %get-tuple-element.46.mine), channel_id=1, source_target_pairs={{0,1},{1,0},{2,3},{3,2},{4,5},{5,4},{6,7},{7,6},{8,9},{9,8},{10,11... | collective-permute-start | bytes 393224 | tf_op jit(solution)/shard_map/ppermute | solution.py:353
  36.9 1.6 %collective-permute-start.10 = (f32[256,256]{1,0:T(8,128)S(1)}, f32[256,256]{1,0:T(8,128)S(1)}, u32[]{:S(2)}, u32[]{:S(2)}) collective-permute-start(f32[256,256]{1,0:T(8,128)S(1)} %get-tuple-element.48), channel_id=1, source_target_pairs={{0,1},{1,0},{2,3},{3,2},{4,5},{5,4},{6,7},{7,6},{8,9},{9,8},{10,11... | collective-permute-start | bytes 786440 | tf_op jit(solution)/shard_map/ppermute | solution.py:353
  39.3 8.5 %collective-permute-start.11 = (bf16[256,256]{1,0:T(8,128)(2,1)S(1)}, bf16[256,256]{1,0:T(8,128)(2,1)S(1)}, u32[]{:S(2)}, u32[]{:S(2)}) collective-permute-start(bf16[256,256]{1,0:T(8,128)(2,1)S(1)} %get-tuple-element.50.mine), channel_id=1, source_target_pairs={{0,2},{1,3},{2,0},{3,1},{4,6},{5,7},{6,4},{7,5},{8,10},{9,11},{10,... | collective-permute-start | bytes 393224 | tf_op jit(solution)/shard_map/ppermute | solution.py:360
  40.6 1.5 %collective-permute-start.12 = (f32[32,128]{1,0:T(8,128)S(1)}, f32[32,128]{1,0:T(8,128)S(1)}, u32[]{:S(2)}, u32[]{:S(2)}) collective-permute-start(f32[32,128]{1,0:T(8,128)S(1)} %get-tuple-element.52), channel_id=1, source_target_pairs={{0,1},{1,0},{2,3},{3,2},{4,5},{5,4},{6,7},{7,6},{8,9},{9,8},{10,11... | collective-permute-start | bytes 49160 | tf_op jit(solution)/shard_map/ppermute | solution.py:353
  42.1 5.6 %collective-permute-start.13 = (f32[32,128]{1,0:T(8,128)S(1)}, f32[32,128]{1,0:T(8,128)S(1)}, u32[]{:S(2)}, u32[]{:S(2)}) collective-permute-start(f32[32,128]{1,0:T(8,128)S(1)} %add_up.2.here), channel_id=1, source_target_pairs={{224,0},{240,16},{0,32},{16,48},{32,64},{48,80},{64,96},{80,112},{... | collective-permute-start | bytes 49160 | tf_op jit(solution)/shard_map/ppermute | solution.py:365
  42.7 5.1 %collective-permute-start.14 = (f32[32,128]{1,0:T(8,128)S(1)}, f32[32,128]{1,0:T(8,128)S(1)}, u32[]{:S(2)}, u32[]{:S(2)}) collective-permute-start(f32[32,128]{1,0:T(8,128)S(1)} %add_up.2.here), channel_id=1, source_target_pairs={{32,0},{48,16},{64,32},{80,48},{96,64},{112,80},{128,96},{144,112}... | collective-permute-start | bytes 49160 | tf_op jit(solution)/shard_map/ppermute | solution.py:365
  47.8 12.7 %collective-permute-start.15 = (bf16[2,256,256]{2,1,0:T(8,128)(2,1)S(1)}, bf16[2,256,256]{2,1,0:T(8,128)(2,1)S(1)}, u32[]{:S(2)}, u32[]{:S(2)}) collective-permute-start(bf16[2,256,256]{2,1,0:T(8,128)(2,1)S(1)} %get-tuple-element.57.refs_0_), channel_id=1, source_target_pairs={{0,8},{1,9},{2,10},{3,11},{4,12},{5,13},{6,14},{7,15},{8,0},{9,1},... | collective-permute-start | bytes 786440 | tf_op jit(solution)/shard_map/ppermute | solution.py:360
  50.0 11.8 %collective-permute-start.16 = (bf16[2,256,256]{2,1,0:T(8,128)(2,1)S(1)}, bf16[2,256,256]{2,1,0:T(8,128)(2,1)S(1)}, u32[]{:S(2)}, u32[]{:S(2)}) collective-permute-start(bf16[2,256,256]{2,1,0:T(8,128)(2,1)S(1)} %get-tuple-element.57.refs_0_), channel_id=1, source_target_pairs={{0,12},{1,13},{2,14},{3,15},{4,0},{5,1},{6,2},{7,3},{8,4},{9,5},{1... | collective-permute-start | bytes 786440 | tf_op jit(solution)/shard_map/ppermute | solution.py:360
  51.1 11.4 %collective-permute-start.17 = (bf16[2,256,256]{2,1,0:T(8,128)(2,1)S(1)}, bf16[2,256,256]{2,1,0:T(8,128)(2,1)S(1)}, u32[]{:S(2)}, u32[]{:S(2)}) collective-permute-start(bf16[2,256,256]{2,1,0:T(8,128)(2,1)S(1)} %get-tuple-element.57.refs_0_), channel_id=1, source_target_pairs={{0,4},{1,5},{2,6},{3,7},{4,8},{5,9},{6,10},{7,11},{8,12},{9,13},{1... | collective-permute-start | bytes 786440 | tf_op jit(solution)/shard_map/ppermute | solution.py:360
  51.4 5.7 %collective-permute-start.18 = (f32[32,128]{1,0:T(8,128)S(1)}, f32[32,128]{1,0:T(8,128)S(1)}, u32[]{:S(2)}, u32[]{:S(2)}) collective-permute-start(f32[32,128]{1,0:T(8,128)S(1)} %get-tuple-element.58.refs_0_), channel_id=1, source_target_pairs={{96,0},{112,16},{128,32},{144,48},{160,64},{176,80},{192,96},{208,... | collective-permute-start | bytes 49160 | tf_op jit(solution)/shard_map/ppermute | solution.py:365
  54.8 5.6 %collective-permute-start.19 = (f32[32,128]{1,0:T(8,128)S(1)}, f32[32,128]{1,0:T(8,128)S(1)}, u32[]{:S(2)}, u32[]{:S(2)}) collective-permute-start(f32[32,128]{1,0:T(8,128)S(1)} %get-tuple-element.59), channel_id=1, source_target_pairs={{160,0},{176,16},{192,32},{208,48},{224,64},{240,80},{0,96},{16,11... | collective-permute-start | bytes 49160 | tf_op jit(solution)/shard_map/ppermute | solution.py:365
  57.1 10.7 %collective-permute-start.20 = (bf16[2,256,256]{2,1,0:T(8,128)(2,1)S(1)}, bf16[2,256,256]{2,1,0:T(8,128)(2,1)S(1)}, u32[]{:S(2)}, u32[]{:S(2)}) collective-permute-start(bf16[2,256,256]{2,1,0:T(8,128)(2,1)S(1)} %get-tuple-element.57.refs_0_), channel_id=1, source_target_pairs={{0,1},{1,0},{2,3},{3,2},{4,5},{5,4},{6,7},{7,6},{8,9},{9,8},{10,11... | collective-permute-start | bytes 786440 | tf_op jit(solution)/shard_map/ppermute | solution.py:353
  62.6 5.3 %collective-permute-start.21 = (bf16[2,256,256]{2,1,0:T(8,128)(2,1)S(1)}, bf16[2,256,256]{2,1,0:T(8,128)(2,1)S(1)}, u32[]{:S(2)}, u32[]{:S(2)}) collective-permute-start(bf16[2,256,256]{2,1,0:T(8,128)(2,1)S(1)} %collective-permute-done.15.refs_1_), channel_id=1, source_target_pairs={{0,1},{1,0},{2,3},{3,2},{4,5},{5,4},{6,7},{7,6},{8,9},{9,8},{10,11... | collective-permute-start | bytes 786440 | tf_op jit(solution)/shard_map/ppermute | solution.py:353
  64.4 3.5 %collective-permute-start.22 = (bf16[2,256,256]{2,1,0:T(8,128)(2,1)S(1)}, bf16[2,256,256]{2,1,0:T(8,128)(2,1)S(1)}, u32[]{:S(2)}, u32[]{:S(2)}) collective-permute-start(bf16[2,256,256]{2,1,0:T(8,128)(2,1)S(1)} %collective-permute-done.16.refs_2_), channel_id=1, source_target_pairs={{0,1},{1,0},{2,3},{3,2},{4,5},{5,4},{6,7},{7,6},{8,9},{9,8},{10,11... | collective-permute-start | bytes 786440 | tf_op jit(solution)/shard_map/ppermute | solution.py:353
  64.5 3.4 %collective-permute-start.23 = (bf16[2,256,256]{2,1,0:T(8,128)(2,1)S(1)}, bf16[2,256,256]{2,1,0:T(8,128)(2,1)S(1)}, u32[]{:S(2)}, u32[]{:S(2)}) collective-permute-start(bf16[2,256,256]{2,1,0:T(8,128)(2,1)S(1)} %collective-permute-done.17.refs_3_), channel_id=1, source_target_pairs={{0,1},{1,0},{2,3},{3,2},{4,5},{5,4},{6,7},{7,6},{8,9},{9,8},{10,11... | collective-permute-start | bytes 786440 | tf_op jit(solution)/shard_map/ppermute | solution.py:353
  64.9 7.2 %collective-permute-start.24 = (f32[32,128]{1,0:T(8,128)S(1)}, f32[32,128]{1,0:T(8,128)S(1)}, u32[]{:S(2)}, u32[]{:S(2)}) collective-permute-start(f32[32,128]{1,0:T(8,128)S(1)} %add_up.3.here), channel_id=1, source_target_pairs={{0,16},{16,0},{32,48},{48,32},{64,80},{80,64},{96,112},{112,96},{1... | collective-permute-start | bytes 49160 | tf_op jit(solution)/shard_map/ppermute | solution.py:408

commit v4 on v3

--- a/solution.py
+++ b/solution.py
@@ -50,7 +50,7 @@
 
 
 CORE_SWAP = tensor_pairs(lambda x, y, core: (x, y, core ^ 1))
-X_ORDER = [0, 2, 1, 3]
+ORDER = [(0, 0), (0, 1), (2, 0), (1, 0), (1, 1), (3, 0), (3, 1), (2, 1)]
 SENT = [(2, 1), (1, 1), (3, 1), (1, 0), (3, 0)]
 KEPT = [(2, 0), (0, 1), (0, 0)]
 
@@ -242,73 +242,106 @@
     )
 
 
-def scale_body(place, keep, recv, base, key_scale, value_scale, low, own, give):
+def scale_body(place, keep, recv, key_scale, value_scale, low):
     sequences = own_sequences(place)
-    tables = []
     for part, scale in enumerate((key_scale, value_scale)):
         columns = slice(part * HEAD, (part + 1) * HEAD)
         grad = keep[:, columns] + recv[:, columns]
         low[:, columns] = (grad * token_factor(place, scale, sequences)).astype(BF)
-        product = grad * base[:, columns]
-        later = [jnp.sum(product, axis=0, keepdims=True)]
+
+
+def scale_grads(*args):
+    return call("scale_grads", scale_body, [((HALF, 2 * HEAD), BF)], args)[0]
+
+
+def table_body(place, keep, send, base, base_other, sums):
+    width = 2 * HEAD
+    totals = [jnp.zeros((1, width), F32)] * (SEQS + 1)
+    for half, grad, values in ((place[0], keep, base), (1 - place[0], send, base_other)):
+        product = grad[...] * values[...]
+        row = lax.broadcasted_iota(jnp.int32, product.shape, 0) + half * HALF
+        totals[0] += jnp.sum(product, axis=0, keepdims=True)
         for seq in range(1, SEQS):
-            later.append(jnp.sum(jnp.where(sequences[seq - 1], product, 0.0), axis=0, keepdims=True))
-        later.append(jnp.zeros_like(later[0]))
-        row = lax.broadcasted_iota(jnp.int32, (NT, HEAD), 0)
-        table = jnp.zeros((NT, HEAD), F32)
-        for seq in range(SEQS):
-            table = table + jnp.where(row == place[5 + seq], later[seq] - later[seq + 1], 0.0)
-        tables.append(table)
-    key, value = tables
-    lower = lax.broadcasted_iota(jnp.int32, (NT, HEAD), 1) < HEAD // 2
-    first = jnp.where(lower, key, pltpu.roll(value, HEAD // 2, 1))
-    second = jnp.where(lower, pltpu.roll(key, HEAD // 2, 1), value)
-    own[...] = jnp.where(place[0] == 0, first, second)
-    give[...] = jnp.where(place[0] == 0, second, first)
-
-
-def scale_grads(*args):
-    outs = [((HALF, 2 * HEAD), BF), ((NT, HEAD), F32), ((NT, HEAD), F32)]
-    return call("scale_grads", scale_body, outs, args)
-
-
-def input_body(place, *refs):
-    mine, other = refs[: CHIPS // 2], refs[CHIPS // 2 : CHIPS]
-    key_weight, value_weight, out, left_key, left_value, totals, sems = refs[CHIPS:]
-    core, chip = place[0], place[9]
-    for half, pieces in ((core, mine), (1 - core, other)):
+            later = jnp.where(row >= place[1 + seq], product, 0.0)
+            totals[seq] += jnp.sum(later, axis=0, keepdims=True)
+    tenant = lax.broadcasted_iota(jnp.int32, sums.shape, 0)
+    table = jnp.zeros(sums.shape, F32)
+    for seq in range(SEQS):
+        table += jnp.where(tenant == place[5 + seq], totals[seq] - totals[seq + 1], 0.0)
+    sums[...] = table
+
+
+def tenant_table(*args):
+    return call("tenant_table", table_body, [((NT, 2 * HEAD), F32)], args, mib=8)[0]
+
+
+def order_body(key_weight, value_weight, out):
+    chip = lax.div(lax.axis_index("tensor"), 2)
+    for index, (across, row) in enumerate(ORDER):
+        columns = pl.ds(pl.multiple_of(home_of(chip, across, row) * HEAD, HEAD), HEAD)
+        start = 2 * index * HEAD
+        out[:, start : start + HEAD] = key_weight[:, columns]
+        out[:, start + HEAD : start + 2 * HEAD] = value_weight[:, columns]
+
+
+def order_weights(key_weight, value_weight):
+    features, depth = key_weight.shape
+    outs = [((features, 2 * depth), BF)]
+    return call("order_weights", order_body, outs, [key_weight, value_weight])[0]
+
+
+def place_rows(place, left, mine, other):
+    for half, pieces in ((place[0], mine), (1 - place[0], other)):
         rows = pl.ds(pl.multiple_of(half * HALF, HALF), HALF)
-        for across, piece in zip(X_ORDER, pieces):
-            for row in range(2):
-                columns = pl.ds(pl.multiple_of(home_of(chip, across, row) * HEAD, HEAD), HEAD)
-                left_key[rows, columns] = piece[row, :, :HEAD]
-                left_value[rows, columns] = piece[row, :, HEAD:]
+        chunks = [piece[row] for piece in pieces for row in range(piece.shape[0])]
+        for index, chunk in enumerate(chunks):
+            left[rows, 2 * index * HEAD : 2 * (index + 1) * HEAD] = chunk
+
+
+def near_body(place, mine, mine_far, other, other_far, weight, out, left):
+    place_rows(place, left, [mine, mine_far], [other, other_far])
+    out[...] = contract_last(left[...], weight[:, : left.shape[1]])
+
+
+def near_grads(place, mine, other, weight):
+    features = weight.shape[0]
+    scratch = [pltpu.VMEM((TOK, 6 * HEAD), BF)]
+    outs = [((TOK, features), F32)]
+    flops = 2 * TOK * features * 6 * HEAD
+    args = [place, *mine, *other, weight]
+    return call("near_grads", near_body, outs, args, scratch, 8, flops)[0]
+
+
+def far_body(place, *refs):
+    count = len(refs) // 2 - 3
+    mine, other = refs[:count], refs[count : 2 * count]
+    near, weight, out, left, totals, sems = refs[2 * count :]
+    place_rows(place, left, mine, other)
     writes = []
     steps, width = totals.shape[0], totals.shape[2]
     for step in range(steps):
         columns = pl.ds(step * width, width)
-        total = contract_last(left_key[...], key_weight[columns, :])
-        total += contract_last(left_value[...], value_weight[columns, :])
-        totals[step] = total.astype(BF)
+        total = contract_last(left[...], weight[columns, weight.shape[1] - left.shape[1] :])
+        totals[step] = (near[:, columns] + total).astype(BF)
         writes.append(pltpu.make_async_copy(totals.at[step], out.at[:, columns], sems.at[step]))
         writes[-1].start()
     for write in writes:
         write.wait()
 
 
-def input_grads(place, mine, other, key_weight, value_weight):
-    features, depth = key_weight.shape
+def far_grads(place, mine, other, near, weight):
+    features = weight.shape[0]
+    depth = 10 * HEAD
     steps = 4
     scratch = [
-        pltpu.VMEM((TOK, depth), BF),
         pltpu.VMEM((TOK, depth), BF),
         pltpu.VMEM((steps, TOK, features // steps), BF),
         pltpu.SemaphoreType.DMA((steps,)),
     ]
     outs = [((TOK, features), BF)]
-    args = [place, *mine, *other, key_weight, value_weight]
-    flops = 4 * TOK * features * depth
-    return call("input_grads", input_body, outs, args, scratch, 20, flops, out_space=pltpu.HBM)[0]
+    args = [place, *mine, *other, near, weight]
+    flops = 2 * TOK * features * depth
+    return call("far_grads", far_body, outs, args, scratch, 16, flops, out_space=pltpu.HBM)[0]
 
 
 def add_body(*refs):
@@ -322,22 +355,44 @@
     return call("add_up", add_body, [(parts[0].shape, F32)], parts, mib=4)[0]
 
 
-def pair_body(mine, other, here, below, above, out, three, two):
+def pair_body(mine, other, out):
     out[0] = mine[...]
     out[1] = other[...]
-    two[...] = here[...] + above[...]
-    three[...] = two[...] + below[...]
-
-
-def pair_up(*args):
-    outs = [((2,) + args[0].shape, BF), (args[2].shape, F32), (args[2].shape, F32)]
-    return call("pair", pair_body, outs, args, mib=4)
+
+
+def pair_up(mine, other):
+    return call("pair", pair_body, [((2,) + mine.shape, BF)], [mine, other], mib=4)[0]
+
+
+def own_core():
+    return lax.rem(lax.axis_index("tensor"), 2)
+
+
+def ring_body(here, direct, swapped, three, give):
+    total = here[...] + direct[...]
+    full = total + swapped[...]
+    three[...] = full
+    give[...] = jnp.where(own_core() == 0, full, total)
+
+
+def ring_sums(*parts):
+    return call("ring_sums", ring_body, [(parts[0].shape, F32)] * 2, parts, mib=4)
+
+
+def ring_end_body(three, recv, out):
+    out[...] = jnp.where(own_core() == 0, three[...], 0.0) + recv[...]
+
+
+def ring_end(*parts):
+    return call("ring_end", ring_end_body, [(parts[0].shape, F32)], parts, mib=4)[0]
 
 
 def total_body(here, recv, key, value):
     total = here[...] + recv[...]
-    key[...] = total[:, : HEAD // 2]
-    value[...] = total[:, HEAD // 2 :]
+    own = lax.broadcasted_iota(jnp.int32, (NT, HEAD // 2), 1) >= 0
+    own = own & (own_core() == 0)
+    key[...] = jnp.where(own, total[:, : HEAD // 2], total[:, HEAD // 2 : HEAD])
+    value[...] = jnp.where(own, total[:, HEAD : HEAD + HEAD // 2], total[:, HEAD + HEAD // 2 :])
 
 
 def tenant_totals(here, recv):
@@ -360,9 +415,16 @@
     return lax.ppermute(array, "tensor", pairs)
 
 
-def depth_from(array, step):
-    pairs = [((z + step) % 8 * 2 + row, z * 2 + row) for z in range(8) for row in range(2)]
-    return lax.ppermute(array, "dp", pairs)
+def depth_from(array, steps):
+    pairs = []
+    for z in range(8):
+        for row in range(2):
+            for chip in range(CHIPS):
+                for core in range(2):
+                    source = (z + steps[core]) % 8 * 2 + row
+                    place = chip * 2 + core
+                    pairs.append((source * 16 + place, (z * 2 + row) * 16 + place))
+    return lax.ppermute(array, ("dp", "tensor"), pairs)
 
 
 def on_device(
@@ -393,24 +455,37 @@
         chip_from(part_20, 2, 0),
         chip_from(part_01, 0, 1),
     ]
+    weight = order_weights(key_weight, value_weight)
+    parts, weight, place = lax.optimization_barrier((parts, weight, place))
     base, low = finish(place, kept_00, *parts, key_scale, value_scale)
-    send, keep = attention(place, low, core_swap(low), queries, out_grad)
-    grad_low, own, give = scale_grads(place, keep, core_swap(send), base, key_scale, value_scale)
-    sums = add_up(own, core_swap(give))
-    arrived = lax.optimization_barrier(
-        (chip_from(grad_low, 0, 1), sums, depth_from(sums, -1), depth_from(sums, 1))
+    low_other = core_swap(low)
+    base_other = core_swap(base)
+    send, keep = attention(place, low, low_other, queries, out_grad)
+    recv = core_swap(send)
+    sums = tenant_table(place, keep, send, base, base_other)
+    recv, sums = lax.optimization_barrier((recv, sums))
+    grad_low = scale_grads(place, keep, recv, key_scale, value_scale)
+    grad_low, sums_other = lax.optimization_barrier((grad_low, core_swap(sums)))
+    sums = add_up(sums, sums_other)
+    row_part, far_part, ring = lax.optimization_barrier(
+        (chip_from(grad_low, 0, 1), chip_from(grad_low, 2, 0), depth_from(sums, (-1, 1)))
     )
-    pair, three, two = pair_up(grad_low, *arrived)
-    near = [chip_from(pair, across, 0) for across in X_ORDER[1:]]
-    far = [depth_from(three, 3), depth_from(two, -3)]
-    near, far = lax.optimization_barrier((near, far))
-    sums = add_up(three, *far)
-    sums_other = lax.ppermute(sums, "dp", [(i, i ^ 1) for i in range(16)])
-    mine = [pair] + near
-    other = [core_swap(piece) for piece in mine]
-    input_grad = input_grads(place, mine, other, key_weight, value_weight)
-    input_grad, sums_other = lax.optimization_barrier((input_grad, sums_other))
-    key_total, value_total = tenant_totals(sums, sums_other)
+    pair = pair_up(grad_low, row_part)
+    three, give = ring_sums(sums, ring, core_swap(ring))
+    early = [pair, far_part[None]]
+    near = near_grads(place, early, [core_swap(piece) for piece in early], weight)
+    arrived = [chip_from(pair, 1, 0), chip_from(pair, 3, 0), chip_from(far_part, 0, 1)]
+    arrived, ring, near = lax.optimization_barrier((arrived, depth_from(give, (3, -3)), near))
+    arrived = arrived[:2] + [arrived[2][None]]
+    sums = ring_end(three, ring)
+    others, sums_other = lax.optimization_barrier(
+        ([core_swap(piece) for piece in arrived], core_swap(sums))
+    )
+    sums = add_up(sums, sums_other)
+    row_sums = lax.ppermute(sums, "dp", [(i, i ^ 1) for i in range(16)])
+    input_grad = far_grads(place, arrived, others, near, weight)
+    input_grad, row_sums = lax.optimization_barrier((input_grad, row_sums))
+    key_total, value_total = tenant_totals(sums, row_sums)
     return input_grad, key_total, value_total
 
 

time: 73 us -> 69.7 us (0.955)
  starting transfers between devices: 37.5 us -> 33.1 us
  Pallas kernels: 17.3 us -> 19.4 us
  waiting for transfers between devices: 14.3 us -> 13.4 us
    ppermute x9 -> x13, starting transfers between devices: 14.1 us -> 10.8 us  [core_swap(): return lax.ppermute(array, 'tensor', CORE_SWAP)]
    ppermute x11 -> x12, waiting for transfers between devices: 8.42 us -> 5.58 us  [chip_from(): return lax.ppermute(array, 'tensor', pairs)]
    ppermute x5 -> x3, starting transfers between devices: 11.8 us -> 9.19 us  [the longest x2 6.48 us: depth_from(): return lax.ppermute(array, ('dp', 'tensor'), pairs)]
    pallas_call x13 -> x18, Pallas kernels: 15.3 us -> 17.4 us  [call(): pl.pallas_call(body, in_specs=[pl.BlockSpec(memory_space=space) for space...]
    ppermute x11 -> x12, starting transfers between devices: 11.7 us -> 13.1 us  [chip_from(): return lax.ppermute(array, 'tensor', pairs)]
    ppermute x5 -> x3, waiting for transfers between devices: 2.6 us -> 3.9 us  [the longest x2 3.89 us: depth_from(): return lax.ppermute(array, ('dp', 'tensor'), pairs)]
    ppermute x9 -> x13, waiting for transfers between devices: 3.28 us -> 3.89 us  [core_swap(): return lax.ppermute(array, 'tensor', CORE_SWAP)]
  transfers between devices with their start and end apart: 25 -> 28, of which waited for: 14 -> 12; matrix products, arithmetic and copies ran while one was open for 0% -> 0% of each run, Pallas kernels for 10% -> 24%
where the time goes in v4:
time: 69.7 us; the launch traced here: 69.6 us
  starting transfers between devices  33.1 us (47%)
  Pallas kernels  19.4 us (28%)
  waiting for transfers between devices  13.4 us (19%)
  local copies, waits for them, and re-layouts  2.86 us (4%)
  between operations  0.88 us (1%)
    pallas_call x18, Pallas kernels, call(): pl.pallas_call(body, in_specs=[pl.BlockSpec(memory_space=space) for space...  17.4 us
    ppermute x12, starting transfers between devices, chip_from(): return lax.ppermute(array, 'tensor', pairs)  13.1 us
    ppermute x13, starting transfers between devices, core_swap(): return lax.ppermute(array, 'tensor', CORE_SWAP)  10.8 us
    ppermute x2, starting transfers between devices, depth_from(): return lax.ppermute(array, ('dp', 'tensor'), pairs)  6.48 us
    ppermute x12, waiting for transfers between devices, chip_from(): return lax.ppermute(array, 'tensor', pairs)  5.58 us
    ppermute x2, waiting for transfers between devices, depth_from(): return lax.ppermute(array, ('dp', 'tensor'), pairs)  3.89 us
    ppermute x13, waiting for transfers between devices, core_swap(): return lax.ppermute(array, 'tensor', CORE_SWAP)  3.89 us
    unnamed x20, local copies, waits for them, and re-layouts  2.86 us
  transfers between devices with their start and end apart: 28, of which 12 were waited for; matrix products, arithmetic and copies ran while one was open for 0% of the time, Pallas kernels for 24%

profile of v4, /device:TPU:1, one launch (start us, length us, event | category | flops | bytes accessed | tf_op | source)
XLA Modules:
  0.0 69.6 jit_solution(17193495763687215638)
XLA Ops:
  0.6 0.0 copy-start
  0.6 1.6 %copy-done = bf16[1024,1024]{1,0:T(8,128)(2,1)S(1)} copy-done((bf16[1024,1024]{1,0:T(8,128)(2,1)S(1)}, bf16[1024,1024]{1,0:T(8,128)(2,1)}, u32[]{:S(2)}) %copy-start) | copy-done | bytes 2097176
  2.2 1.2 %copy-done.3 = bf16[512,1024]{1,0:T(8,128)(2,1)S(1)} copy-done((bf16[512,1024]{1,0:T(8,128)(2,1)S(1)}, bf16[512,1024]{1,0:T(8,128)(2,1)}, u32[]{:S(2)}) %copy-start.3) | copy-done | bytes 1048600
  3.5 0.7 %project_key.1 = f32[256,1024]{1,0:T(8,128)S(1)} custom-call(bf16[512,1024]{1,0:T(8,128)(2,1)S(1)} %copy-done.3, bf16[1024,1024]{1,0:T(8,128)(2,1)S(1)} %copy-done), custom_call_target="tpu_custom_call" | custom-call | flops 536870912 | bytes 3145728 | tf_op jit(solution)/shard_map/project_key/pallas_call | solution.py:31
  4.2 0.0 copy-start.1
  4.2 3.3 %collective-permute-start = (f32[256,1024]{1,0:T(8,128)S(1)}, f32[256,1024]{1,0:T(8,128)S(1)}, u32[]{:S(2)}, u32[]{:S(2)}) collective-permute-start(f32[256,1024]{1,0:T(8,128)S(1)} %project_key.1), channel_id=1, source_target_pairs={{0,1},{1,0},{2,3},{3,2},{4,5},{5,4},{6,7},{7,6},{8,9},{9,8},{10,11... | collective-permute-start | bytes 3145736 | tf_op jit(solution)/shard_map/ppermute | solution.py:408
  7.5 0.7 %project_value.1 = bf16[256,1024]{1,0:T(8,128)(2,1)S(1)} custom-call(bf16[512,1024]{1,0:T(8,128)(2,1)S(1)} %copy-done.3, bf16[1024,1024]{1,0:T(8,128)(2,1)S(1)} %copy-done.2), custom_call_target="tpu_custom_call" | custom-call | flops 536870912 | bytes 3145728 | tf_op jit(solution)/shard_map/project_value/pallas_call | solution.py:31
  8.2 0.9 %collective-permute-start.1 = (bf16[256,1024]{1,0:T(8,128)(2,1)S(1)}, bf16[256,1024]{1,0:T(8,128)(2,1)S(1)}, u32[]{:S(2)}, u32[]{:S(2)}) collective-permute-start(bf16[256,1024]{1,0:T(8,128)(2,1)S(1)} %project_value.1), channel_id=1, source_target_pairs={{0,1},{1,0},{2,3},{3,2},{4,5},{5,4},{6,7},{7,6},{8,9},{9,8},{10,11... | collective-permute-start | bytes 1572872 | tf_op jit(solution)/shard_map/ppermute | solution.py:408
  9.1 1.3 %project_keep.1 = (f32[256,1024]{1,0:T(8,128)S(1)}, f32[256,1024]{1,0:T(8,128)S(1)}) custom-call(bf16[512,1024]{1,0:T(8,128)(2,1)S(1)} %copy-done.3, bf16[1024,1024]{1,0:T(8,128)(2,1)S(1)} %copy-done.1, bf16[1024,1024]{1,0:T(8,128)(2,1)S(1)} %copy-done.2), custom_call_target="tpu_custom_call" | custom-call | flops 1073741824 | bytes 5242880 | tf_op jit(solution)/shard_map/project_keep/pallas_call | solution.py:31
  10.4 0.3 collective-permute-done.1.value_recv
  10.6 0.0 collective-permute-done.key_recv
  10.6 0.6 pack.1
  11.2 0.1 collective-permute-start.4
  11.3 0.8 %collective-permute-start.6 = (bf16[256,384]{1,0:T(8,128)(2,1)S(1)}, bf16[256,384]{1,0:T(8,128)(2,1)S(1)}, u32[]{:S(2)}, u32[]{:S(2)}) collective-permute-start(bf16[256,384]{1,0:T(8,128)(2,1)S(1)} %get-tuple-element.52), channel_id=1, source_target_pairs={{0,4},{1,5},{2,6},{3,7},{4,8},{5,9},{6,10},{7,11},{8,12},{9,13},{1... | collective-permute-start | bytes 589832 | tf_op jit(solution)/shard_map/ppermute | solution.py:415
  12.1 2.0 %collective-permute-start.7 = (bf16[256,384]{1,0:T(8,128)(2,1)S(1)}, bf16[256,384]{1,0:T(8,128)(2,1)S(1)}, u32[]{:S(2)}, u32[]{:S(2)}) collective-permute-start(bf16[256,384]{1,0:T(8,128)(2,1)S(1)} %get-tuple-element.53), channel_id=1, source_target_pairs={{0,12},{1,13},{2,14},{3,15},{4,0},{5,1},{6,2},{7,3},{8,4},{9,5},{1... | collective-permute-start | bytes 589832 | tf_op jit(solution)/shard_map/ppermute | solution.py:415
  14.1 2.7 %collective-permute-start.3 = (bf16[256,384]{1,0:T(8,128)(2,1)S(1)}, bf16[256,384]{1,0:T(8,128)(2,1)S(1)}, u32[]{:S(2)}, u32[]{:S(2)}) collective-permute-start(bf16[256,384]{1,0:T(8,128)(2,1)S(1)} %get-tuple-element.48), channel_id=1, source_target_pairs={{0,12},{1,13},{2,14},{3,15},{4,0},{5,1},{6,2},{7,3},{8,4},{9,5},{1... | collective-permute-start | bytes 589832 | tf_op jit(solution)/shard_map/ppermute | solution.py:415
  16.7 0.7 collective-permute-done.4.refs_0_
  17.4 0.1 relay.2
  17.5 1.1 %collective-permute-start.5 = (bf16[256,384]{1,0:T(8,128)(2,1)S(1)}, bf16[256,384]{1,0:T(8,128)(2,1)S(1)}, u32[]{:S(2)}, u32[]{:S(2)}) collective-permute-start(bf16[256,384]{1,0:T(8,128)(2,1)S(1)} %relay.2), channel_id=1, source_target_pairs={{0,8},{1,9},{2,10},{3,11},{4,12},{5,13},{6,14},{7,15},{8,0},{9,1},... | collective-permute-start | bytes 589832 | tf_op jit(solution)/shard_map/ppermute | solution.py:415
  18.6 0.1 collective-permute-done.6.refs_0_
  18.7 0.1 relay.3
  18.8 0.0 copy-start.8
  18.8 0.0 copy-start.9
  18.8 0.0 copy-start.6
  18.8 0.0 copy-start.7
  18.8 0.0 copy-start.4
  18.9 0.0 copy-start.5
  18.9 1.2 %collective-permute-start.8 = (bf16[256,384]{1,0:T(8,128)(2,1)S(1)}, bf16[256,384]{1,0:T(8,128)(2,1)S(1)}, u32[]{:S(2)}, u32[]{:S(2)}) collective-permute-start(bf16[256,384]{1,0:T(8,128)(2,1)S(1)} %relay.3), channel_id=1, source_target_pairs={{0,2},{1,3},{2,0},{3,1},{4,6},{5,7},{6,4},{7,5},{8,10},{9,11},{10,... | collective-permute-start | bytes 589832 | tf_op jit(solution)/shard_map/ppermute | solution.py:415
  20.1 1.1 %order_weights.1.weight.refs_7_ = bf16[1024,2048]{1,0:T(8,128)(2,1)S(1)} custom-call(bf16[1024,1024]{1,0:T(8,128)(2,1)S(1)} %copy-done.1, bf16[1024,1024]{1,0:T(8,128)(2,1)S(1)} %copy-done.2), custom_call_target="tpu_custom_call" | custom-call | bytes 4194304 | tf_op jit(solution)/shard_map/order_weights/pallas_call | solution.py:31
  21.2 1.3 %place.1 = s32[10]{0:T(128)S(1)} custom-call(s32[1,512]{1,0:T(1,128)S(1)} %copy-done.8, s32[1,4]{1,0:T(1,128)S(1)} %copy-done.9), custom_call_target="tpu_custom_call" | custom-call | tf_op jit(solution)/shard_map/place/pallas_call | solution.py:136
  22.5 0.4 collective-permute-done.2.refs_0_
  22.9 4.3 %collective-permute-done.5.refs_2_ = bf16[256,384]{1,0:T(8,128)(2,1)S(1)} collective-permute-done((bf16[256,384]{1,0:T(8,128)(2,1)S(1)}, bf16[256,384]{1,0:T(8,128)(2,1)S(1)}, u32[]{:S(2)}, u32[]{:S(2)}) %collective-permute-start.5) | collective-permute-done | bytes 196640 | tf_op jit(solution)/shard_map/ppermute | solution.py:415
  27.3 0.7 %finish.1 = (f32[256,256]{1,0:T(8,128)S(1)}, bf16[256,256]{1,0:T(8,128)(2,1)S(1)}) custom-call(s32[10]{0:T(128)S(1)} %place.1, f32[256,256]{1,0:T(8,128)S(1)} %get-tuple-element.55.kept, bf16[256,384]{1,0:T(8,128)(2,1)S(1)} %collective-permute-done.2.refs_0_, bf16[256,384]{1,0:T(8,128)(2,1)S(1)} %collective-permute-done.3.refs_1_, ...), custom_call_target="tpu_custom_call" | custom-call | bytes 1310760 | tf_op jit(solution)/shard_map/finish/pallas_call | solution.py:31
  28.0 1.6 %collective-permute-start.9 = (bf16[256,256]{1,0:T(8,128)(2,1)S(1)}, bf16[256,256]{1,0:T(8,128)(2,1)S(1)}, u32[]{:S(2)}, u32[]{:S(2)}) collective-permute-start(bf16[256,256]{1,0:T(8,128)(2,1)S(1)} %get-tuple-element.60.mine), channel_id=1, source_target_pairs={{0,1},{1,0},{2,3},{3,2},{4,5},{5,4},{6,7},{7,6},{8,9},{9,8},{10,11... | collective-permute-start | bytes 393224 | tf_op jit(solution)/shard_map/ppermute | solution.py:408
  29.6 0.3 collective-permute-start.11
  29.9 0.7 %collective-permute-done.9.other = bf16[256,256]{1,0:T(8,128)(2,1)S(1)} collective-permute-done((bf16[256,256]{1,0:T(8,128)(2,1)S(1)}, bf16[256,256]{1,0:T(8,128)(2,1)S(1)}, u32[]{:S(2)}, u32[]{:S(2)}) %collective-permute-start.9) | collective-permute-done | bytes 131104 | tf_op jit(solution)/shard_map/ppermute | solution.py:408
  30.6 6.2 %attention.1 = (f32[256,256]{1,0:T(8,128)S(1)}, f32[256,256]{1,0:T(8,128)S(1)}) custom-call(s32[10]{0:T(128)S(1)} %place.1, bf16[256,256]{1,0:T(8,128)(2,1)S(1)} %get-tuple-element.60.mine, bf16[256,256]{1,0:T(8,128)(2,1)S(1)} %collective-permute-done.9.other, bf16[512,1024]{1,0:T(8,128)(2,1)S(1)} %copy-done.4, bf16[512,1024]{1,0:T(8,128)(2,1)S(1)} %copy-done.5), custom_call_target="tpu_custom_call" | custom-call | bytes 2359336 | tf_op jit(solution)/shard_map/attention/pallas_call | solution.py:31
  36.8 0.4 collective-permute-start.10
  37.2 0.8 %tenant_table.1.refs_0_ = f32[32,256]{1,0:T(8,128)S(1)} custom-call(s32[10]{0:T(128)S(1)} %place.1, f32[256,256]{1,0:T(8,128)S(1)} %get-tuple-element.61.keep, f32[256,256]{1,0:T(8,128)S(1)} %get-tuple-element.62.send, f32[256,256]{1,0:T(8,128)S(1)} %get-tuple-element.63.base, f32[256,256]{1,0:T(8,128)S(1)} %collective-permute-done.11.base_other), custom_call_target="tpu_custom_call" | custom-call | bytes 1048616 | tf_op jit(solution)/shard_map/tenant_table/pallas_call | solution.py:31
  38.0 0.4 collective-permute-done.10.recv
  38.4 0.4 collective-permute-start.12
  38.8 0.6 scale_grads.1.mine
  39.4 0.2 collective-permute-done.12.refs_1_
  39.6 0.6 collective-permute-start.14
  40.2 0.7 collective-permute-start.13
  40.9 5.1 %collective-permute-start.15 = (f32[32,256]{1,0:T(8,128)S(1)}, f32[32,256]{1,0:T(8,128)S(1)}, u32[]{:S(2)}, u32[]{:S(2)}) collective-permute-start(f32[32,256]{1,0:T(8,128)S(1)} %add_up.2.here), channel_id=1, source_target_pairs={{224,0},{33,1},{226,2},{35,3},{228,4},{37,5},{230,6},{39,7},{232,8... | collective-permute-start | bytes 98312 | tf_op jit(solution)/shard_map/ppermute | solution.py:427
  45.9 1.0 %collective-permute-done.15.direct = f32[32,256]{1,0:T(8,128)S(1)} collective-permute-done((f32[32,256]{1,0:T(8,128)S(1)}, f32[32,256]{1,0:T(8,128)S(1)}, u32[]{:S(2)}, u32[]{:S(2)}) %collective-permute-start.15) | collective-permute-done | bytes 32800 | tf_op jit(solution)/shard_map/ppermute | solution.py:427
  47.0 2.1 %collective-permute-start.21 = (bf16[2,256,256]{2,1,0:T(8,128)(2,1)S(1)}, bf16[2,256,256]{2,1,0:T(8,128)(2,1)S(1)}, u32[]{:S(2)}, u32[]{:S(2)}) collective-permute-start(bf16[2,256,256]{2,1,0:T(8,128)(2,1)S(1)} %pair.1.mine), channel_id=1, source_target_pairs={{0,1},{1,0},{2,3},{3,2},{4,5},{5,4},{6,7},{7,6},{8,9},{9,8},{10,11... | collective-permute-start | bytes 786440 | tf_op jit(solution)/shard_map/ppermute | solution.py:408
  49.1 1.8 %collective-permute-start.17 = (bf16[2,256,256]{2,1,0:T(8,128)(2,1)S(1)}, bf16[2,256,256]{2,1,0:T(8,128)(2,1)S(1)}, u32[]{:S(2)}, u32[]{:S(2)}) collective-permute-start(bf16[2,256,256]{2,1,0:T(8,128)(2,1)S(1)} %pair.1.mine), channel_id=1, source_target_pairs={{0,4},{1,5},{2,6},{3,7},{4,8},{5,9},{6,10},{7,11},{8,12},{9,13},{1... | collective-permute-start | bytes 786440 | tf_op jit(solution)/shard_map/ppermute | solution.py:415
  50.9 0.9 %collective-permute-start.16 = (bf16[2,256,256]{2,1,0:T(8,128)(2,1)S(1)}, bf16[2,256,256]{2,1,0:T(8,128)(2,1)S(1)}, u32[]{:S(2)}, u32[]{:S(2)}) collective-permute-start(bf16[2,256,256]{2,1,0:T(8,128)(2,1)S(1)} %pair.1.mine), channel_id=1, source_target_pairs={{0,12},{1,13},{2,14},{3,15},{4,0},{5,1},{6,2},{7,3},{8,4},{9,5},{1... | collective-permute-start | bytes 786440 | tf_op jit(solution)/shard_map/ppermute | solution.py:415
  51.8 0.6 collective-permute-start.22
  52.5 1.2 %collective-permute-done.19.swapped = f32[32,256]{1,0:T(8,128)S(1)} collective-permute-done((f32[32,256]{1,0:T(8,128)S(1)}, f32[32,256]{1,0:T(8,128)S(1)}, u32[]{:S(2)}, u32[]{:S(2)}) %collective-permute-start.19) | collective-permute-done | bytes 32800 | tf_op jit(solution)/shard_map/ppermute | solution.py:408
  53.7 1.3 %collective-permute-start.18 = (bf16[256,256]{1,0:T(8,128)(2,1)S(1)}, bf16[256,256]{1,0:T(8,128)(2,1)S(1)}, u32[]{:S(2)}, u32[]{:S(2)}) collective-permute-start(bf16[256,256]{1,0:T(8,128)(2,1)S(1)} %collective-permute-done.14), channel_id=1, source_target_pairs={{0,2},{1,3},{2,0},{3,1},{4,6},{5,7},{6,4},{7,5},{8,10},{9,11},{10,... | collective-permute-start | bytes 393224 | tf_op jit(solution)/shard_map/ppermute | solution.py:415
  55.0 1.4 %collective-permute-start.20 = (f32[32,256]{1,0:T(8,128)S(1)}, f32[32,256]{1,0:T(8,128)S(1)}, u32[]{:S(2)}, u32[]{:S(2)}) collective-permute-start(f32[32,256]{1,0:T(8,128)S(1)} %get-tuple-element.71), channel_id=1, source_target_pairs={{96,0},{161,1},{98,2},{163,3},{100,4},{165,5},{102,6},{167,7},{104... | collective-permute-start | bytes 98312 | tf_op jit(solution)/shard_map/ppermute | solution.py:427
  56.4 1.6 %near_grads.1.refs_6_ = f32[512,1024]{1,0:T(8,128)S(1)} custom-call(s32[10]{0:T(128)S(1)} %place.1, bf16[2,256,256]{2,1,0:T(8,128)(2,1)S(1)} %pair.1.mine, bf16[1,256,256]{2,1,0:T(8,128)(2,1)S(1)} %bitcast.5, bf16[2,256,256]{2,1,0:T(8,128)(2,1)S(1)} %collective-permute-done.21.other, bf16[1,256,256]{2,1,0:T(8,128)(2,1)S(1)} %collective-permute-done.22.other_far, ...), custom_call_target="tpu_custom_call" | custom-call | flops 805306368 | bytes 4980776 | tf_op jit(solution)/shard_map/near_grads/pallas_call | solution.py:31
  58.0 2.9 %collective-permute-done.20.recv = f32[32,256]{1,0:T(8,128)S(1)} collective-permute-done((f32[32,256]{1,0:T(8,128)S(1)}, f32[32,256]{1,0:T(8,128)S(1)}, u32[]{:S(2)}, u32[]{:S(2)}) %collective-permute-start.20) | collective-permute-done | bytes 32800 | tf_op jit(solution)/shard_map/ppermute | solution.py:427
  60.9 0.5 collective-permute-start.23
  61.3 0.1 collective-permute-start.24
  61.5 0.4 collective-permute-start.25
  61.9 0.1 collective-permute-start.26
  62.0 1.1 %collective-permute-done.26.refs_1_ = f32[32,256]{1,0:T(8,128)S(1)} collective-permute-done((f32[32,256]{1,0:T(8,128)S(1)}, f32[32,256]{1,0:T(8,128)S(1)}, u32[]{:S(2)}, u32[]{:S(2)}) %collective-permute-start.26) | collective-permute-done | bytes 32800 | tf_op jit(solution)/shard_map/ppermute | solution.py:408
  63.1 2.7 %collective-permute-start.27 = (f32[32,256]{1,0:T(8,128)S(1)}, f32[32,256]{1,0:T(8,128)S(1)}, u32[]{:S(2)}, u32[]{:S(2)}) collective-permute-start(f32[32,256]{1,0:T(8,128)S(1)} %add_up.3.here), channel_id=1, source_target_pairs={{0,16},{16,0},{32,48},{48,32},{64,80},{80,64},{96,112},{112,96},{1... | collective-permute-start | bytes 98312 | tf_op jit(solution)/shard_map/ppermute | solution.py:485
  65.9 3.0 %far_grads.1 = bf16[512,1024]{1,0:T(8,128)(2,1)} custom-call(s32[10]{0:T(128)S(1)} %place.1, bf16[2,256,256]{2,1,0:T(8,128)(2,1)S(1)} %collective-permute-done.16.refs_0_, bf16[2,256,256]{2,1,0:T(8,128)(2,1)S(1)} %collective-permute-done.17.refs_1_, bf16[1,256,256]{2,1,0:T(8,128)(2,1)S(1)} %bitcast.3, ...), custom_call_target="tpu_custom_call" | custom-call | flops 1342177280 | bytes 7602216 | tf_op jit(solution)/shard_map/far_grads/pallas_call | solution.py:31
  68.9 0.7 tenant_totals.1
  (32 shorter events, 0.1 us)
Async XLA Ops:
  0.6 1.6 %copy-start = (bf16[1024,1024]{1,0:T(8,128)(2,1)S(1)}, bf16[1024,1024]{1,0:T(8,128)(2,1)}, u32[]{:S(2)}) copy-start(bf16[1024,1024]{1,0:T(8,128)(2,1)} %key_weight.1) | copy-start | bytes 6291460
  2.2 1.2 %copy-start.3 = (bf16[512,1024]{1,0:T(8,128)(2,1)S(1)}, bf16[512,1024]{1,0:T(8,128)(2,1)}, u32[]{:S(2)}) copy-start(bf16[512,1024]{1,0:T(8,128)(2,1)} %tokens.5) | copy-start | bytes 3145732
  3.4 4.1 %copy-start.2 = (bf16[1024,1024]{1,0:T(8,128)(2,1)S(1)}, bf16[1024,1024]{1,0:T(8,128)(2,1)}, u32[]{:S(2)}) copy-start(bf16[1024,1024]{1,0:T(8,128)(2,1)} %value_weight.1) | copy-start | bytes 6291460
  4.2 4.9 %copy-start.1 = (bf16[1024,1024]{1,0:T(8,128)(2,1)S(1)}, bf16[1024,1024]{1,0:T(8,128)(2,1)}, u32[]{:S(2)}) copy-start(bf16[1024,1024]{1,0:T(8,128)(2,1)} %key_weight.1) | copy-start | bytes 6291460
  4.2 6.5 %collective-permute-start = (f32[256,1024]{1,0:T(8,128)S(1)}, f32[256,1024]{1,0:T(8,128)S(1)}, u32[]{:S(2)}, u32[]{:S(2)}) collective-permute-start(f32[256,1024]{1,0:T(8,128)S(1)} %project_key.1), channel_id=1, source_target_pairs={{0,1},{1,0},{2,3},{3,2},{4,5},{5,4},{6,7},{7,6},{8,9},{9,8},{10,11... | collective-permute-start | bytes 3145736 | tf_op jit(solution)/shard_map/ppermute | solution.py:408
  8.2 2.4 %collective-permute-start.1 = (bf16[256,1024]{1,0:T(8,128)(2,1)S(1)}, bf16[256,1024]{1,0:T(8,128)(2,1)S(1)}, u32[]{:S(2)}, u32[]{:S(2)}) collective-permute-start(bf16[256,1024]{1,0:T(8,128)(2,1)S(1)} %project_value.1), channel_id=1, source_target_pairs={{0,1},{1,0},{2,3},{3,2},{4,5},{5,4},{6,7},{7,6},{8,9},{9,8},{10,11... | collective-permute-start | bytes 1572872 | tf_op jit(solution)/shard_map/ppermute | solution.py:408
  11.2 6.2 %collective-permute-start.4 = (bf16[256,384]{1,0:T(8,128)(2,1)S(1)}, bf16[256,384]{1,0:T(8,128)(2,1)S(1)}, u32[]{:S(2)}, u32[]{:S(2)}) collective-permute-start(bf16[256,384]{1,0:T(8,128)(2,1)S(1)} %get-tuple-element.50), channel_id=1, source_target_pairs={{0,2},{1,3},{2,0},{3,1},{4,6},{5,7},{6,4},{7,5},{8,10},{9,11},{10,... | collective-permute-start | bytes 589832 | tf_op jit(solution)/shard_map/ppermute | solution.py:415
  11.3 7.4 %collective-permute-start.6 = (bf16[256,384]{1,0:T(8,128)(2,1)S(1)}, bf16[256,384]{1,0:T(8,128)(2,1)S(1)}, u32[]{:S(2)}, u32[]{:S(2)}) collective-permute-start(bf16[256,384]{1,0:T(8,128)(2,1)S(1)} %get-tuple-element.52), channel_id=1, source_target_pairs={{0,4},{1,5},{2,6},{3,7},{4,8},{5,9},{6,10},{7,11},{8,12},{9,13},{1... | collective-permute-start | bytes 589832 | tf_op jit(solution)/shard_map/ppermute | solution.py:415
  12.1 6.6 %collective-permute-start.7 = (bf16[256,384]{1,0:T(8,128)(2,1)S(1)}, bf16[256,384]{1,0:T(8,128)(2,1)S(1)}, u32[]{:S(2)}, u32[]{:S(2)}) collective-permute-start(bf16[256,384]{1,0:T(8,128)(2,1)S(1)} %get-tuple-element.53), channel_id=1, source_target_pairs={{0,12},{1,13},{2,14},{3,15},{4,0},{5,1},{6,2},{7,3},{8,4},{9,5},{1... | collective-permute-start | bytes 589832 | tf_op jit(solution)/shard_map/ppermute | solution.py:415
  14.1 8.9 %collective-permute-start.2 = (bf16[256,384]{1,0:T(8,128)(2,1)S(1)}, bf16[256,384]{1,0:T(8,128)(2,1)S(1)}, u32[]{:S(2)}, u32[]{:S(2)}) collective-permute-start(bf16[256,384]{1,0:T(8,128)(2,1)S(1)} %get-tuple-element.47), channel_id=1, source_target_pairs={{0,4},{1,5},{2,6},{3,7},{4,8},{5,9},{6,10},{7,11},{8,12},{9,13},{1... | collective-permute-start | bytes 589832 | tf_op jit(solution)/shard_map/ppermute | solution.py:415
  14.1 8.9 %collective-permute-start.3 = (bf16[256,384]{1,0:T(8,128)(2,1)S(1)}, bf16[256,384]{1,0:T(8,128)(2,1)S(1)}, u32[]{:S(2)}, u32[]{:S(2)}) collective-permute-start(bf16[256,384]{1,0:T(8,128)(2,1)S(1)} %get-tuple-element.48), channel_id=1, source_target_pairs={{0,12},{1,13},{2,14},{3,15},{4,0},{5,1},{6,2},{7,3},{8,4},{9,5},{1... | collective-permute-start | bytes 589832 | tf_op jit(solution)/shard_map/ppermute | solution.py:415
  17.5 9.8 %collective-permute-start.5 = (bf16[256,384]{1,0:T(8,128)(2,1)S(1)}, bf16[256,384]{1,0:T(8,128)(2,1)S(1)}, u32[]{:S(2)}, u32[]{:S(2)}) collective-permute-start(bf16[256,384]{1,0:T(8,128)(2,1)S(1)} %relay.2), channel_id=1, source_target_pairs={{0,8},{1,9},{2,10},{3,11},{4,12},{5,13},{6,14},{7,15},{8,0},{9,1},... | collective-permute-start | bytes 589832 | tf_op jit(solution)/shard_map/ppermute | solution.py:415
  18.8 2.4 %copy-start.8 = (s32[1,512]{1,0:T(1,128)S(1)}, s32[1,512]{1,0:T(1,128)}, u32[]{:S(2)}) copy-start(s32[1,512]{1,0:T(1,128)} %segments.1) | copy-start | bytes 6148
  18.8 2.4 %copy-start.9 = (s32[1,4]{1,0:T(1,128)S(1)}, s32[1,4]{1,0:T(1,128)}, u32[]{:S(2)}) copy-start(s32[1,4]{1,0:T(1,128)} %tenants.1) | copy-start | bytes 52
  18.8 8.4 %copy-start.6 = (f32[32,1024]{1,0:T(8,128)S(1)}, f32[32,1024]{1,0:T(8,128)}, u32[]{:S(2)}) copy-start(f32[32,1024]{1,0:T(8,128)} %key_scale.1) | copy-start | bytes 393220
  18.8 8.4 %copy-start.7 = (f32[32,1024]{1,0:T(8,128)S(1)}, f32[32,1024]{1,0:T(8,128)}, u32[]{:S(2)}) copy-start(f32[32,1024]{1,0:T(8,128)} %value_scale.1) | copy-start | bytes 393220
  18.8 11.8 %copy-start.4 = (bf16[512,1024]{1,0:T(8,128)(2,1)S(1)}, bf16[512,1024]{1,0:T(8,128)(2,1)}, u32[]{:S(2)}) copy-start(bf16[512,1024]{1,0:T(8,128)(2,1)} %queries.1) | copy-start | bytes 3145732
  18.9 11.8 %copy-start.5 = (bf16[512,1024]{1,0:T(8,128)(2,1)S(1)}, bf16[512,1024]{1,0:T(8,128)(2,1)}, u32[]{:S(2)}) copy-start(bf16[512,1024]{1,0:T(8,128)(2,1)} %out_grad.1) | copy-start | bytes 3145732
  18.9 8.4 %collective-permute-start.8 = (bf16[256,384]{1,0:T(8,128)(2,1)S(1)}, bf16[256,384]{1,0:T(8,128)(2,1)S(1)}, u32[]{:S(2)}, u32[]{:S(2)}) collective-permute-start(bf16[256,384]{1,0:T(8,128)(2,1)S(1)} %relay.3), channel_id=1, source_target_pairs={{0,2},{1,3},{2,0},{3,1},{4,6},{5,7},{6,4},{7,5},{8,10},{9,11},{10,... | collective-permute-start | bytes 589832 | tf_op jit(solution)/shard_map/ppermute | solution.py:415
  28.0 2.6 %collective-permute-start.9 = (bf16[256,256]{1,0:T(8,128)(2,1)S(1)}, bf16[256,256]{1,0:T(8,128)(2,1)S(1)}, u32[]{:S(2)}, u32[]{:S(2)}) collective-permute-start(bf16[256,256]{1,0:T(8,128)(2,1)S(1)} %get-tuple-element.60.mine), channel_id=1, source_target_pairs={{0,1},{1,0},{2,3},{3,2},{4,5},{5,4},{6,7},{7,6},{8,9},{9,8},{10,11... | collective-permute-start | bytes 393224 | tf_op jit(solution)/shard_map/ppermute | solution.py:408
  29.6 7.6 %collective-permute-start.11 = (f32[256,256]{1,0:T(8,128)S(1)}, f32[256,256]{1,0:T(8,128)S(1)}, u32[]{:S(2)}, u32[]{:S(2)}) collective-permute-start(f32[256,256]{1,0:T(8,128)S(1)} %get-tuple-element.63.base), channel_id=1, source_target_pairs={{0,1},{1,0},{2,3},{3,2},{4,5},{5,4},{6,7},{7,6},{8,9},{9,8},{10,11... | collective-permute-start | bytes 786440 | tf_op jit(solution)/shard_map/ppermute | solution.py:408
  36.8 1.6 %collective-permute-start.10 = (f32[256,256]{1,0:T(8,128)S(1)}, f32[256,256]{1,0:T(8,128)S(1)}, u32[]{:S(2)}, u32[]{:S(2)}) collective-permute-start(f32[256,256]{1,0:T(8,128)S(1)} %get-tuple-element.62.send), channel_id=1, source_target_pairs={{0,1},{1,0},{2,3},{3,2},{4,5},{5,4},{6,7},{7,6},{8,9},{9,8},{10,11... | collective-permute-start | bytes 786440 | tf_op jit(solution)/shard_map/ppermute | solution.py:408
  38.4 1.2 %collective-permute-start.12 = (f32[32,256]{1,0:T(8,128)S(1)}, f32[32,256]{1,0:T(8,128)S(1)}, u32[]{:S(2)}, u32[]{:S(2)}) collective-permute-start(f32[32,256]{1,0:T(8,128)S(1)} %tenant_table.1.refs_0_), channel_id=1, source_target_pairs={{0,1},{1,0},{2,3},{3,2},{4,5},{5,4},{6,7},{7,6},{8,9},{9,8},{10,11... | collective-permute-start | bytes 98312 | tf_op jit(solution)/shard_map/ppermute | solution.py:408
  39.6 7.3 %collective-permute-start.14 = (bf16[256,256]{1,0:T(8,128)(2,1)S(1)}, bf16[256,256]{1,0:T(8,128)(2,1)S(1)}, u32[]{:S(2)}, u32[]{:S(2)}) collective-permute-start(bf16[256,256]{1,0:T(8,128)(2,1)S(1)} %scale_grads.1.mine), channel_id=1, source_target_pairs={{0,8},{1,9},{2,10},{3,11},{4,12},{5,13},{6,14},{7,15},{8,0},{9,1},... | collective-permute-start | bytes 393224 | tf_op jit(solution)/shard_map/ppermute | solution.py:415
  40.2 6.8 %collective-permute-start.13 = (bf16[256,256]{1,0:T(8,128)(2,1)S(1)}, bf16[256,256]{1,0:T(8,128)(2,1)S(1)}, u32[]{:S(2)}, u32[]{:S(2)}) collective-permute-start(bf16[256,256]{1,0:T(8,128)(2,1)S(1)} %scale_grads.1.mine), channel_id=1, source_target_pairs={{0,2},{1,3},{2,0},{3,1},{4,6},{5,7},{6,4},{7,5},{8,10},{9,11},{10,... | collective-permute-start | bytes 393224 | tf_op jit(solution)/shard_map/ppermute | solution.py:415
  40.9 6.1 %collective-permute-start.15 = (f32[32,256]{1,0:T(8,128)S(1)}, f32[32,256]{1,0:T(8,128)S(1)}, u32[]{:S(2)}, u32[]{:S(2)}) collective-permute-start(f32[32,256]{1,0:T(8,128)S(1)} %add_up.2.here), channel_id=1, source_target_pairs={{224,0},{33,1},{226,2},{35,3},{228,4},{37,5},{230,6},{39,7},{232,8... | collective-permute-start | bytes 98312 | tf_op jit(solution)/shard_map/ppermute | solution.py:427
  47.0 9.4 %collective-permute-start.21 = (bf16[2,256,256]{2,1,0:T(8,128)(2,1)S(1)}, bf16[2,256,256]{2,1,0:T(8,128)(2,1)S(1)}, u32[]{:S(2)}, u32[]{:S(2)}) collective-permute-start(bf16[2,256,256]{2,1,0:T(8,128)(2,1)S(1)} %pair.1.mine), channel_id=1, source_target_pairs={{0,1},{1,0},{2,3},{3,2},{4,5},{5,4},{6,7},{7,6},{8,9},{9,8},{10,11... | collective-permute-start | bytes 786440 | tf_op jit(solution)/shard_map/ppermute | solution.py:408
  49.1 11.7 %collective-permute-start.17 = (bf16[2,256,256]{2,1,0:T(8,128)(2,1)S(1)}, bf16[2,256,256]{2,1,0:T(8,128)(2,1)S(1)}, u32[]{:S(2)}, u32[]{:S(2)}) collective-permute-start(bf16[2,256,256]{2,1,0:T(8,128)(2,1)S(1)} %pair.1.mine), channel_id=1, source_target_pairs={{0,4},{1,5},{2,6},{3,7},{4,8},{5,9},{6,10},{7,11},{8,12},{9,13},{1... | collective-permute-start | bytes 786440 | tf_op jit(solution)/shard_map/ppermute | solution.py:415
  50.9 10.0 %collective-permute-start.16 = (bf16[2,256,256]{2,1,0:T(8,128)(2,1)S(1)}, bf16[2,256,256]{2,1,0:T(8,128)(2,1)S(1)}, u32[]{:S(2)}, u32[]{:S(2)}) collective-permute-start(bf16[2,256,256]{2,1,0:T(8,128)(2,1)S(1)} %pair.1.mine), channel_id=1, source_target_pairs={{0,12},{1,13},{2,14},{3,15},{4,0},{5,1},{6,2},{7,3},{8,4},{9,5},{1... | collective-permute-start | bytes 786440 | tf_op jit(solution)/shard_map/ppermute | solution.py:415
  51.8 3.1 %collective-permute-start.22 = (bf16[1,256,256]{2,1,0:T(8,128)(2,1)S(1)}, bf16[1,256,256]{2,1,0:T(8,128)(2,1)S(1)}, u32[]{:S(2)}, u32[]{:S(2)}) collective-permute-start(bf16[1,256,256]{2,1,0:T(8,128)(2,1)S(1)} %bitcast.4), channel_id=1, source_target_pairs={{0,1},{1,0},{2,3},{3,2},{4,5},{5,4},{6,7},{7,6},{8,9},{9,8},{10,11... | collective-permute-start | bytes 393224 | tf_op jit(solution)/shard_map/ppermute | solution.py:408
  52.5 1.2 %collective-permute-start.19 = (f32[32,256]{1,0:T(8,128)S(1)}, f32[32,256]{1,0:T(8,128)S(1)}, u32[]{:S(2)}, u32[]{:S(2)}) collective-permute-start(f32[32,256]{1,0:T(8,128)S(1)} %collective-permute-done.15.direct), channel_id=1, source_target_pairs={{0,1},{1,0},{2,3},{3,2},{4,5},{5,4},{6,7},{7,6},{8,9},{9,8},{10,11... | collective-permute-start | bytes 98312 | tf_op jit(solution)/shard_map/ppermute | solution.py:408
  53.7 7.2 %collective-permute-start.18 = (bf16[256,256]{1,0:T(8,128)(2,1)S(1)}, bf16[256,256]{1,0:T(8,128)(2,1)S(1)}, u32[]{:S(2)}, u32[]{:S(2)}) collective-permute-start(bf16[256,256]{1,0:T(8,128)(2,1)S(1)} %collective-permute-done.14), channel_id=1, source_target_pairs={{0,2},{1,3},{2,0},{3,1},{4,6},{5,7},{6,4},{7,5},{8,10},{9,11},{10,... | collective-permute-start | bytes 393224 | tf_op jit(solution)/shard_map/ppermute | solution.py:415
  55.0 5.9 %collective-permute-start.20 = (f32[32,256]{1,0:T(8,128)S(1)}, f32[32,256]{1,0:T(8,128)S(1)}, u32[]{:S(2)}, u32[]{:S(2)}) collective-permute-start(f32[32,256]{1,0:T(8,128)S(1)} %get-tuple-element.71), channel_id=1, source_target_pairs={{96,0},{161,1},{98,2},{163,3},{100,4},{165,5},{102,6},{167,7},{104... | collective-permute-start | bytes 98312 | tf_op jit(solution)/shard_map/ppermute | solution.py:427
  60.9 2.3 %collective-permute-start.23 = (bf16[2,256,256]{2,1,0:T(8,128)(2,1)S(1)}, bf16[2,256,256]{2,1,0:T(8,128)(2,1)S(1)}, u32[]{:S(2)}, u32[]{:S(2)}) collective-permute-start(bf16[2,256,256]{2,1,0:T(8,128)(2,1)S(1)} %collective-permute-done.16.refs_0_), channel_id=1, source_target_pairs={{0,1},{1,0},{2,3},{3,2},{4,5},{5,4},{6,7},{7,6},{8,9},{9,8},{10,11... | collective-permute-start | bytes 786440 | tf_op jit(solution)/shard_map/ppermute | solution.py:408
  61.3 1.8 %collective-permute-start.24 = (bf16[2,256,256]{2,1,0:T(8,128)(2,1)S(1)}, bf16[2,256,256]{2,1,0:T(8,128)(2,1)S(1)}, u32[]{:S(2)}, u32[]{:S(2)}) collective-permute-start(bf16[2,256,256]{2,1,0:T(8,128)(2,1)S(1)} %collective-permute-done.17.refs_1_), channel_id=1, source_target_pairs={{0,1},{1,0},{2,3},{3,2},{4,5},{5,4},{6,7},{7,6},{8,9},{9,8},{10,11... | collective-permute-start | bytes 786440 | tf_op jit(solution)/shard_map/ppermute | solution.py:408
  61.5 1.7 %collective-permute-start.25 = (bf16[1,256,256]{2,1,0:T(8,128)(2,1)S(1)}, bf16[1,256,256]{2,1,0:T(8,128)(2,1)S(1)}, u32[]{:S(2)}, u32[]{:S(2)}) collective-permute-start(bf16[1,256,256]{2,1,0:T(8,128)(2,1)S(1)} %bitcast.2), channel_id=1, source_target_pairs={{0,1},{1,0},{2,3},{3,2},{4,5},{5,4},{6,7},{7,6},{8,9},{9,8},{10,11... | collective-permute-start | bytes 393224 | tf_op jit(solution)/shard_map/ppermute | solution.py:408
  61.9 1.3 %collective-permute-start.26 = (f32[32,256]{1,0:T(8,128)S(1)}, f32[32,256]{1,0:T(8,128)S(1)}, u32[]{:S(2)}, u32[]{:S(2)}) collective-permute-start(f32[32,256]{1,0:T(8,128)S(1)} %ring_end.1.refs_0_), channel_id=1, source_target_pairs={{0,1},{1,0},{2,3},{3,2},{4,5},{5,4},{6,7},{7,6},{8,9},{9,8},{10,11... | collective-permute-start | bytes 98312 | tf_op jit(solution)/shard_map/ppermute | solution.py:408
  63.1 5.7 %collective-permute-start.27 = (f32[32,256]{1,0:T(8,128)S(1)}, f32[32,256]{1,0:T(8,128)S(1)}, u32[]{:S(2)}, u32[]{:S(2)}) collective-permute-start(f32[32,256]{1,0:T(8,128)S(1)} %add_up.3.here), channel_id=1, source_target_pairs={{0,16},{16,0},{32,48},{48,32},{64,80},{80,64},{96,112},{112,96},{1... | collective-permute-start | bytes 98312 | tf_op jit(solution)/shard_map/ppermute | solution.py:485

commit v5 on v4

--- a/solution.py
+++ b/solution.py
@@ -208,8 +208,7 @@
         bias = jnp.concatenate([bias, bias], axis=1)
         key_tile = tile[visible, :HEAD]
         value_tile = tile[visible, HEAD:]
-        key_total = jnp.zeros((reach, HEAD), F32)
-        value_total = jnp.zeros((reach, HEAD), F32)
+        probs_parts, score_parts, query_parts, out_parts = [], [], [], []
         for pair in range(heads // 2):
             columns = [slice(h * HEAD, (h + 1) * HEAD) for h in (2 * pair, 2 * pair + 1)]
             query = jnp.concatenate([queries[rows, c] for c in columns], axis=0)
@@ -221,11 +220,16 @@
             probs_low = probs.astype(BF)
             prob_grad = contract_last(value_tile, out)
             delta = jnp.sum(probs_low.astype(F32) * prob_grad, axis=0, keepdims=True)
-            score_grad = (probs * (prob_grad - delta)).astype(BF)
-            value_total += jnp.dot(probs_low, out, preferred_element_type=F32)
-            key_total += jnp.dot(score_grad, query, preferred_element_type=F32)
-        grads[visible, :HEAD] += key_total
-        grads[visible, HEAD:] += value_total
+            score_parts.append((probs * (prob_grad - delta)).astype(BF))
+            probs_parts.append(probs_low)
+            query_parts.append(query)
+            out_parts.append(out)
+        for part, left, right in (
+            (slice(0, HEAD), score_parts, query_parts),
+            (slice(HEAD, 2 * HEAD), probs_parts, out_parts),
+        ):
+            left, right = jnp.concatenate(left, axis=1), jnp.concatenate(right, axis=0)
+            grads[visible, part] += jnp.dot(left, right, preferred_element_type=F32)
     for rows, target in ((other_rows, send), (own_rows, keep)):
         target[:, :HEAD] = grads[rows, :HEAD] * SCALE
         target[:, HEAD:] = grads[rows, HEAD:]

time: 69.7 us -> 68.4 us (0.981)
  Pallas kernels: 19.4 us -> 17.8 us
    pallas_call x18, Pallas kernels: 17.4 us -> 15.8 us  [call(): pl.pallas_call(body, in_specs=[pl.BlockSpec(memory_space=space) for space...]
  transfers between devices with their start and end apart: 28 -> 28, of which waited for: 12 -> 12; matrix products, arithmetic and copies ran while one was open for 0% -> 0% of each run, Pallas kernels for 24% -> 22%
where the time goes in v5:
time: 68.4 us; the launch traced here: 68.2 us
  starting transfers between devices  33.3 us (49%)
  Pallas kernels  17.8 us (26%)
  waiting for transfers between devices  13.4 us (20%)
  local copies, waits for them, and re-layouts  2.86 us (4%)
  between operations  0.88 us (1%)
    pallas_call x18, Pallas kernels, call(): pl.pallas_call(body, in_specs=[pl.BlockSpec(memory_space=space) for space...  15.8 us
    ppermute x12, starting transfers between devices, chip_from(): return lax.ppermute(array, 'tensor', pairs)  13.1 us
    ppermute x13, starting transfers between devices, core_swap(): return lax.ppermute(array, 'tensor', CORE_SWAP)  10.8 us
    ppermute x2, starting transfers between devices, depth_from(): return lax.ppermute(array, ('dp', 'tensor'), pairs)  6.69 us
    ppermute x12, waiting for transfers between devices, chip_from(): return lax.ppermute(array, 'tensor', pairs)  5.58 us
    ppermute x2, waiting for transfers between devices, depth_from(): return lax.ppermute(array, ('dp', 'tensor'), pairs)  3.9 us
    ppermute x13, waiting for transfers between devices, core_swap(): return lax.ppermute(array, 'tensor', CORE_SWAP)  3.89 us
    unnamed x20, local copies, waits for them, and re-layouts  2.86 us
  transfers between devices with their start and end apart: 28, of which 12 were waited for; matrix products, arithmetic and copies ran while one was open for 0% of the time, Pallas kernels for 22%

profile of v5, /device:TPU:1, one launch (start us, length us, event | category | flops | bytes accessed | tf_op | source)
XLA Modules:
  0.0 68.2 jit_solution(2073341956776429524)
XLA Ops:
  0.6 0.0 copy-start
  0.6 1.6 %copy-done = bf16[1024,1024]{1,0:T(8,128)(2,1)S(1)} copy-done((bf16[1024,1024]{1,0:T(8,128)(2,1)S(1)}, bf16[1024,1024]{1,0:T(8,128)(2,1)}, u32[]{:S(2)}) %copy-start) | copy-done | bytes 2097176
  2.2 1.2 %copy-done.3 = bf16[512,1024]{1,0:T(8,128)(2,1)S(1)} copy-done((bf16[512,1024]{1,0:T(8,128)(2,1)S(1)}, bf16[512,1024]{1,0:T(8,128)(2,1)}, u32[]{:S(2)}) %copy-start.3) | copy-done | bytes 1048600
  3.5 0.7 %project_key.1 = f32[256,1024]{1,0:T(8,128)S(1)} custom-call(bf16[512,1024]{1,0:T(8,128)(2,1)S(1)} %copy-done.3, bf16[1024,1024]{1,0:T(8,128)(2,1)S(1)} %copy-done), custom_call_target="tpu_custom_call" | custom-call | flops 536870912 | bytes 3145728 | tf_op jit(solution)/shard_map/project_key/pallas_call | solution.py:31
  4.2 0.0 copy-start.1
  4.2 3.3 %collective-permute-start = (f32[256,1024]{1,0:T(8,128)S(1)}, f32[256,1024]{1,0:T(8,128)S(1)}, u32[]{:S(2)}, u32[]{:S(2)}) collective-permute-start(f32[256,1024]{1,0:T(8,128)S(1)} %project_key.1), channel_id=1, source_target_pairs={{0,1},{1,0},{2,3},{3,2},{4,5},{5,4},{6,7},{7,6},{8,9},{9,8},{10,11... | collective-permute-start | bytes 3145736 | tf_op jit(solution)/shard_map/ppermute | solution.py:412
  7.5 0.7 %project_value.1 = bf16[256,1024]{1,0:T(8,128)(2,1)S(1)} custom-call(bf16[512,1024]{1,0:T(8,128)(2,1)S(1)} %copy-done.3, bf16[1024,1024]{1,0:T(8,128)(2,1)S(1)} %copy-done.2), custom_call_target="tpu_custom_call" | custom-call | flops 536870912 | bytes 3145728 | tf_op jit(solution)/shard_map/project_value/pallas_call | solution.py:31
  8.2 0.9 %collective-permute-start.1 = (bf16[256,1024]{1,0:T(8,128)(2,1)S(1)}, bf16[256,1024]{1,0:T(8,128)(2,1)S(1)}, u32[]{:S(2)}, u32[]{:S(2)}) collective-permute-start(bf16[256,1024]{1,0:T(8,128)(2,1)S(1)} %project_value.1), channel_id=1, source_target_pairs={{0,1},{1,0},{2,3},{3,2},{4,5},{5,4},{6,7},{7,6},{8,9},{9,8},{10,11... | collective-permute-start | bytes 1572872 | tf_op jit(solution)/shard_map/ppermute | solution.py:412
  9.1 1.3 %project_keep.1 = (f32[256,1024]{1,0:T(8,128)S(1)}, f32[256,1024]{1,0:T(8,128)S(1)}) custom-call(bf16[512,1024]{1,0:T(8,128)(2,1)S(1)} %copy-done.3, bf16[1024,1024]{1,0:T(8,128)(2,1)S(1)} %copy-done.1, bf16[1024,1024]{1,0:T(8,128)(2,1)S(1)} %copy-done.2), custom_call_target="tpu_custom_call" | custom-call | flops 1073741824 | bytes 5242880 | tf_op jit(solution)/shard_map/project_keep/pallas_call | solution.py:31
  10.4 0.3 collective-permute-done.1.value_recv
  10.6 0.6 pack.1
  11.2 0.1 collective-permute-start.4
  11.3 0.8 %collective-permute-start.6 = (bf16[256,384]{1,0:T(8,128)(2,1)S(1)}, bf16[256,384]{1,0:T(8,128)(2,1)S(1)}, u32[]{:S(2)}, u32[]{:S(2)}) collective-permute-start(bf16[256,384]{1,0:T(8,128)(2,1)S(1)} %get-tuple-element.52), channel_id=1, source_target_pairs={{0,4},{1,5},{2,6},{3,7},{4,8},{5,9},{6,10},{7,11},{8,12},{9,13},{1... | collective-permute-start | bytes 589832 | tf_op jit(solution)/shard_map/ppermute | solution.py:419
  12.1 2.0 %collective-permute-start.7 = (bf16[256,384]{1,0:T(8,128)(2,1)S(1)}, bf16[256,384]{1,0:T(8,128)(2,1)S(1)}, u32[]{:S(2)}, u32[]{:S(2)}) collective-permute-start(bf16[256,384]{1,0:T(8,128)(2,1)S(1)} %get-tuple-element.53), channel_id=1, source_target_pairs={{0,12},{1,13},{2,14},{3,15},{4,0},{5,1},{6,2},{7,3},{8,4},{9,5},{1... | collective-permute-start | bytes 589832 | tf_op jit(solution)/shard_map/ppermute | solution.py:419
  14.1 2.7 %collective-permute-start.3 = (bf16[256,384]{1,0:T(8,128)(2,1)S(1)}, bf16[256,384]{1,0:T(8,128)(2,1)S(1)}, u32[]{:S(2)}, u32[]{:S(2)}) collective-permute-start(bf16[256,384]{1,0:T(8,128)(2,1)S(1)} %get-tuple-element.48), channel_id=1, source_target_pairs={{0,12},{1,13},{2,14},{3,15},{4,0},{5,1},{6,2},{7,3},{8,4},{9,5},{1... | collective-permute-start | bytes 589832 | tf_op jit(solution)/shard_map/ppermute | solution.py:419
  16.7 0.7 collective-permute-done.4.refs_0_
  17.4 0.1 relay.2
  17.5 1.1 %collective-permute-start.5 = (bf16[256,384]{1,0:T(8,128)(2,1)S(1)}, bf16[256,384]{1,0:T(8,128)(2,1)S(1)}, u32[]{:S(2)}, u32[]{:S(2)}) collective-permute-start(bf16[256,384]{1,0:T(8,128)(2,1)S(1)} %relay.2), channel_id=1, source_target_pairs={{0,8},{1,9},{2,10},{3,11},{4,12},{5,13},{6,14},{7,15},{8,0},{9,1},... | collective-permute-start | bytes 589832 | tf_op jit(solution)/shard_map/ppermute | solution.py:419
  18.6 0.1 collective-permute-done.6.refs_0_
  18.7 0.1 relay.3
  18.8 0.0 copy-start.8
  18.8 0.0 copy-start.9
  18.8 0.0 copy-start.6
  18.8 0.0 copy-start.7
  18.8 0.0 copy-start.4
  18.9 0.0 copy-start.5
  18.9 1.2 %collective-permute-start.8 = (bf16[256,384]{1,0:T(8,128)(2,1)S(1)}, bf16[256,384]{1,0:T(8,128)(2,1)S(1)}, u32[]{:S(2)}, u32[]{:S(2)}) collective-permute-start(bf16[256,384]{1,0:T(8,128)(2,1)S(1)} %relay.3), channel_id=1, source_target_pairs={{0,2},{1,3},{2,0},{3,1},{4,6},{5,7},{6,4},{7,5},{8,10},{9,11},{10,... | collective-permute-start | bytes 589832 | tf_op jit(solution)/shard_map/ppermute | solution.py:419
  20.1 1.1 %order_weights.1.weight.refs_7_ = bf16[1024,2048]{1,0:T(8,128)(2,1)S(1)} custom-call(bf16[1024,1024]{1,0:T(8,128)(2,1)S(1)} %copy-done.1, bf16[1024,1024]{1,0:T(8,128)(2,1)S(1)} %copy-done.2), custom_call_target="tpu_custom_call" | custom-call | bytes 4194304 | tf_op jit(solution)/shard_map/order_weights/pallas_call | solution.py:31
  21.2 1.3 %place.1 = s32[10]{0:T(128)S(1)} custom-call(s32[1,512]{1,0:T(1,128)S(1)} %copy-done.8, s32[1,4]{1,0:T(1,128)S(1)} %copy-done.9), custom_call_target="tpu_custom_call" | custom-call | tf_op jit(solution)/shard_map/place/pallas_call | solution.py:136
  22.5 0.4 collective-permute-done.2.refs_0_
  22.9 0.0 collective-permute-done.3.refs_1_
  22.9 4.3 %collective-permute-done.5.refs_2_ = bf16[256,384]{1,0:T(8,128)(2,1)S(1)} collective-permute-done((bf16[256,384]{1,0:T(8,128)(2,1)S(1)}, bf16[256,384]{1,0:T(8,128)(2,1)S(1)}, u32[]{:S(2)}, u32[]{:S(2)}) %collective-permute-start.5) | collective-permute-done | bytes 196640 | tf_op jit(solution)/shard_map/ppermute | solution.py:419
  27.3 0.7 %finish.1 = (f32[256,256]{1,0:T(8,128)S(1)}, bf16[256,256]{1,0:T(8,128)(2,1)S(1)}) custom-call(s32[10]{0:T(128)S(1)} %place.1, f32[256,256]{1,0:T(8,128)S(1)} %get-tuple-element.55.kept, bf16[256,384]{1,0:T(8,128)(2,1)S(1)} %collective-permute-done.2.refs_0_, bf16[256,384]{1,0:T(8,128)(2,1)S(1)} %collective-permute-done.3.refs_1_, ...), custom_call_target="tpu_custom_call" | custom-call | bytes 1310760 | tf_op jit(solution)/shard_map/finish/pallas_call | solution.py:31
  28.0 1.6 %collective-permute-start.9 = (bf16[256,256]{1,0:T(8,128)(2,1)S(1)}, bf16[256,256]{1,0:T(8,128)(2,1)S(1)}, u32[]{:S(2)}, u32[]{:S(2)}) collective-permute-start(bf16[256,256]{1,0:T(8,128)(2,1)S(1)} %get-tuple-element.60.mine), channel_id=1, source_target_pairs={{0,1},{1,0},{2,3},{3,2},{4,5},{5,4},{6,7},{7,6},{8,9},{9,8},{10,11... | collective-permute-start | bytes 393224 | tf_op jit(solution)/shard_map/ppermute | solution.py:412
  29.6 0.3 collective-permute-start.11
  29.9 0.7 %collective-permute-done.9.other = bf16[256,256]{1,0:T(8,128)(2,1)S(1)} collective-permute-done((bf16[256,256]{1,0:T(8,128)(2,1)S(1)}, bf16[256,256]{1,0:T(8,128)(2,1)S(1)}, u32[]{:S(2)}, u32[]{:S(2)}) %collective-permute-start.9) | collective-permute-done | bytes 131104 | tf_op jit(solution)/shard_map/ppermute | solution.py:412
  30.6 4.6 %attention.1 = (f32[256,256]{1,0:T(8,128)S(1)}, f32[256,256]{1,0:T(8,128)S(1)}) custom-call(s32[10]{0:T(128)S(1)} %place.1, bf16[256,256]{1,0:T(8,128)(2,1)S(1)} %get-tuple-element.60.mine, bf16[256,256]{1,0:T(8,128)(2,1)S(1)} %collective-permute-done.9.other, bf16[512,1024]{1,0:T(8,128)(2,1)S(1)} %copy-done.4, bf16[512,1024]{1,0:T(8,128)(2,1)S(1)} %copy-done.5), custom_call_target="tpu_custom_call" | custom-call | bytes 2359336 | tf_op jit(solution)/shard_map/attention/pallas_call | solution.py:31
  35.2 0.4 collective-permute-start.10
  35.7 0.8 %tenant_table.1.refs_0_ = f32[32,256]{1,0:T(8,128)S(1)} custom-call(s32[10]{0:T(128)S(1)} %place.1, f32[256,256]{1,0:T(8,128)S(1)} %get-tuple-element.61.keep, f32[256,256]{1,0:T(8,128)S(1)} %get-tuple-element.62.send, f32[256,256]{1,0:T(8,128)S(1)} %get-tuple-element.63.base, f32[256,256]{1,0:T(8,128)S(1)} %collective-permute-done.11.base_other), custom_call_target="tpu_custom_call" | custom-call | bytes 1048616 | tf_op jit(solution)/shard_map/tenant_table/pallas_call | solution.py:31
  36.4 0.4 collective-permute-done.10.recv
  36.8 0.4 collective-permute-start.12
  37.2 0.6 scale_grads.1.mine
  37.8 0.2 collective-permute-done.12.refs_1_
  38.0 0.6 collective-permute-start.14
  38.6 0.7 collective-permute-start.13
  39.3 5.1 %collective-permute-start.15 = (f32[32,256]{1,0:T(8,128)S(1)}, f32[32,256]{1,0:T(8,128)S(1)}, u32[]{:S(2)}, u32[]{:S(2)}) collective-permute-start(f32[32,256]{1,0:T(8,128)S(1)} %add_up.2.here), channel_id=1, source_target_pairs={{224,0},{33,1},{226,2},{35,3},{228,4},{37,5},{230,6},{39,7},{232,8... | collective-permute-start | bytes 98312 | tf_op jit(solution)/shard_map/ppermute | solution.py:431
  44.3 1.0 %collective-permute-done.15.direct = f32[32,256]{1,0:T(8,128)S(1)} collective-permute-done((f32[32,256]{1,0:T(8,128)S(1)}, f32[32,256]{1,0:T(8,128)S(1)}, u32[]{:S(2)}, u32[]{:S(2)}) %collective-permute-start.15) | collective-permute-done | bytes 32800 | tf_op jit(solution)/shard_map/ppermute | solution.py:431
  45.4 2.1 %collective-permute-start.21 = (bf16[2,256,256]{2,1,0:T(8,128)(2,1)S(1)}, bf16[2,256,256]{2,1,0:T(8,128)(2,1)S(1)}, u32[]{:S(2)}, u32[]{:S(2)}) collective-permute-start(bf16[2,256,256]{2,1,0:T(8,128)(2,1)S(1)} %pair.1.mine), channel_id=1, source_target_pairs={{0,1},{1,0},{2,3},{3,2},{4,5},{5,4},{6,7},{7,6},{8,9},{9,8},{10,11... | collective-permute-start | bytes 786440 | tf_op jit(solution)/shard_map/ppermute | solution.py:412
  47.5 1.8 %collective-permute-start.17 = (bf16[2,256,256]{2,1,0:T(8,128)(2,1)S(1)}, bf16[2,256,256]{2,1,0:T(8,128)(2,1)S(1)}, u32[]{:S(2)}, u32[]{:S(2)}) collective-permute-start(bf16[2,256,256]{2,1,0:T(8,128)(2,1)S(1)} %pair.1.mine), channel_id=1, source_target_pairs={{0,4},{1,5},{2,6},{3,7},{4,8},{5,9},{6,10},{7,11},{8,12},{9,13},{1... | collective-permute-start | bytes 786440 | tf_op jit(solution)/shard_map/ppermute | solution.py:419
  49.3 0.9 %collective-permute-start.16 = (bf16[2,256,256]{2,1,0:T(8,128)(2,1)S(1)}, bf16[2,256,256]{2,1,0:T(8,128)(2,1)S(1)}, u32[]{:S(2)}, u32[]{:S(2)}) collective-permute-start(bf16[2,256,256]{2,1,0:T(8,128)(2,1)S(1)} %pair.1.mine), channel_id=1, source_target_pairs={{0,12},{1,13},{2,14},{3,15},{4,0},{5,1},{6,2},{7,3},{8,4},{9,5},{1... | collective-permute-start | bytes 786440 | tf_op jit(solution)/shard_map/ppermute | solution.py:419
  50.3 0.6 collective-permute-start.22
  50.9 1.2 %collective-permute-done.19.swapped = f32[32,256]{1,0:T(8,128)S(1)} collective-permute-done((f32[32,256]{1,0:T(8,128)S(1)}, f32[32,256]{1,0:T(8,128)S(1)}, u32[]{:S(2)}, u32[]{:S(2)}) %collective-permute-start.19) | collective-permute-done | bytes 32800 | tf_op jit(solution)/shard_map/ppermute | solution.py:412
  52.1 1.3 %collective-permute-start.18 = (bf16[256,256]{1,0:T(8,128)(2,1)S(1)}, bf16[256,256]{1,0:T(8,128)(2,1)S(1)}, u32[]{:S(2)}, u32[]{:S(2)}) collective-permute-start(bf16[256,256]{1,0:T(8,128)(2,1)S(1)} %collective-permute-done.14), channel_id=1, source_target_pairs={{0,2},{1,3},{2,0},{3,1},{4,6},{5,7},{6,4},{7,5},{8,10},{9,11},{10,... | collective-permute-start | bytes 393224 | tf_op jit(solution)/shard_map/ppermute | solution.py:419
  53.4 1.6 %collective-permute-start.20 = (f32[32,256]{1,0:T(8,128)S(1)}, f32[32,256]{1,0:T(8,128)S(1)}, u32[]{:S(2)}, u32[]{:S(2)}) collective-permute-start(f32[32,256]{1,0:T(8,128)S(1)} %get-tuple-element.71), channel_id=1, source_target_pairs={{96,0},{161,1},{98,2},{163,3},{100,4},{165,5},{102,6},{167,7},{104... | collective-permute-start | bytes 98312 | tf_op jit(solution)/shard_map/ppermute | solution.py:431
  55.0 1.6 %near_grads.1.refs_6_ = f32[512,1024]{1,0:T(8,128)S(1)} custom-call(s32[10]{0:T(128)S(1)} %place.1, bf16[2,256,256]{2,1,0:T(8,128)(2,1)S(1)} %pair.1.mine, bf16[1,256,256]{2,1,0:T(8,128)(2,1)S(1)} %bitcast.5, bf16[2,256,256]{2,1,0:T(8,128)(2,1)S(1)} %collective-permute-done.21.other, bf16[1,256,256]{2,1,0:T(8,128)(2,1)S(1)} %collective-permute-done.22.other_far, ...), custom_call_target="tpu_custom_call" | custom-call | flops 805306368 | bytes 4980776 | tf_op jit(solution)/shard_map/near_grads/pallas_call | solution.py:31
  56.6 2.9 %collective-permute-done.20.recv = f32[32,256]{1,0:T(8,128)S(1)} collective-permute-done((f32[32,256]{1,0:T(8,128)S(1)}, f32[32,256]{1,0:T(8,128)S(1)}, u32[]{:S(2)}, u32[]{:S(2)}) %collective-permute-start.20) | collective-permute-done | bytes 32800 | tf_op jit(solution)/shard_map/ppermute | solution.py:431
  59.5 0.5 collective-permute-start.23
  60.0 0.1 collective-permute-start.24
  60.1 0.4 collective-permute-start.25
  60.5 0.1 collective-permute-start.26
  60.6 1.1 %collective-permute-done.26.refs_1_ = f32[32,256]{1,0:T(8,128)S(1)} collective-permute-done((f32[32,256]{1,0:T(8,128)S(1)}, f32[32,256]{1,0:T(8,128)S(1)}, u32[]{:S(2)}, u32[]{:S(2)}) %collective-permute-start.26) | collective-permute-done | bytes 32800 | tf_op jit(solution)/shard_map/ppermute | solution.py:412
  61.8 2.7 %collective-permute-start.27 = (f32[32,256]{1,0:T(8,128)S(1)}, f32[32,256]{1,0:T(8,128)S(1)}, u32[]{:S(2)}, u32[]{:S(2)}) collective-permute-start(f32[32,256]{1,0:T(8,128)S(1)} %add_up.3.here), channel_id=1, source_target_pairs={{0,16},{16,0},{32,48},{48,32},{64,80},{80,64},{96,112},{112,96},{1... | collective-permute-start | bytes 98312 | tf_op jit(solution)/shard_map/ppermute | solution.py:489
  64.5 3.0 %far_grads.1 = bf16[512,1024]{1,0:T(8,128)(2,1)} custom-call(s32[10]{0:T(128)S(1)} %place.1, bf16[2,256,256]{2,1,0:T(8,128)(2,1)S(1)} %collective-permute-done.16.refs_0_, bf16[2,256,256]{2,1,0:T(8,128)(2,1)S(1)} %collective-permute-done.17.refs_1_, bf16[1,256,256]{2,1,0:T(8,128)(2,1)S(1)} %bitcast.3, ...), custom_call_target="tpu_custom_call" | custom-call | flops 1342177280 | bytes 7602216 | tf_op jit(solution)/shard_map/far_grads/pallas_call | solution.py:31
  67.5 0.7 %tenant_totals.1 = (f32[32,64]{1,0:T(8,128)}, f32[32,64]{1,0:T(8,128)}) custom-call(f32[32,256]{1,0:T(8,128)S(1)} %add_up.3.here, f32[32,256]{1,0:T(8,128)S(1)} %collective-permute-done.27.recv), custom_call_target="tpu_custom_call" | custom-call | tf_op jit(solution)/shard_map/tenant_totals/pallas_call | solution.py:403
  (32 shorter events, 0.1 us)
Async XLA Ops:
  0.6 1.6 %copy-start = (bf16[1024,1024]{1,0:T(8,128)(2,1)S(1)}, bf16[1024,1024]{1,0:T(8,128)(2,1)}, u32[]{:S(2)}) copy-start(bf16[1024,1024]{1,0:T(8,128)(2,1)} %key_weight.1) | copy-start | bytes 6291460
  2.2 1.2 %copy-start.3 = (bf16[512,1024]{1,0:T(8,128)(2,1)S(1)}, bf16[512,1024]{1,0:T(8,128)(2,1)}, u32[]{:S(2)}) copy-start(bf16[512,1024]{1,0:T(8,128)(2,1)} %tokens.5) | copy-start | bytes 3145732
  3.4 4.1 %copy-start.2 = (bf16[1024,1024]{1,0:T(8,128)(2,1)S(1)}, bf16[1024,1024]{1,0:T(8,128)(2,1)}, u32[]{:S(2)}) copy-start(bf16[1024,1024]{1,0:T(8,128)(2,1)} %value_weight.1) | copy-start | bytes 6291460
  4.2 4.9 %copy-start.1 = (bf16[1024,1024]{1,0:T(8,128)(2,1)S(1)}, bf16[1024,1024]{1,0:T(8,128)(2,1)}, u32[]{:S(2)}) copy-start(bf16[1024,1024]{1,0:T(8,128)(2,1)} %key_weight.1) | copy-start | bytes 6291460
  4.2 6.5 %collective-permute-start = (f32[256,1024]{1,0:T(8,128)S(1)}, f32[256,1024]{1,0:T(8,128)S(1)}, u32[]{:S(2)}, u32[]{:S(2)}) collective-permute-start(f32[256,1024]{1,0:T(8,128)S(1)} %project_key.1), channel_id=1, source_target_pairs={{0,1},{1,0},{2,3},{3,2},{4,5},{5,4},{6,7},{7,6},{8,9},{9,8},{10,11... | collective-permute-start | bytes 3145736 | tf_op jit(solution)/shard_map/ppermute | solution.py:412
  8.2 2.4 %collective-permute-start.1 = (bf16[256,1024]{1,0:T(8,128)(2,1)S(1)}, bf16[256,1024]{1,0:T(8,128)(2,1)S(1)}, u32[]{:S(2)}, u32[]{:S(2)}) collective-permute-start(bf16[256,1024]{1,0:T(8,128)(2,1)S(1)} %project_value.1), channel_id=1, source_target_pairs={{0,1},{1,0},{2,3},{3,2},{4,5},{5,4},{6,7},{7,6},{8,9},{9,8},{10,11... | collective-permute-start | bytes 1572872 | tf_op jit(solution)/shard_map/ppermute | solution.py:412
  11.2 6.2 %collective-permute-start.4 = (bf16[256,384]{1,0:T(8,128)(2,1)S(1)}, bf16[256,384]{1,0:T(8,128)(2,1)S(1)}, u32[]{:S(2)}, u32[]{:S(2)}) collective-permute-start(bf16[256,384]{1,0:T(8,128)(2,1)S(1)} %get-tuple-element.50), channel_id=1, source_target_pairs={{0,2},{1,3},{2,0},{3,1},{4,6},{5,7},{6,4},{7,5},{8,10},{9,11},{10,... | collective-permute-start | bytes 589832 | tf_op jit(solution)/shard_map/ppermute | solution.py:419
  11.3 7.4 %collective-permute-start.6 = (bf16[256,384]{1,0:T(8,128)(2,1)S(1)}, bf16[256,384]{1,0:T(8,128)(2,1)S(1)}, u32[]{:S(2)}, u32[]{:S(2)}) collective-permute-start(bf16[256,384]{1,0:T(8,128)(2,1)S(1)} %get-tuple-element.52), channel_id=1, source_target_pairs={{0,4},{1,5},{2,6},{3,7},{4,8},{5,9},{6,10},{7,11},{8,12},{9,13},{1... | collective-permute-start | bytes 589832 | tf_op jit(solution)/shard_map/ppermute | solution.py:419
  12.1 6.6 %collective-permute-start.7 = (bf16[256,384]{1,0:T(8,128)(2,1)S(1)}, bf16[256,384]{1,0:T(8,128)(2,1)S(1)}, u32[]{:S(2)}, u32[]{:S(2)}) collective-permute-start(bf16[256,384]{1,0:T(8,128)(2,1)S(1)} %get-tuple-element.53), channel_id=1, source_target_pairs={{0,12},{1,13},{2,14},{3,15},{4,0},{5,1},{6,2},{7,3},{8,4},{9,5},{1... | collective-permute-start | bytes 589832 | tf_op jit(solution)/shard_map/ppermute | solution.py:419
  14.1 8.9 %collective-permute-start.2 = (bf16[256,384]{1,0:T(8,128)(2,1)S(1)}, bf16[256,384]{1,0:T(8,128)(2,1)S(1)}, u32[]{:S(2)}, u32[]{:S(2)}) collective-permute-start(bf16[256,384]{1,0:T(8,128)(2,1)S(1)} %get-tuple-element.47), channel_id=1, source_target_pairs={{0,4},{1,5},{2,6},{3,7},{4,8},{5,9},{6,10},{7,11},{8,12},{9,13},{1... | collective-permute-start | bytes 589832 | tf_op jit(solution)/shard_map/ppermute | solution.py:419
  14.1 8.9 %collective-permute-start.3 = (bf16[256,384]{1,0:T(8,128)(2,1)S(1)}, bf16[256,384]{1,0:T(8,128)(2,1)S(1)}, u32[]{:S(2)}, u32[]{:S(2)}) collective-permute-start(bf16[256,384]{1,0:T(8,128)(2,1)S(1)} %get-tuple-element.48), channel_id=1, source_target_pairs={{0,12},{1,13},{2,14},{3,15},{4,0},{5,1},{6,2},{7,3},{8,4},{9,5},{1... | collective-permute-start | bytes 589832 | tf_op jit(solution)/shard_map/ppermute | solution.py:419
  17.5 9.8 %collective-permute-start.5 = (bf16[256,384]{1,0:T(8,128)(2,1)S(1)}, bf16[256,384]{1,0:T(8,128)(2,1)S(1)}, u32[]{:S(2)}, u32[]{:S(2)}) collective-permute-start(bf16[256,384]{1,0:T(8,128)(2,1)S(1)} %relay.2), channel_id=1, source_target_pairs={{0,8},{1,9},{2,10},{3,11},{4,12},{5,13},{6,14},{7,15},{8,0},{9,1},... | collective-permute-start | bytes 589832 | tf_op jit(solution)/shard_map/ppermute | solution.py:419
  18.8 2.4 %copy-start.8 = (s32[1,512]{1,0:T(1,128)S(1)}, s32[1,512]{1,0:T(1,128)}, u32[]{:S(2)}) copy-start(s32[1,512]{1,0:T(1,128)} %segments.1) | copy-start | bytes 6148
  18.8 2.4 %copy-start.9 = (s32[1,4]{1,0:T(1,128)S(1)}, s32[1,4]{1,0:T(1,128)}, u32[]{:S(2)}) copy-start(s32[1,4]{1,0:T(1,128)} %tenants.1) | copy-start | bytes 52
  18.8 8.4 %copy-start.6 = (f32[32,1024]{1,0:T(8,128)S(1)}, f32[32,1024]{1,0:T(8,128)}, u32[]{:S(2)}) copy-start(f32[32,1024]{1,0:T(8,128)} %key_scale.1) | copy-start | bytes 393220
  18.8 8.4 %copy-start.7 = (f32[32,1024]{1,0:T(8,128)S(1)}, f32[32,1024]{1,0:T(8,128)}, u32[]{:S(2)}) copy-start(f32[32,1024]{1,0:T(8,128)} %value_scale.1) | copy-start | bytes 393220
  18.8 11.8 %copy-start.4 = (bf16[512,1024]{1,0:T(8,128)(2,1)S(1)}, bf16[512,1024]{1,0:T(8,128)(2,1)}, u32[]{:S(2)}) copy-start(bf16[512,1024]{1,0:T(8,128)(2,1)} %queries.1) | copy-start | bytes 3145732
  18.9 11.8 %copy-start.5 = (bf16[512,1024]{1,0:T(8,128)(2,1)S(1)}, bf16[512,1024]{1,0:T(8,128)(2,1)}, u32[]{:S(2)}) copy-start(bf16[512,1024]{1,0:T(8,128)(2,1)} %out_grad.1) | copy-start | bytes 3145732
  18.9 8.4 %collective-permute-start.8 = (bf16[256,384]{1,0:T(8,128)(2,1)S(1)}, bf16[256,384]{1,0:T(8,128)(2,1)S(1)}, u32[]{:S(2)}, u32[]{:S(2)}) collective-permute-start(bf16[256,384]{1,0:T(8,128)(2,1)S(1)} %relay.3), channel_id=1, source_target_pairs={{0,2},{1,3},{2,0},{3,1},{4,6},{5,7},{6,4},{7,5},{8,10},{9,11},{10,... | collective-permute-start | bytes 589832 | tf_op jit(solution)/shard_map/ppermute | solution.py:419
  28.0 2.6 %collective-permute-start.9 = (bf16[256,256]{1,0:T(8,128)(2,1)S(1)}, bf16[256,256]{1,0:T(8,128)(2,1)S(1)}, u32[]{:S(2)}, u32[]{:S(2)}) collective-permute-start(bf16[256,256]{1,0:T(8,128)(2,1)S(1)} %get-tuple-element.60.mine), channel_id=1, source_target_pairs={{0,1},{1,0},{2,3},{3,2},{4,5},{5,4},{6,7},{7,6},{8,9},{9,8},{10,11... | collective-permute-start | bytes 393224 | tf_op jit(solution)/shard_map/ppermute | solution.py:412
  29.6 6.0 %collective-permute-start.11 = (f32[256,256]{1,0:T(8,128)S(1)}, f32[256,256]{1,0:T(8,128)S(1)}, u32[]{:S(2)}, u32[]{:S(2)}) collective-permute-start(f32[256,256]{1,0:T(8,128)S(1)} %get-tuple-element.63.base), channel_id=1, source_target_pairs={{0,1},{1,0},{2,3},{3,2},{4,5},{5,4},{6,7},{7,6},{8,9},{9,8},{10,11... | collective-permute-start | bytes 786440 | tf_op jit(solution)/shard_map/ppermute | solution.py:412
  35.2 1.6 %collective-permute-start.10 = (f32[256,256]{1,0:T(8,128)S(1)}, f32[256,256]{1,0:T(8,128)S(1)}, u32[]{:S(2)}, u32[]{:S(2)}) collective-permute-start(f32[256,256]{1,0:T(8,128)S(1)} %get-tuple-element.62.send), channel_id=1, source_target_pairs={{0,1},{1,0},{2,3},{3,2},{4,5},{5,4},{6,7},{7,6},{8,9},{9,8},{10,11... | collective-permute-start | bytes 786440 | tf_op jit(solution)/shard_map/ppermute | solution.py:412
  36.8 1.2 %collective-permute-start.12 = (f32[32,256]{1,0:T(8,128)S(1)}, f32[32,256]{1,0:T(8,128)S(1)}, u32[]{:S(2)}, u32[]{:S(2)}) collective-permute-start(f32[32,256]{1,0:T(8,128)S(1)} %tenant_table.1.refs_0_), channel_id=1, source_target_pairs={{0,1},{1,0},{2,3},{3,2},{4,5},{5,4},{6,7},{7,6},{8,9},{9,8},{10,11... | collective-permute-start | bytes 98312 | tf_op jit(solution)/shard_map/ppermute | solution.py:412
  38.0 7.3 %collective-permute-start.14 = (bf16[256,256]{1,0:T(8,128)(2,1)S(1)}, bf16[256,256]{1,0:T(8,128)(2,1)S(1)}, u32[]{:S(2)}, u32[]{:S(2)}) collective-permute-start(bf16[256,256]{1,0:T(8,128)(2,1)S(1)} %scale_grads.1.mine), channel_id=1, source_target_pairs={{0,8},{1,9},{2,10},{3,11},{4,12},{5,13},{6,14},{7,15},{8,0},{9,1},... | collective-permute-start | bytes 393224 | tf_op jit(solution)/shard_map/ppermute | solution.py:419
  38.6 6.8 %collective-permute-start.13 = (bf16[256,256]{1,0:T(8,128)(2,1)S(1)}, bf16[256,256]{1,0:T(8,128)(2,1)S(1)}, u32[]{:S(2)}, u32[]{:S(2)}) collective-permute-start(bf16[256,256]{1,0:T(8,128)(2,1)S(1)} %scale_grads.1.mine), channel_id=1, source_target_pairs={{0,2},{1,3},{2,0},{3,1},{4,6},{5,7},{6,4},{7,5},{8,10},{9,11},{10,... | collective-permute-start | bytes 393224 | tf_op jit(solution)/shard_map/ppermute | solution.py:419
  39.3 6.1 %collective-permute-start.15 = (f32[32,256]{1,0:T(8,128)S(1)}, f32[32,256]{1,0:T(8,128)S(1)}, u32[]{:S(2)}, u32[]{:S(2)}) collective-permute-start(f32[32,256]{1,0:T(8,128)S(1)} %add_up.2.here), channel_id=1, source_target_pairs={{224,0},{33,1},{226,2},{35,3},{228,4},{37,5},{230,6},{39,7},{232,8... | collective-permute-start | bytes 98312 | tf_op jit(solution)/shard_map/ppermute | solution.py:431
  45.4 9.6 %collective-permute-start.21 = (bf16[2,256,256]{2,1,0:T(8,128)(2,1)S(1)}, bf16[2,256,256]{2,1,0:T(8,128)(2,1)S(1)}, u32[]{:S(2)}, u32[]{:S(2)}) collective-permute-start(bf16[2,256,256]{2,1,0:T(8,128)(2,1)S(1)} %pair.1.mine), channel_id=1, source_target_pairs={{0,1},{1,0},{2,3},{3,2},{4,5},{5,4},{6,7},{7,6},{8,9},{9,8},{10,11... | collective-permute-start | bytes 786440 | tf_op jit(solution)/shard_map/ppermute | solution.py:412
  47.5 11.9 %collective-permute-start.17 = (bf16[2,256,256]{2,1,0:T(8,128)(2,1)S(1)}, bf16[2,256,256]{2,1,0:T(8,128)(2,1)S(1)}, u32[]{:S(2)}, u32[]{:S(2)}) collective-permute-start(bf16[2,256,256]{2,1,0:T(8,128)(2,1)S(1)} %pair.1.mine), channel_id=1, source_target_pairs={{0,4},{1,5},{2,6},{3,7},{4,8},{5,9},{6,10},{7,11},{8,12},{9,13},{1... | collective-permute-start | bytes 786440 | tf_op jit(solution)/shard_map/ppermute | solution.py:419
  49.3 10.2 %collective-permute-start.16 = (bf16[2,256,256]{2,1,0:T(8,128)(2,1)S(1)}, bf16[2,256,256]{2,1,0:T(8,128)(2,1)S(1)}, u32[]{:S(2)}, u32[]{:S(2)}) collective-permute-start(bf16[2,256,256]{2,1,0:T(8,128)(2,1)S(1)} %pair.1.mine), channel_id=1, source_target_pairs={{0,12},{1,13},{2,14},{3,15},{4,0},{5,1},{6,2},{7,3},{8,4},{9,5},{1... | collective-permute-start | bytes 786440 | tf_op jit(solution)/shard_map/ppermute | solution.py:419
  50.3 3.1 %collective-permute-start.22 = (bf16[1,256,256]{2,1,0:T(8,128)(2,1)S(1)}, bf16[1,256,256]{2,1,0:T(8,128)(2,1)S(1)}, u32[]{:S(2)}, u32[]{:S(2)}) collective-permute-start(bf16[1,256,256]{2,1,0:T(8,128)(2,1)S(1)} %bitcast.4), channel_id=1, source_target_pairs={{0,1},{1,0},{2,3},{3,2},{4,5},{5,4},{6,7},{7,6},{8,9},{9,8},{10,11... | collective-permute-start | bytes 393224 | tf_op jit(solution)/shard_map/ppermute | solution.py:412
  50.9 1.2 %collective-permute-start.19 = (f32[32,256]{1,0:T(8,128)S(1)}, f32[32,256]{1,0:T(8,128)S(1)}, u32[]{:S(2)}, u32[]{:S(2)}) collective-permute-start(f32[32,256]{1,0:T(8,128)S(1)} %collective-permute-done.15.direct), channel_id=1, source_target_pairs={{0,1},{1,0},{2,3},{3,2},{4,5},{5,4},{6,7},{7,6},{8,9},{9,8},{10,11... | collective-permute-start | bytes 98312 | tf_op jit(solution)/shard_map/ppermute | solution.py:412
  52.1 7.4 %collective-permute-start.18 = (bf16[256,256]{1,0:T(8,128)(2,1)S(1)}, bf16[256,256]{1,0:T(8,128)(2,1)S(1)}, u32[]{:S(2)}, u32[]{:S(2)}) collective-permute-start(bf16[256,256]{1,0:T(8,128)(2,1)S(1)} %collective-permute-done.14), channel_id=1, source_target_pairs={{0,2},{1,3},{2,0},{3,1},{4,6},{5,7},{6,4},{7,5},{8,10},{9,11},{10,... | collective-permute-start | bytes 393224 | tf_op jit(solution)/shard_map/ppermute | solution.py:419
  53.4 6.1 %collective-permute-start.20 = (f32[32,256]{1,0:T(8,128)S(1)}, f32[32,256]{1,0:T(8,128)S(1)}, u32[]{:S(2)}, u32[]{:S(2)}) collective-permute-start(f32[32,256]{1,0:T(8,128)S(1)} %get-tuple-element.71), channel_id=1, source_target_pairs={{96,0},{161,1},{98,2},{163,3},{100,4},{165,5},{102,6},{167,7},{104... | collective-permute-start | bytes 98312 | tf_op jit(solution)/shard_map/ppermute | solution.py:431
  59.5 2.3 %collective-permute-start.23 = (bf16[2,256,256]{2,1,0:T(8,128)(2,1)S(1)}, bf16[2,256,256]{2,1,0:T(8,128)(2,1)S(1)}, u32[]{:S(2)}, u32[]{:S(2)}) collective-permute-start(bf16[2,256,256]{2,1,0:T(8,128)(2,1)S(1)} %collective-permute-done.16.refs_0_), channel_id=1, source_target_pairs={{0,1},{1,0},{2,3},{3,2},{4,5},{5,4},{6,7},{7,6},{8,9},{9,8},{10,11... | collective-permute-start | bytes 786440 | tf_op jit(solution)/shard_map/ppermute | solution.py:412
  60.0 1.8 %collective-permute-start.24 = (bf16[2,256,256]{2,1,0:T(8,128)(2,1)S(1)}, bf16[2,256,256]{2,1,0:T(8,128)(2,1)S(1)}, u32[]{:S(2)}, u32[]{:S(2)}) collective-permute-start(bf16[2,256,256]{2,1,0:T(8,128)(2,1)S(1)} %collective-permute-done.17.refs_1_), channel_id=1, source_target_pairs={{0,1},{1,0},{2,3},{3,2},{4,5},{5,4},{6,7},{7,6},{8,9},{9,8},{10,11... | collective-permute-start | bytes 786440 | tf_op jit(solution)/shard_map/ppermute | solution.py:412
  60.1 1.7 %collective-permute-start.25 = (bf16[1,256,256]{2,1,0:T(8,128)(2,1)S(1)}, bf16[1,256,256]{2,1,0:T(8,128)(2,1)S(1)}, u32[]{:S(2)}, u32[]{:S(2)}) collective-permute-start(bf16[1,256,256]{2,1,0:T(8,128)(2,1)S(1)} %bitcast.2), channel_id=1, source_target_pairs={{0,1},{1,0},{2,3},{3,2},{4,5},{5,4},{6,7},{7,6},{8,9},{9,8},{10,11... | collective-permute-start | bytes 393224 | tf_op jit(solution)/shard_map/ppermute | solution.py:412
  60.5 1.3 %collective-permute-start.26 = (f32[32,256]{1,0:T(8,128)S(1)}, f32[32,256]{1,0:T(8,128)S(1)}, u32[]{:S(2)}, u32[]{:S(2)}) collective-permute-start(f32[32,256]{1,0:T(8,128)S(1)} %ring_end.1.refs_0_), channel_id=1, source_target_pairs={{0,1},{1,0},{2,3},{3,2},{4,5},{5,4},{6,7},{7,6},{8,9},{9,8},{10,11... | collective-permute-start | bytes 98312 | tf_op jit(solution)/shard_map/ppermute | solution.py:412
  61.8 5.7 %collective-permute-start.27 = (f32[32,256]{1,0:T(8,128)S(1)}, f32[32,256]{1,0:T(8,128)S(1)}, u32[]{:S(2)}, u32[]{:S(2)}) collective-permute-start(f32[32,256]{1,0:T(8,128)S(1)} %add_up.3.here), channel_id=1, source_target_pairs={{0,16},{16,0},{32,48},{48,32},{64,80},{80,64},{96,112},{112,96},{1... | collective-permute-start | bytes 98312 | tf_op jit(solution)/shard_map/ppermute | solution.py:489

commit v6 on v5

--- a/solution.py
+++ b/solution.py
@@ -53,6 +53,42 @@
 ORDER = [(0, 0), (0, 1), (2, 0), (1, 0), (1, 1), (3, 0), (3, 1), (2, 1)]
 SENT = [(2, 1), (1, 1), (3, 1), (1, 0), (3, 0)]
 KEPT = [(2, 0), (0, 1), (0, 0)]
+
+
+def load_body(tokens, key_weight, value_weight, send, rows, key_out, value_out, sems):
+    core = lax.rem(lax.axis_index("tensor"), 2)
+    halves = [pl.ds(pl.multiple_of(half * HALF, HALF), HALF) for half in (1 - core, core)]
+    steps = 4
+    width = send.shape[1] // steps
+    chunks = [pl.ds(step * width, width) for step in range(steps)]
+    pairs = [(tokens.at[halves[0], :], rows.at[halves[0], :])]
+    pairs += [(key_weight.at[:, chunk], key_out.at[:, chunk]) for chunk in chunks]
+    pairs += [(tokens.at[halves[1], :], rows.at[halves[1], :]), (value_weight, value_out)]
+    copies = [pltpu.make_async_copy(*pair, sems.at[i]) for i, pair in enumerate(pairs)]
+    for copy in copies:
+        copy.start()
+    copies[0].wait()
+    for chunk, copy in zip(chunks, copies[1:]):
+        copy.wait()
+        send[:, chunk] = jnp.dot(
+            rows[halves[0], :], key_out[:, chunk], preferred_element_type=F32
+        )
+    for copy in copies[steps + 1 :]:
+        copy.wait()
+
+
+def load_project(tokens, key_weight, value_weight):
+    args = [pltpu.with_memory_space_constraint(x, pltpu.HBM) for x in (tokens, key_weight, value_weight)]
+    outs = [((HALF, CHIPS * HEAD), F32)] + [(x.shape, BF) for x in args]
+    return pl.pallas_call(
+        load_body,
+        in_specs=[pl.BlockSpec(memory_space=pltpu.HBM)] * 3,
+        out_specs=[pl.BlockSpec(memory_space=pltpu.VMEM)] * 4,
+        out_shape=[pltpu.VMEM(*out) for out in outs],
+        scratch_shapes=[pltpu.SemaphoreType.DMA((7,))],
+        compiler_params=pltpu.CompilerParams(vmem_limit_bytes=16 * MIB),
+        name="project_key",
+    )(*args)
 
 
 def home_of(chip, across, row):
@@ -316,36 +352,58 @@
     return call("near_grads", near_body, outs, args, scratch, 8, flops)[0]
 
 
-def far_body(place, *refs):
-    count = len(refs) // 2 - 3
-    mine, other = refs[:count], refs[count : 2 * count]
-    near, weight, out, left, totals, sems = refs[2 * count :]
-    place_rows(place, left, mine, other)
-    writes = []
-    steps, width = totals.shape[0], totals.shape[2]
+def far_half(half, pieces, near, weight, columns):
+    chunks = [piece[row] for piece in pieces for row in range(piece.shape[0])]
+    left = jnp.concatenate(chunks, axis=1)
+    rows = pl.ds(pl.multiple_of(half * HALF, HALF), HALF)
+    right = weight[columns, weight.shape[1] - left.shape[1] :]
+    return (near[rows, columns] + contract_last(left, right)).astype(BF)
+
+
+def far_own_body(place, *refs):
+    pieces, (near, weight, out) = refs[:-3], refs[-3:]
+    steps = 4
+    width = out.shape[1] // steps
     for step in range(steps):
         columns = pl.ds(step * width, width)
-        total = contract_last(left[...], weight[columns, weight.shape[1] - left.shape[1] :])
-        totals[step] = (near[:, columns] + total).astype(BF)
-        writes.append(pltpu.make_async_copy(totals.at[step], out.at[:, columns], sems.at[step]))
+        out[:, columns] = far_half(place[0], pieces, near, weight, columns)
+
+
+def far_own(place, pieces, near, weight):
+    outs = [((HALF, weight.shape[0]), BF)]
+    flops = 2 * HALF * weight.shape[0] * 10 * HEAD
+    return call("far_own", far_own_body, outs, [place, *pieces, near, weight], (), 12, flops)[0]
+
+
+def far_body(place, *refs):
+    pieces, (own, near, weight, out, totals, sems) = refs[:-6], refs[-6:]
+    own_rows, other_rows = [
+        pl.ds(pl.multiple_of(half * HALF, HALF), HALF) for half in (place[0], 1 - place[0])
+    ]
+    steps, width = totals.shape[0], totals.shape[2]
+    writes = [pltpu.make_async_copy(own, out.at[own_rows, :], sems.at[steps])]
+    writes[0].start()
+    for step in range(steps):
+        columns = pl.ds(step * width, width)
+        totals[step] = far_half(1 - place[0], pieces, near, weight, columns)
+        target = out.at[other_rows, columns]
+        writes.append(pltpu.make_async_copy(totals.at[step], target, sems.at[step]))
         writes[-1].start()
     for write in writes:
         write.wait()
 
 
-def far_grads(place, mine, other, near, weight):
+def far_grads(place, pieces, own, near, weight):
     features = weight.shape[0]
-    depth = 10 * HEAD
     steps = 4
     scratch = [
-        pltpu.VMEM((TOK, depth), BF),
-        pltpu.VMEM((steps, TOK, features // steps), BF),
-        pltpu.SemaphoreType.DMA((steps,)),
+        pltpu.VMEM((steps, HALF, features // steps), BF),
+        pltpu.SemaphoreType.DMA((steps + 1,)),
     ]
     outs = [((TOK, features), BF)]
-    args = [place, *mine, *other, near, weight]
-    flops = 2 * TOK * features * depth
-    return call("far_grads", far_body, outs, args, scratch, 16, flops, out_space=pltpu.HBM)[0]
+    args = [place, *pieces, own, near, weight]
+    flops = 2 * HALF * features * 10 * HEAD
+    return call("far_grads", far_body, outs, args, scratch, 12, flops, out_space=pltpu.HBM)[0]
 
 
 def add_body(*refs):
@@ -443,7 +501,7 @@
     tenant_ids,
 ):
     place = find_place(segment_ids, tenant_ids)
-    key_send = project("project_key", True, tokens, [key_weight], [F32])[0]
+    key_send, tokens, key_weight, value_weight = load_project(tokens, key_weight, value_weight)
     key_recv = core_swap(key_send)
     value_send = project("project_value", True, tokens, [value_weight], [BF])[0]
     value_recv = core_swap(value_send)
@@ -482,12 +540,13 @@
     arrived, ring, near = lax.optimization_barrier((arrived, depth_from(give, (3, -3)), near))
     arrived = arrived[:2] + [arrived[2][None]]
     sums = ring_end(three, ring)
-    others, sums_other = lax.optimization_barrier(
-        ([core_swap(piece) for piece in arrived], core_swap(sums))
+    own_half = far_own(place, arrived, near, weight)
+    others, sums_other, own_half = lax.optimization_barrier(
+        ([core_swap(piece) for piece in arrived], core_swap(sums), own_half)
     )
     sums = add_up(sums, sums_other)
     row_sums = lax.ppermute(sums, "dp", [(i, i ^ 1) for i in range(16)])
-    input_grad = far_grads(place, arrived, others, near, weight)
+    input_grad = far_grads(place, others, own_half, near, weight)
     input_grad, row_sums = lax.optimization_barrier((input_grad, row_sums))
     key_total, value_total = tenant_totals(sums, row_sums)
     return input_grad, key_total, value_total

time: 68.4 us -> 67.5 us (0.987)
  Pallas kernels: 17.8 us -> 20.7 us
  local copies, waits for them, and re-layouts: 2.86 us -> 0.04 us
  waiting for transfers between devices: 13.4 us -> 12.2 us
    pallas_call x0 -> x1, Pallas kernels: none -> 2.97 us  [load_project(): pl.pallas_call(load_body, in_specs=[pl.BlockSpec(memory_space=pltpu.HBM)]...]
    unnamed x20 -> x12, local copies, waits for them, and re-layouts: 2.86 us -> 0.04 us
    ppermute x12, starting transfers between devices: 13.1 us -> 11.9 us  [chip_from(): return lax.ppermute(array, 'tensor', pairs)]
    ppermute x13, starting transfers between devices: 10.8 us -> 11.5 us  [core_swap(): return lax.ppermute(array, 'tensor', CORE_SWAP)]
  transfers between devices with their start and end apart: 28 -> 28, of which waited for: 12 -> 11; matrix products, arithmetic and copies ran while one was open for 0% -> 0% of each run, Pallas kernels for 22% -> 23%
where the time goes in v6:
time: 67.5 us; the launch traced here: 67.4 us
  starting transfers between devices  33.5 us (50%)
  Pallas kernels  20.7 us (31%)
  waiting for transfers between devices  12.2 us (18%)
  between operations  0.91 us (1%)
    pallas_call x18, Pallas kernels, call(): pl.pallas_call(body, in_specs=[pl.BlockSpec(memory_space=space) for space...  15.8 us
    ppermute x12, starting transfers between devices, chip_from(): return lax.ppermute(array, 'tensor', pairs)  11.9 us
    ppermute x13, starting transfers between devices, core_swap(): return lax.ppermute(array, 'tensor', CORE_SWAP)  11.5 us
    ppermute x2, starting transfers between devices, depth_from(): return lax.ppermute(array, ('dp', 'tensor'), pairs)  7.29 us
    ppermute x12, waiting for transfers between devices, chip_from(): return lax.ppermute(array, 'tensor', pairs)  5.06 us
    ppermute x2, waiting for transfers between devices, depth_from(): return lax.ppermute(array, ('dp', 'tensor'), pairs)  3.65 us
    ppermute x13, waiting for transfers between devices, core_swap(): return lax.ppermute(array, 'tensor', CORE_SWAP)  3.46 us
    pallas_call x1, Pallas kernels, load_project(): pl.pallas_call(load_body, in_specs=[pl.BlockSpec(memory_space=pltpu.HBM)]...  2.97 us
  transfers between devices with their start and end apart: 28, of which 11 were waited for; matrix products, arithmetic and copies ran while one was open for 0% of the time, Pallas kernels for 23%

profile of v6, /device:TPU:1, one launch (start us, length us, event | category | flops | bytes accessed | tf_op | source)
XLA Modules:
  0.0 67.4 jit_solution(5823216423722648535)
XLA Ops:
  0.6 3.0 %project_key.1 = (f32[256,1024]{1,0:T(8,128)S(1)}, bf16[512,1024]{1,0:T(8,128)(2,1)S(1)}, bf16[1024,1024]{1,0:T(8,128)(2,1)S(1)}, bf16[1024,1024]{1,0:T(8,128)(2,1)S(1)}) custom-call(bf16[512,1024]{1,0:T(8,128)(2,1)} %tokens.1, bf16[1024,1024]{1,0:T(8,128)(2,1)} %key_weight.1, bf16[1024,1024]{1,0:T(8,128)(2,1)} %value_weight.1), custom_call_target="tpu_custom_call" | custom-call | tf_op jit(solution)/shard_map/project_key/pallas_call | solution.py:83
  3.6 3.3 %collective-permute-start = (f32[256,1024]{1,0:T(8,128)S(1)}, f32[256,1024]{1,0:T(8,128)S(1)}, u32[]{:S(2)}, u32[]{:S(2)}) collective-permute-start(f32[256,1024]{1,0:T(8,128)S(1)} %get-tuple-element.55), channel_id=1, source_target_pairs={{0,1},{1,0},{2,3},{3,2},{4,5},{5,4},{6,7},{7,6},{8,9},{9,8},{10,11... | collective-permute-start | bytes 3145736 | tf_op jit(solution)/shard_map/ppermute | solution.py:470
  6.9 0.7 %project_value.1 = bf16[256,1024]{1,0:T(8,128)(2,1)S(1)} custom-call(bf16[512,1024]{1,0:T(8,128)(2,1)S(1)} %get-tuple-element.50.tokens, bf16[1024,1024]{1,0:T(8,128)(2,1)S(1)} %get-tuple-element.52.refs_1_.refs_0_.value_weight), custom_call_target="tpu_custom_call" | custom-call | flops 536870912 | bytes 3145728 | tf_op jit(solution)/shard_map/project_value/pallas_call | solution.py:31
  7.7 0.1 collective-permute-start.1
  7.8 1.3 %project_keep.1 = (f32[256,1024]{1,0:T(8,128)S(1)}, f32[256,1024]{1,0:T(8,128)S(1)}) custom-call(bf16[512,1024]{1,0:T(8,128)(2,1)S(1)} %get-tuple-element.50.tokens, bf16[1024,1024]{1,0:T(8,128)(2,1)S(1)} %get-tuple-element.51.refs_0_.key_weight, bf16[1024,1024]{1,0:T(8,128)(2,1)S(1)} %get-tuple-element.52.refs_1_.refs_0_.value_weight), custom_call_target="tpu_custom_call" | custom-call | flops 1073741824 | bytes 5242880 | tf_op jit(solution)/shard_map/project_keep/pallas_call | solution.py:31
  9.0 0.9 %collective-permute-done.1.value_recv = bf16[256,1024]{1,0:T(8,128)(2,1)S(1)} collective-permute-done((bf16[256,1024]{1,0:T(8,128)(2,1)S(1)}, bf16[256,1024]{1,0:T(8,128)(2,1)S(1)}, u32[]{:S(2)}, u32[]{:S(2)}) %collective-permute-start.1) | collective-permute-done | bytes 524320 | tf_op jit(solution)/shard_map/ppermute | solution.py:470
  10.0 0.0 collective-permute-done.key_recv
  10.0 0.6 pack.1
  10.5 0.1 collective-permute-start.6
  10.6 2.7 %collective-permute-start.7 = (bf16[256,384]{1,0:T(8,128)(2,1)S(1)}, bf16[256,384]{1,0:T(8,128)(2,1)S(1)}, u32[]{:S(2)}, u32[]{:S(2)}) collective-permute-start(bf16[256,384]{1,0:T(8,128)(2,1)S(1)} %get-tuple-element.62), channel_id=1, source_target_pairs={{0,12},{1,13},{2,14},{3,15},{4,0},{5,1},{6,2},{7,3},{8,4},{9,5},{1... | collective-permute-start | bytes 589832 | tf_op jit(solution)/shard_map/ppermute | solution.py:477
  13.3 2.7 %collective-permute-start.3 = (bf16[256,384]{1,0:T(8,128)(2,1)S(1)}, bf16[256,384]{1,0:T(8,128)(2,1)S(1)}, u32[]{:S(2)}, u32[]{:S(2)}) collective-permute-start(bf16[256,384]{1,0:T(8,128)(2,1)S(1)} %get-tuple-element.57), channel_id=1, source_target_pairs={{0,12},{1,13},{2,14},{3,15},{4,0},{5,1},{6,2},{7,3},{8,4},{9,5},{1... | collective-permute-start | bytes 589832 | tf_op jit(solution)/shard_map/ppermute | solution.py:477
  16.0 2.0 %collective-permute-done.6.refs_0_ = bf16[256,384]{1,0:T(8,128)(2,1)S(1)} collective-permute-done((bf16[256,384]{1,0:T(8,128)(2,1)S(1)}, bf16[256,384]{1,0:T(8,128)(2,1)S(1)}, u32[]{:S(2)}, u32[]{:S(2)}) %collective-permute-start.6) | collective-permute-done | bytes 196640 | tf_op jit(solution)/shard_map/ppermute | solution.py:477
  17.9 0.0 collective-permute-done.7.refs_1_
  17.9 0.1 relay.3
  18.0 0.1 collective-permute-start.8
  18.1 0.6 collective-permute-done.4.refs_0_
  18.8 0.1 relay.2
  18.8 0.0 copy-start.4
  18.8 0.0 copy-start.5
  18.8 0.0 copy-start.2
  18.9 0.0 copy-start.3
  18.9 0.0 copy-start
  18.9 0.0 copy-start.1
  18.9 1.1 %collective-permute-start.5 = (bf16[256,384]{1,0:T(8,128)(2,1)S(1)}, bf16[256,384]{1,0:T(8,128)(2,1)S(1)}, u32[]{:S(2)}, u32[]{:S(2)}) collective-permute-start(bf16[256,384]{1,0:T(8,128)(2,1)S(1)} %relay.2), channel_id=1, source_target_pairs={{0,8},{1,9},{2,10},{3,11},{4,12},{5,13},{6,14},{7,15},{8,0},{9,1},... | collective-permute-start | bytes 589832 | tf_op jit(solution)/shard_map/ppermute | solution.py:477
  20.0 1.2 %order_weights.1.weight.refs_4_.refs_5_ = bf16[1024,2048]{1,0:T(8,128)(2,1)S(1)} custom-call(bf16[1024,1024]{1,0:T(8,128)(2,1)S(1)} %get-tuple-element.51.refs_0_.key_weight, bf16[1024,1024]{1,0:T(8,128)(2,1)S(1)} %get-tuple-element.52.refs_1_.refs_0_.value_weight), custom_call_target="tpu_custom_call" | custom-call | bytes 4194304 | tf_op jit(solution)/shard_map/order_weights/pallas_call | solution.py:31
  21.3 1.3 %place.1 = s32[10]{0:T(128)S(1)} custom-call(s32[1,512]{1,0:T(1,128)S(1)} %copy-done.4, s32[1,4]{1,0:T(1,128)S(1)} %copy-done.5), custom_call_target="tpu_custom_call" | custom-call | tf_op jit(solution)/shard_map/place/pallas_call | solution.py:172
  22.5 0.0 collective-permute-done.3.refs_1_
  22.6 0.4 collective-permute-done.8.refs_3_
  22.9 2.1 %collective-permute-done.5.refs_2_ = bf16[256,384]{1,0:T(8,128)(2,1)S(1)} collective-permute-done((bf16[256,384]{1,0:T(8,128)(2,1)S(1)}, bf16[256,384]{1,0:T(8,128)(2,1)S(1)}, u32[]{:S(2)}, u32[]{:S(2)}) %collective-permute-start.5) | collective-permute-done | bytes 196640 | tf_op jit(solution)/shard_map/ppermute | solution.py:477
  25.0 0.7 %finish.1 = (f32[256,256]{1,0:T(8,128)S(1)}, bf16[256,256]{1,0:T(8,128)(2,1)S(1)}) custom-call(s32[10]{0:T(128)S(1)} %place.1, f32[256,256]{1,0:T(8,128)S(1)} %get-tuple-element.64.kept, bf16[256,384]{1,0:T(8,128)(2,1)S(1)} %collective-permute-done.2.refs_0_, bf16[256,384]{1,0:T(8,128)(2,1)S(1)} %collective-permute-done.3.refs_1_, ...), custom_call_target="tpu_custom_call" | custom-call | bytes 1310760 | tf_op jit(solution)/shard_map/finish/pallas_call | solution.py:31
  25.8 3.1 %collective-permute-start.9 = (bf16[256,256]{1,0:T(8,128)(2,1)S(1)}, bf16[256,256]{1,0:T(8,128)(2,1)S(1)}, u32[]{:S(2)}, u32[]{:S(2)}) collective-permute-start(bf16[256,256]{1,0:T(8,128)(2,1)S(1)} %get-tuple-element.69.mine), channel_id=1, source_target_pairs={{0,1},{1,0},{2,3},{3,2},{4,5},{5,4},{6,7},{7,6},{8,9},{9,8},{10,11... | collective-permute-start | bytes 393224 | tf_op jit(solution)/shard_map/ppermute | solution.py:470
  28.8 0.3 collective-permute-start.11
  29.1 0.7 %collective-permute-done.9.other = bf16[256,256]{1,0:T(8,128)(2,1)S(1)} collective-permute-done((bf16[256,256]{1,0:T(8,128)(2,1)S(1)}, bf16[256,256]{1,0:T(8,128)(2,1)S(1)}, u32[]{:S(2)}, u32[]{:S(2)}) %collective-permute-start.9) | collective-permute-done | bytes 131104 | tf_op jit(solution)/shard_map/ppermute | solution.py:470
  29.8 4.6 %attention.1 = (f32[256,256]{1,0:T(8,128)S(1)}, f32[256,256]{1,0:T(8,128)S(1)}) custom-call(s32[10]{0:T(128)S(1)} %place.1, bf16[256,256]{1,0:T(8,128)(2,1)S(1)} %get-tuple-element.69.mine, bf16[256,256]{1,0:T(8,128)(2,1)S(1)} %collective-permute-done.9.other, bf16[512,1024]{1,0:T(8,128)(2,1)S(1)} %copy-done, bf16[512,1024]{1,0:T(8,128)(2,1)S(1)} %copy-done.1), custom_call_target="tpu_custom_call" | custom-call | bytes 2359336 | tf_op jit(solution)/shard_map/attention/pallas_call | solution.py:31
  34.4 0.4 collective-permute-start.10
  34.9 0.0 collective-permute-done.11.base_other
  34.9 0.8 %tenant_table.1.refs_0_ = f32[32,256]{1,0:T(8,128)S(1)} custom-call(s32[10]{0:T(128)S(1)} %place.1, f32[256,256]{1,0:T(8,128)S(1)} %get-tuple-element.70.keep, f32[256,256]{1,0:T(8,128)S(1)} %get-tuple-element.71.send, f32[256,256]{1,0:T(8,128)S(1)} %get-tuple-element.72.base, f32[256,256]{1,0:T(8,128)S(1)} %collective-permute-done.11.base_other), custom_call_target="tpu_custom_call" | custom-call | bytes 1048616 | tf_op jit(solution)/shard_map/tenant_table/pallas_call | solution.py:31
  35.7 0.4 collective-permute-done.10.recv
  36.0 0.4 collective-permute-start.12
  36.4 0.6 scale_grads.1.mine
  37.1 0.2 collective-permute-done.12.refs_1_
  37.3 1.3 %collective-permute-start.13 = (bf16[256,256]{1,0:T(8,128)(2,1)S(1)}, bf16[256,256]{1,0:T(8,128)(2,1)S(1)}, u32[]{:S(2)}, u32[]{:S(2)}) collective-permute-start(bf16[256,256]{1,0:T(8,128)(2,1)S(1)} %scale_grads.1.mine), channel_id=1, source_target_pairs={{0,2},{1,3},{2,0},{3,1},{4,6},{5,7},{6,4},{7,5},{8,10},{9,11},{10,... | collective-permute-start | bytes 393224 | tf_op jit(solution)/shard_map/ppermute | solution.py:477
  38.5 1.2 %collective-permute-start.14 = (bf16[256,256]{1,0:T(8,128)(2,1)S(1)}, bf16[256,256]{1,0:T(8,128)(2,1)S(1)}, u32[]{:S(2)}, u32[]{:S(2)}) collective-permute-start(bf16[256,256]{1,0:T(8,128)(2,1)S(1)} %scale_grads.1.mine), channel_id=1, source_target_pairs={{0,8},{1,9},{2,10},{3,11},{4,12},{5,13},{6,14},{7,15},{8,0},{9,1},... | collective-permute-start | bytes 393224 | tf_op jit(solution)/shard_map/ppermute | solution.py:477
  39.7 5.4 %collective-permute-start.15 = (f32[32,256]{1,0:T(8,128)S(1)}, f32[32,256]{1,0:T(8,128)S(1)}, u32[]{:S(2)}, u32[]{:S(2)}) collective-permute-start(f32[32,256]{1,0:T(8,128)S(1)} %add_up.2.here), channel_id=1, source_target_pairs={{224,0},{33,1},{226,2},{35,3},{228,4},{37,5},{230,6},{39,7},{232,8... | collective-permute-start | bytes 98312 | tf_op jit(solution)/shard_map/ppermute | solution.py:489
  45.1 1.0 %collective-permute-done.15.direct = f32[32,256]{1,0:T(8,128)S(1)} collective-permute-done((f32[32,256]{1,0:T(8,128)S(1)}, f32[32,256]{1,0:T(8,128)S(1)}, u32[]{:S(2)}, u32[]{:S(2)}) %collective-permute-start.15) | collective-permute-done | bytes 32800 | tf_op jit(solution)/shard_map/ppermute | solution.py:489
  46.2 2.1 %collective-permute-start.21 = (bf16[2,256,256]{2,1,0:T(8,128)(2,1)S(1)}, bf16[2,256,256]{2,1,0:T(8,128)(2,1)S(1)}, u32[]{:S(2)}, u32[]{:S(2)}) collective-permute-start(bf16[2,256,256]{2,1,0:T(8,128)(2,1)S(1)} %pair.1.mine), channel_id=1, source_target_pairs={{0,1},{1,0},{2,3},{3,2},{4,5},{5,4},{6,7},{7,6},{8,9},{9,8},{10,11... | collective-permute-start | bytes 786440 | tf_op jit(solution)/shard_map/ppermute | solution.py:470
  48.3 1.2 %collective-permute-start.16 = (bf16[2,256,256]{2,1,0:T(8,128)(2,1)S(1)}, bf16[2,256,256]{2,1,0:T(8,128)(2,1)S(1)}, u32[]{:S(2)}, u32[]{:S(2)}) collective-permute-start(bf16[2,256,256]{2,1,0:T(8,128)(2,1)S(1)} %pair.1.mine), channel_id=1, source_target_pairs={{0,12},{1,13},{2,14},{3,15},{4,0},{5,1},{6,2},{7,3},{8,4},{9,5},{1... | collective-permute-start | bytes 786440 | tf_op jit(solution)/shard_map/ppermute | solution.py:477
  49.5 0.3 collective-permute-start.17
  49.8 0.6 collective-permute-start.22
  50.5 0.0 collective-permute-start.19
  50.5 1.2 %collective-permute-done.19.swapped = f32[32,256]{1,0:T(8,128)S(1)} collective-permute-done((f32[32,256]{1,0:T(8,128)S(1)}, f32[32,256]{1,0:T(8,128)S(1)}, u32[]{:S(2)}, u32[]{:S(2)}) %collective-permute-start.19) | collective-permute-done | bytes 32800 | tf_op jit(solution)/shard_map/ppermute | solution.py:470
  51.7 1.3 %collective-permute-start.18 = (bf16[256,256]{1,0:T(8,128)(2,1)S(1)}, bf16[256,256]{1,0:T(8,128)(2,1)S(1)}, u32[]{:S(2)}, u32[]{:S(2)}) collective-permute-start(bf16[256,256]{1,0:T(8,128)(2,1)S(1)} %collective-permute-done.14), channel_id=1, source_target_pairs={{0,2},{1,3},{2,0},{3,1},{4,6},{5,7},{6,4},{7,5},{8,10},{9,11},{10,... | collective-permute-start | bytes 393224 | tf_op jit(solution)/shard_map/ppermute | solution.py:477
  53.0 0.0 collective-permute-done.22.other_far
  53.0 1.9 %collective-permute-start.20 = (f32[32,256]{1,0:T(8,128)S(1)}, f32[32,256]{1,0:T(8,128)S(1)}, u32[]{:S(2)}, u32[]{:S(2)}) collective-permute-start(f32[32,256]{1,0:T(8,128)S(1)} %get-tuple-element.80), channel_id=1, source_target_pairs={{96,0},{161,1},{98,2},{163,3},{100,4},{165,5},{102,6},{167,7},{104... | collective-permute-start | bytes 98312 | tf_op jit(solution)/shard_map/ppermute | solution.py:489
  54.9 1.6 %near_grads.1.refs_3_.refs_4_ = f32[512,1024]{1,0:T(8,128)S(1)} custom-call(s32[10]{0:T(128)S(1)} %place.1, bf16[2,256,256]{2,1,0:T(8,128)(2,1)S(1)} %pair.1.mine, bf16[1,256,256]{2,1,0:T(8,128)(2,1)S(1)} %bitcast.3, bf16[2,256,256]{2,1,0:T(8,128)(2,1)S(1)} %collective-permute-done.21.other, bf16[1,256,256]{2,1,0:T(8,128)(2,1)S(1)} %collective-permute-done.22.other_far, ...), custom_call_target="tpu_custom_call" | custom-call | flops 805306368 | bytes 4980776 | tf_op jit(solution)/shard_map/near_grads/pallas_call | solution.py:31
  56.4 2.6 %collective-permute-done.20.recv = f32[32,256]{1,0:T(8,128)S(1)} collective-permute-done((f32[32,256]{1,0:T(8,128)S(1)}, f32[32,256]{1,0:T(8,128)S(1)}, u32[]{:S(2)}, u32[]{:S(2)}) %collective-permute-start.20) | collective-permute-done | bytes 32800 | tf_op jit(solution)/shard_map/ppermute | solution.py:489
  59.1 0.5 collective-permute-start.23
  59.6 0.1 collective-permute-start.24
  59.7 0.4 collective-permute-start.25
  60.1 0.1 collective-permute-start.26
  60.2 1.4 %far_own.1.refs_3_ = bf16[256,1024]{1,0:T(8,128)(2,1)S(1)} custom-call(s32[10]{0:T(128)S(1)} %place.1, bf16[2,256,256]{2,1,0:T(8,128)(2,1)S(1)} %collective-permute-done.16.refs_0_, bf16[2,256,256]{2,1,0:T(8,128)(2,1)S(1)} %collective-permute-done.17.refs_1_, bf16[1,256,256]{2,1,0:T(8,128)(2,1)S(1)} %bitcast.5, f32[512,1024]{1,0:T(8,128)S(1)} %near_grads.1.refs_3_.refs_4_, ...), custom_call_target="tpu_custom_call" | custom-call | flops 671088640 | bytes 6946856 | tf_op jit(solution)/shard_map/far_own/pallas_call | solution.py:31
  61.7 2.8 %collective-permute-start.27 = (f32[32,256]{1,0:T(8,128)S(1)}, f32[32,256]{1,0:T(8,128)S(1)}, u32[]{:S(2)}, u32[]{:S(2)}) collective-permute-start(f32[32,256]{1,0:T(8,128)S(1)} %add_up.3.here), channel_id=1, source_target_pairs={{0,16},{16,0},{32,48},{48,32},{64,80},{80,64},{96,112},{112,96},{1... | collective-permute-start | bytes 98312 | tf_op jit(solution)/shard_map/ppermute | solution.py:548
  64.5 2.2 %far_grads.1 = bf16[512,1024]{1,0:T(8,128)(2,1)} custom-call(s32[10]{0:T(128)S(1)} %place.1, bf16[2,256,256]{2,1,0:T(8,128)(2,1)S(1)} %collective-permute-done.23.refs_0_, bf16[2,256,256]{2,1,0:T(8,128)(2,1)S(1)} %collective-permute-done.24.refs_1_, bf16[1,256,256]{2,1,0:T(8,128)(2,1)S(1)} %collective-permute-done.25.refs_2_, ...), custom_call_target="tpu_custom_call" | custom-call | flops 671088640 | bytes 7471144 | tf_op jit(solution)/shard_map/far_grads/pallas_call | solution.py:31
  66.7 0.7 %tenant_totals.1 = (f32[32,64]{1,0:T(8,128)}, f32[32,64]{1,0:T(8,128)}) custom-call(f32[32,256]{1,0:T(8,128)S(1)} %add_up.3.here, f32[32,256]{1,0:T(8,128)S(1)} %collective-permute-done.27.recv), custom_call_target="tpu_custom_call" | custom-call | tf_op jit(solution)/shard_map/tenant_totals/pallas_call | solution.py:461
  (25 shorter events, 0.1 us)
Async XLA Ops:
  3.6 6.4 %collective-permute-start = (f32[256,1024]{1,0:T(8,128)S(1)}, f32[256,1024]{1,0:T(8,128)S(1)}, u32[]{:S(2)}, u32[]{:S(2)}) collective-permute-start(f32[256,1024]{1,0:T(8,128)S(1)} %get-tuple-element.55), channel_id=1, source_target_pairs={{0,1},{1,0},{2,3},{3,2},{4,5},{5,4},{6,7},{7,6},{8,9},{9,8},{10,11... | collective-permute-start | bytes 3145736 | tf_op jit(solution)/shard_map/ppermute | solution.py:470
  7.7 2.3 %collective-permute-start.1 = (bf16[256,1024]{1,0:T(8,128)(2,1)S(1)}, bf16[256,1024]{1,0:T(8,128)(2,1)S(1)}, u32[]{:S(2)}, u32[]{:S(2)}) collective-permute-start(bf16[256,1024]{1,0:T(8,128)(2,1)S(1)} %project_value.1), channel_id=1, source_target_pairs={{0,1},{1,0},{2,3},{3,2},{4,5},{5,4},{6,7},{7,6},{8,9},{9,8},{10,11... | collective-permute-start | bytes 1572872 | tf_op jit(solution)/shard_map/ppermute | solution.py:470
  10.5 7.4 %collective-permute-start.6 = (bf16[256,384]{1,0:T(8,128)(2,1)S(1)}, bf16[256,384]{1,0:T(8,128)(2,1)S(1)}, u32[]{:S(2)}, u32[]{:S(2)}) collective-permute-start(bf16[256,384]{1,0:T(8,128)(2,1)S(1)} %get-tuple-element.61), channel_id=1, source_target_pairs={{0,4},{1,5},{2,6},{3,7},{4,8},{5,9},{6,10},{7,11},{8,12},{9,13},{1... | collective-permute-start | bytes 589832 | tf_op jit(solution)/shard_map/ppermute | solution.py:477
  10.6 7.3 %collective-permute-start.7 = (bf16[256,384]{1,0:T(8,128)(2,1)S(1)}, bf16[256,384]{1,0:T(8,128)(2,1)S(1)}, u32[]{:S(2)}, u32[]{:S(2)}) collective-permute-start(bf16[256,384]{1,0:T(8,128)(2,1)S(1)} %get-tuple-element.62), channel_id=1, source_target_pairs={{0,12},{1,13},{2,14},{3,15},{4,0},{5,1},{6,2},{7,3},{8,4},{9,5},{1... | collective-permute-start | bytes 589832 | tf_op jit(solution)/shard_map/ppermute | solution.py:477
  13.3 5.5 %collective-permute-start.4 = (bf16[256,384]{1,0:T(8,128)(2,1)S(1)}, bf16[256,384]{1,0:T(8,128)(2,1)S(1)}, u32[]{:S(2)}, u32[]{:S(2)}) collective-permute-start(bf16[256,384]{1,0:T(8,128)(2,1)S(1)} %get-tuple-element.59), channel_id=1, source_target_pairs={{0,2},{1,3},{2,0},{3,1},{4,6},{5,7},{6,4},{7,5},{8,10},{9,11},{10,... | collective-permute-start | bytes 589832 | tf_op jit(solution)/shard_map/ppermute | solution.py:477
  13.3 9.2 %collective-permute-start.2 = (bf16[256,384]{1,0:T(8,128)(2,1)S(1)}, bf16[256,384]{1,0:T(8,128)(2,1)S(1)}, u32[]{:S(2)}, u32[]{:S(2)}) collective-permute-start(bf16[256,384]{1,0:T(8,128)(2,1)S(1)} %get-tuple-element.56), channel_id=1, source_target_pairs={{0,4},{1,5},{2,6},{3,7},{4,8},{5,9},{6,10},{7,11},{8,12},{9,13},{1... | collective-permute-start | bytes 589832 | tf_op jit(solution)/shard_map/ppermute | solution.py:477
  13.3 9.2 %collective-permute-start.3 = (bf16[256,384]{1,0:T(8,128)(2,1)S(1)}, bf16[256,384]{1,0:T(8,128)(2,1)S(1)}, u32[]{:S(2)}, u32[]{:S(2)}) collective-permute-start(bf16[256,384]{1,0:T(8,128)(2,1)S(1)} %get-tuple-element.57), channel_id=1, source_target_pairs={{0,12},{1,13},{2,14},{3,15},{4,0},{5,1},{6,2},{7,3},{8,4},{9,5},{1... | collective-permute-start | bytes 589832 | tf_op jit(solution)/shard_map/ppermute | solution.py:477
  18.0 4.9 %collective-permute-start.8 = (bf16[256,384]{1,0:T(8,128)(2,1)S(1)}, bf16[256,384]{1,0:T(8,128)(2,1)S(1)}, u32[]{:S(2)}, u32[]{:S(2)}) collective-permute-start(bf16[256,384]{1,0:T(8,128)(2,1)S(1)} %relay.3), channel_id=1, source_target_pairs={{0,2},{1,3},{2,0},{3,1},{4,6},{5,7},{6,4},{7,5},{8,10},{9,11},{10,... | collective-permute-start | bytes 589832 | tf_op jit(solution)/shard_map/ppermute | solution.py:477
  18.8 2.4 %copy-start.4 = (s32[1,512]{1,0:T(1,128)S(1)}, s32[1,512]{1,0:T(1,128)}, u32[]{:S(2)}) copy-start(s32[1,512]{1,0:T(1,128)} %segments.1) | copy-start | bytes 6148
  18.8 2.4 %copy-start.5 = (s32[1,4]{1,0:T(1,128)S(1)}, s32[1,4]{1,0:T(1,128)}, u32[]{:S(2)}) copy-start(s32[1,4]{1,0:T(1,128)} %tenants.1) | copy-start | bytes 52
  18.8 6.2 %copy-start.2 = (f32[32,1024]{1,0:T(8,128)S(1)}, f32[32,1024]{1,0:T(8,128)}, u32[]{:S(2)}) copy-start(f32[32,1024]{1,0:T(8,128)} %key_scale.1) | copy-start | bytes 393220
  18.9 6.2 %copy-start.3 = (f32[32,1024]{1,0:T(8,128)S(1)}, f32[32,1024]{1,0:T(8,128)}, u32[]{:S(2)}) copy-start(f32[32,1024]{1,0:T(8,128)} %value_scale.1) | copy-start | bytes 393220
  18.9 11.0 %copy-start = (bf16[512,1024]{1,0:T(8,128)(2,1)S(1)}, bf16[512,1024]{1,0:T(8,128)(2,1)}, u32[]{:S(2)}) copy-start(bf16[512,1024]{1,0:T(8,128)(2,1)} %queries.1) | copy-start | bytes 3145732
  18.9 11.0 %copy-start.1 = (bf16[512,1024]{1,0:T(8,128)(2,1)S(1)}, bf16[512,1024]{1,0:T(8,128)(2,1)}, u32[]{:S(2)}) copy-start(bf16[512,1024]{1,0:T(8,128)(2,1)} %out_grad.1) | copy-start | bytes 3145732
  18.9 6.1 %collective-permute-start.5 = (bf16[256,384]{1,0:T(8,128)(2,1)S(1)}, bf16[256,384]{1,0:T(8,128)(2,1)S(1)}, u32[]{:S(2)}, u32[]{:S(2)}) collective-permute-start(bf16[256,384]{1,0:T(8,128)(2,1)S(1)} %relay.2), channel_id=1, source_target_pairs={{0,8},{1,9},{2,10},{3,11},{4,12},{5,13},{6,14},{7,15},{8,0},{9,1},... | collective-permute-start | bytes 589832 | tf_op jit(solution)/shard_map/ppermute | solution.py:477
  25.8 4.1 %collective-permute-start.9 = (bf16[256,256]{1,0:T(8,128)(2,1)S(1)}, bf16[256,256]{1,0:T(8,128)(2,1)S(1)}, u32[]{:S(2)}, u32[]{:S(2)}) collective-permute-start(bf16[256,256]{1,0:T(8,128)(2,1)S(1)} %get-tuple-element.69.mine), channel_id=1, source_target_pairs={{0,1},{1,0},{2,3},{3,2},{4,5},{5,4},{6,7},{7,6},{8,9},{9,8},{10,11... | collective-permute-start | bytes 393224 | tf_op jit(solution)/shard_map/ppermute | solution.py:470
  28.8 6.0 %collective-permute-start.11 = (f32[256,256]{1,0:T(8,128)S(1)}, f32[256,256]{1,0:T(8,128)S(1)}, u32[]{:S(2)}, u32[]{:S(2)}) collective-permute-start(f32[256,256]{1,0:T(8,128)S(1)} %get-tuple-element.72.base), channel_id=1, source_target_pairs={{0,1},{1,0},{2,3},{3,2},{4,5},{5,4},{6,7},{7,6},{8,9},{9,8},{10,11... | collective-permute-start | bytes 786440 | tf_op jit(solution)/shard_map/ppermute | solution.py:470
  34.4 1.6 %collective-permute-start.10 = (f32[256,256]{1,0:T(8,128)S(1)}, f32[256,256]{1,0:T(8,128)S(1)}, u32[]{:S(2)}, u32[]{:S(2)}) collective-permute-start(f32[256,256]{1,0:T(8,128)S(1)} %get-tuple-element.71.send), channel_id=1, source_target_pairs={{0,1},{1,0},{2,3},{3,2},{4,5},{5,4},{6,7},{7,6},{8,9},{9,8},{10,11... | collective-permute-start | bytes 786440 | tf_op jit(solution)/shard_map/ppermute | solution.py:470
  36.0 1.2 %collective-permute-start.12 = (f32[32,256]{1,0:T(8,128)S(1)}, f32[32,256]{1,0:T(8,128)S(1)}, u32[]{:S(2)}, u32[]{:S(2)}) collective-permute-start(f32[32,256]{1,0:T(8,128)S(1)} %tenant_table.1.refs_0_), channel_id=1, source_target_pairs={{0,1},{1,0},{2,3},{3,2},{4,5},{5,4},{6,7},{7,6},{8,9},{9,8},{10,11... | collective-permute-start | bytes 98312 | tf_op jit(solution)/shard_map/ppermute | solution.py:470
  37.3 8.9 %collective-permute-start.13 = (bf16[256,256]{1,0:T(8,128)(2,1)S(1)}, bf16[256,256]{1,0:T(8,128)(2,1)S(1)}, u32[]{:S(2)}, u32[]{:S(2)}) collective-permute-start(bf16[256,256]{1,0:T(8,128)(2,1)S(1)} %scale_grads.1.mine), channel_id=1, source_target_pairs={{0,2},{1,3},{2,0},{3,1},{4,6},{5,7},{6,4},{7,5},{8,10},{9,11},{10,... | collective-permute-start | bytes 393224 | tf_op jit(solution)/shard_map/ppermute | solution.py:477
  38.5 7.6 %collective-permute-start.14 = (bf16[256,256]{1,0:T(8,128)(2,1)S(1)}, bf16[256,256]{1,0:T(8,128)(2,1)S(1)}, u32[]{:S(2)}, u32[]{:S(2)}) collective-permute-start(bf16[256,256]{1,0:T(8,128)(2,1)S(1)} %scale_grads.1.mine), channel_id=1, source_target_pairs={{0,8},{1,9},{2,10},{3,11},{4,12},{5,13},{6,14},{7,15},{8,0},{9,1},... | collective-permute-start | bytes 393224 | tf_op jit(solution)/shard_map/ppermute | solution.py:477
  39.7 6.5 %collective-permute-start.15 = (f32[32,256]{1,0:T(8,128)S(1)}, f32[32,256]{1,0:T(8,128)S(1)}, u32[]{:S(2)}, u32[]{:S(2)}) collective-permute-start(f32[32,256]{1,0:T(8,128)S(1)} %add_up.2.here), channel_id=1, source_target_pairs={{224,0},{33,1},{226,2},{35,3},{228,4},{37,5},{230,6},{39,7},{232,8... | collective-permute-start | bytes 98312 | tf_op jit(solution)/shard_map/ppermute | solution.py:489
  46.2 8.7 %collective-permute-start.21 = (bf16[2,256,256]{2,1,0:T(8,128)(2,1)S(1)}, bf16[2,256,256]{2,1,0:T(8,128)(2,1)S(1)}, u32[]{:S(2)}, u32[]{:S(2)}) collective-permute-start(bf16[2,256,256]{2,1,0:T(8,128)(2,1)S(1)} %pair.1.mine), channel_id=1, source_target_pairs={{0,1},{1,0},{2,3},{3,2},{4,5},{5,4},{6,7},{7,6},{8,9},{9,8},{10,11... | collective-permute-start | bytes 786440 | tf_op jit(solution)/shard_map/ppermute | solution.py:470
  48.3 10.7 %collective-permute-start.16 = (bf16[2,256,256]{2,1,0:T(8,128)(2,1)S(1)}, bf16[2,256,256]{2,1,0:T(8,128)(2,1)S(1)}, u32[]{:S(2)}, u32[]{:S(2)}) collective-permute-start(bf16[2,256,256]{2,1,0:T(8,128)(2,1)S(1)} %pair.1.mine), channel_id=1, source_target_pairs={{0,12},{1,13},{2,14},{3,15},{4,0},{5,1},{6,2},{7,3},{8,4},{9,5},{1... | collective-permute-start | bytes 786440 | tf_op jit(solution)/shard_map/ppermute | solution.py:477
  49.5 9.6 %collective-permute-start.17 = (bf16[2,256,256]{2,1,0:T(8,128)(2,1)S(1)}, bf16[2,256,256]{2,1,0:T(8,128)(2,1)S(1)}, u32[]{:S(2)}, u32[]{:S(2)}) collective-permute-start(bf16[2,256,256]{2,1,0:T(8,128)(2,1)S(1)} %pair.1.mine), channel_id=1, source_target_pairs={{0,4},{1,5},{2,6},{3,7},{4,8},{5,9},{6,10},{7,11},{8,12},{9,13},{1... | collective-permute-start | bytes 786440 | tf_op jit(solution)/shard_map/ppermute | solution.py:477
  49.8 3.2 %collective-permute-start.22 = (bf16[1,256,256]{2,1,0:T(8,128)(2,1)S(1)}, bf16[1,256,256]{2,1,0:T(8,128)(2,1)S(1)}, u32[]{:S(2)}, u32[]{:S(2)}) collective-permute-start(bf16[1,256,256]{2,1,0:T(8,128)(2,1)S(1)} %bitcast.2), channel_id=1, source_target_pairs={{0,1},{1,0},{2,3},{3,2},{4,5},{5,4},{6,7},{7,6},{8,9},{9,8},{10,11... | collective-permute-start | bytes 393224 | tf_op jit(solution)/shard_map/ppermute | solution.py:470
  50.5 1.2 %collective-permute-start.19 = (f32[32,256]{1,0:T(8,128)S(1)}, f32[32,256]{1,0:T(8,128)S(1)}, u32[]{:S(2)}, u32[]{:S(2)}) collective-permute-start(f32[32,256]{1,0:T(8,128)S(1)} %collective-permute-done.15.direct), channel_id=1, source_target_pairs={{0,1},{1,0},{2,3},{3,2},{4,5},{5,4},{6,7},{7,6},{8,9},{9,8},{10,11... | collective-permute-start | bytes 98312 | tf_op jit(solution)/shard_map/ppermute | solution.py:470
  51.7 7.4 %collective-permute-start.18 = (bf16[256,256]{1,0:T(8,128)(2,1)S(1)}, bf16[256,256]{1,0:T(8,128)(2,1)S(1)}, u32[]{:S(2)}, u32[]{:S(2)}) collective-permute-start(bf16[256,256]{1,0:T(8,128)(2,1)S(1)} %collective-permute-done.14), channel_id=1, source_target_pairs={{0,2},{1,3},{2,0},{3,1},{4,6},{5,7},{6,4},{7,5},{8,10},{9,11},{10,... | collective-permute-start | bytes 393224 | tf_op jit(solution)/shard_map/ppermute | solution.py:477
  53.0 6.1 %collective-permute-start.20 = (f32[32,256]{1,0:T(8,128)S(1)}, f32[32,256]{1,0:T(8,128)S(1)}, u32[]{:S(2)}, u32[]{:S(2)}) collective-permute-start(f32[32,256]{1,0:T(8,128)S(1)} %get-tuple-element.80), channel_id=1, source_target_pairs={{96,0},{161,1},{98,2},{163,3},{100,4},{165,5},{102,6},{167,7},{104... | collective-permute-start | bytes 98312 | tf_op jit(solution)/shard_map/ppermute | solution.py:489
  59.1 2.6 %collective-permute-start.23 = (bf16[2,256,256]{2,1,0:T(8,128)(2,1)S(1)}, bf16[2,256,256]{2,1,0:T(8,128)(2,1)S(1)}, u32[]{:S(2)}, u32[]{:S(2)}) collective-permute-start(bf16[2,256,256]{2,1,0:T(8,128)(2,1)S(1)} %collective-permute-done.16.refs_0_), channel_id=1, source_target_pairs={{0,1},{1,0},{2,3},{3,2},{4,5},{5,4},{6,7},{7,6},{8,9},{9,8},{10,11... | collective-permute-start | bytes 786440 | tf_op jit(solution)/shard_map/ppermute | solution.py:470
  59.6 2.1 %collective-permute-start.24 = (bf16[2,256,256]{2,1,0:T(8,128)(2,1)S(1)}, bf16[2,256,256]{2,1,0:T(8,128)(2,1)S(1)}, u32[]{:S(2)}, u32[]{:S(2)}) collective-permute-start(bf16[2,256,256]{2,1,0:T(8,128)(2,1)S(1)} %collective-permute-done.17.refs_1_), channel_id=1, source_target_pairs={{0,1},{1,0},{2,3},{3,2},{4,5},{5,4},{6,7},{7,6},{8,9},{9,8},{10,11... | collective-permute-start | bytes 786440 | tf_op jit(solution)/shard_map/ppermute | solution.py:470
  59.7 2.0 %collective-permute-start.25 = (bf16[1,256,256]{2,1,0:T(8,128)(2,1)S(1)}, bf16[1,256,256]{2,1,0:T(8,128)(2,1)S(1)}, u32[]{:S(2)}, u32[]{:S(2)}) collective-permute-start(bf16[1,256,256]{2,1,0:T(8,128)(2,1)S(1)} %bitcast.4), channel_id=1, source_target_pairs={{0,1},{1,0},{2,3},{3,2},{4,5},{5,4},{6,7},{7,6},{8,9},{9,8},{10,11... | collective-permute-start | bytes 393224 | tf_op jit(solution)/shard_map/ppermute | solution.py:470
  60.1 1.6 %collective-permute-start.26 = (f32[32,256]{1,0:T(8,128)S(1)}, f32[32,256]{1,0:T(8,128)S(1)}, u32[]{:S(2)}, u32[]{:S(2)}) collective-permute-start(f32[32,256]{1,0:T(8,128)S(1)} %ring_end.1.refs_0_), channel_id=1, source_target_pairs={{0,1},{1,0},{2,3},{3,2},{4,5},{5,4},{6,7},{7,6},{8,9},{9,8},{10,11... | collective-permute-start | bytes 98312 | tf_op jit(solution)/shard_map/ppermute | solution.py:470
  61.7 5.0 %collective-permute-start.27 = (f32[32,256]{1,0:T(8,128)S(1)}, f32[32,256]{1,0:T(8,128)S(1)}, u32[]{:S(2)}, u32[]{:S(2)}) collective-permute-start(f32[32,256]{1,0:T(8,128)S(1)} %add_up.3.here), channel_id=1, source_target_pairs={{0,16},{16,0},{32,48},{48,32},{64,80},{80,64},{96,112},{112,96},{1... | collective-permute-start | bytes 98312 | tf_op jit(solution)/shard_map/ppermute | solution.py:548

commit v7 on v6

--- a/solution.py
+++ b/solution.py
@@ -129,9 +129,9 @@
     return jnp.concatenate([key, part[:, 2 * HEAD :].astype(F32)], axis=1)
 
 
-def pack_body(key_keep, value_keep, key_recv, value_recv, *outs):
+def pack_body(chunks, key_keep, value_keep, key_recv, value_recv, *outs):
     chip = lax.div(lax.axis_index("tensor"), 2)
-    for (across, row), out in zip(SENT + KEPT, outs):
+    for (across, row), out in zip(chunks, outs):
         columns = pl.ds(pl.multiple_of(home_of(chip, across, row) * HEAD, HEAD), HEAD)
         key = key_keep[:, columns] + key_recv[:, columns]
         value = value_keep[:, columns] + value_recv[:, columns].astype(F32)
@@ -142,9 +142,11 @@
             encode(total, out)
 
 
-def pack(*parts):
-    outs = [((HALF, 3 * HEAD), BF)] * len(SENT) + [((HALF, 2 * HEAD), F32)] * len(KEPT)
-    return call("pack", pack_body, outs, parts)
+def pack(name, chunks, *parts):
+    outs = [
+        ((HALF, 2 * HEAD), F32) if chunk in KEPT else ((HALF, 3 * HEAD), BF) for chunk in chunks
+    ]
+    return call(name, functools.partial(pack_body, chunks), outs, parts)
 
 
 def relay_body(kept, *refs):
@@ -507,8 +509,9 @@
     value_recv = core_swap(value_send)
     weights = [key_weight, value_weight]
     key_keep, value_keep = project("project_keep", False, tokens, weights, [F32, F32])
-    packed = pack(key_keep, value_keep, key_recv, value_recv)
-    part_21, part_11, part_31, part_10, part_30, kept_20, kept_01, kept_00 = packed
+    sides = (key_keep, value_keep, key_recv, value_recv)
+    part_21, part_11, part_31 = pack("pack_relayed", SENT[:3], *sides)
+    part_10, part_30, kept_20, kept_01, kept_00 = pack("pack_rest", SENT[3:] + KEPT, *sides)
     part_20 = relay(kept_20, chip_from(part_21, 0, 1))
     part_01 = relay(kept_01, chip_from(part_11, -1, 0), chip_from(part_31, 1, 0))
     parts = [
@@ -529,10 +532,12 @@
     grad_low = scale_grads(place, keep, recv, key_scale, value_scale)
     grad_low, sums_other = lax.optimization_barrier((grad_low, core_swap(sums)))
     sums = add_up(sums, sums_other)
-    row_part, far_part, ring = lax.optimization_barrier(
-        (chip_from(grad_low, 0, 1), chip_from(grad_low, 2, 0), depth_from(sums, (-1, 1)))
+    row_part, ring = lax.optimization_barrier(
+        (chip_from(grad_low, 0, 1), depth_from(sums, (-1, 1)))
     )
-    pair = pair_up(grad_low, row_part)
+    pair, far_part = lax.optimization_barrier(
+        (pair_up(grad_low, row_part), chip_from(grad_low, 2, 0))
+    )
     three, give = ring_sums(sums, ring, core_swap(ring))
     early = [pair, far_part[None]]
     near = near_grads(place, early, [core_swap(piece) for piece in early], weight)

time: 67.5 us -> 67.1 us (level)
    pallas_call x18 -> x19, Pallas kernels: 15.8 us -> 15.8 us  [call(): pl.pallas_call(body, in_specs=[pl.BlockSpec(memory_space=space) for space...]
  transfers between devices with their start and end apart: 28 -> 28, of which waited for: 11 -> 11; matrix products, arithmetic and copies ran while one was open for 0% -> 0% of each run, Pallas kernels for 23% -> 24%
where the time goes in v7:
time: 67.1 us; the launch traced here: 67 us
  starting transfers between devices  33.3 us (50%)
  Pallas kernels  20.7 us (31%)
  waiting for transfers between devices  12 us (18%)
  between operations  0.93 us (1%)
    pallas_call x19, Pallas kernels, call(): pl.pallas_call(body, in_specs=[pl.BlockSpec(memory_space=space) for space...  15.8 us
    ppermute x12, starting transfers between devices, chip_from(): return lax.ppermute(array, 'tensor', pairs)  12.1 us
    ppermute x13, starting transfers between devices, core_swap(): return lax.ppermute(array, 'tensor', CORE_SWAP)  11.5 us
    ppermute x2, starting transfers between devices, depth_from(): return lax.ppermute(array, ('dp', 'tensor'), pairs)  6.88 us
    ppermute x12, waiting for transfers between devices, chip_from(): return lax.ppermute(array, 'tensor', pairs)  4.65 us
    ppermute x2, waiting for transfers between devices, depth_from(): return lax.ppermute(array, ('dp', 'tensor'), pairs)  3.89 us
    ppermute x13, waiting for transfers between devices, core_swap(): return lax.ppermute(array, 'tensor', CORE_SWAP)  3.46 us
    pallas_call x1, Pallas kernels, load_project(): pl.pallas_call(load_body, in_specs=[pl.BlockSpec(memory_space=pltpu.HBM)]...  2.97 us
  transfers between devices with their start and end apart: 28, of which 11 were waited for; matrix products, arithmetic and copies ran while one was open for 0% of the time, Pallas kernels for 24%

profile of v7, /device:TPU:1, one launch (start us, length us, event | category | flops | bytes accessed | tf_op | source)
XLA Modules:
  0.0 67.0 jit_solution(3353972151782442572)
XLA Ops:
  0.6 3.0 %project_key.1 = (f32[256,1024]{1,0:T(8,128)S(1)}, bf16[512,1024]{1,0:T(8,128)(2,1)S(1)}, bf16[1024,1024]{1,0:T(8,128)(2,1)S(1)}, bf16[1024,1024]{1,0:T(8,128)(2,1)S(1)}) custom-call(bf16[512,1024]{1,0:T(8,128)(2,1)} %tokens.1, bf16[1024,1024]{1,0:T(8,128)(2,1)} %key_weight.1, bf16[1024,1024]{1,0:T(8,128)(2,1)} %value_weight.1), custom_call_target="tpu_custom_call" | custom-call | tf_op jit(solution)/shard_map/project_key/pallas_call | solution.py:83
  3.6 3.3 %collective-permute-start = (f32[256,1024]{1,0:T(8,128)S(1)}, f32[256,1024]{1,0:T(8,128)S(1)}, u32[]{:S(2)}, u32[]{:S(2)}) collective-permute-start(f32[256,1024]{1,0:T(8,128)S(1)} %get-tuple-element.56), channel_id=1, source_target_pairs={{0,1},{1,0},{2,3},{3,2},{4,5},{5,4},{6,7},{7,6},{8,9},{9,8},{10,11... | collective-permute-start | bytes 3145736 | tf_op jit(solution)/shard_map/ppermute | solution.py:472
  6.9 0.7 %project_value.1 = bf16[256,1024]{1,0:T(8,128)(2,1)S(1)} custom-call(bf16[512,1024]{1,0:T(8,128)(2,1)S(1)} %get-tuple-element.51.tokens, bf16[1024,1024]{1,0:T(8,128)(2,1)S(1)} %get-tuple-element.53.refs_1_.refs_0_.value_weight), custom_call_target="tpu_custom_call" | custom-call | flops 536870912 | bytes 3145728 | tf_op jit(solution)/shard_map/project_value/pallas_call | solution.py:31
  7.7 0.1 collective-permute-start.1
  7.8 1.3 %project_keep.1 = (f32[256,1024]{1,0:T(8,128)S(1)}, f32[256,1024]{1,0:T(8,128)S(1)}) custom-call(bf16[512,1024]{1,0:T(8,128)(2,1)S(1)} %get-tuple-element.51.tokens, bf16[1024,1024]{1,0:T(8,128)(2,1)S(1)} %get-tuple-element.52.refs_0_.key_weight, bf16[1024,1024]{1,0:T(8,128)(2,1)S(1)} %get-tuple-element.53.refs_1_.refs_0_.value_weight), custom_call_target="tpu_custom_call" | custom-call | flops 1073741824 | bytes 5242880 | tf_op jit(solution)/shard_map/project_keep/pallas_call | solution.py:31
  9.0 0.9 %collective-permute-done.1.value_recv = bf16[256,1024]{1,0:T(8,128)(2,1)S(1)} collective-permute-done((bf16[256,1024]{1,0:T(8,128)(2,1)S(1)}, bf16[256,1024]{1,0:T(8,128)(2,1)S(1)}, u32[]{:S(2)}, u32[]{:S(2)}) %collective-permute-start.1) | collective-permute-done | bytes 524320 | tf_op jit(solution)/shard_map/ppermute | solution.py:472
  10.0 0.0 collective-permute-done.key_recv
  10.0 0.2 pack_relayed.1
  10.2 0.1 collective-permute-start.6
  10.3 2.7 %collective-permute-start.7 = (bf16[256,384]{1,0:T(8,128)(2,1)S(1)}, bf16[256,384]{1,0:T(8,128)(2,1)S(1)}, u32[]{:S(2)}, u32[]{:S(2)}) collective-permute-start(bf16[256,384]{1,0:T(8,128)(2,1)S(1)} %get-tuple-element.63), channel_id=1, source_target_pairs={{0,12},{1,13},{2,14},{3,15},{4,0},{5,1},{6,2},{7,3},{8,4},{9,5},{1... | collective-permute-start | bytes 589832 | tf_op jit(solution)/shard_map/ppermute | solution.py:479
  13.0 0.3 pack_rest.1
  13.3 0.1 collective-permute-start.2
  13.4 2.7 %collective-permute-start.3 = (bf16[256,384]{1,0:T(8,128)(2,1)S(1)}, bf16[256,384]{1,0:T(8,128)(2,1)S(1)}, u32[]{:S(2)}, u32[]{:S(2)}) collective-permute-start(bf16[256,384]{1,0:T(8,128)(2,1)S(1)} %get-tuple-element.58), channel_id=1, source_target_pairs={{0,12},{1,13},{2,14},{3,15},{4,0},{5,1},{6,2},{7,3},{8,4},{9,5},{1... | collective-permute-start | bytes 589832 | tf_op jit(solution)/shard_map/ppermute | solution.py:479
  16.1 1.5 %collective-permute-done.6.refs_0_ = bf16[256,384]{1,0:T(8,128)(2,1)S(1)} collective-permute-done((bf16[256,384]{1,0:T(8,128)(2,1)S(1)}, bf16[256,384]{1,0:T(8,128)(2,1)S(1)}, u32[]{:S(2)}, u32[]{:S(2)}) %collective-permute-start.6) | collective-permute-done | bytes 196640 | tf_op jit(solution)/shard_map/ppermute | solution.py:479
  17.6 0.0 collective-permute-done.7.refs_1_
  17.6 0.1 relay.3
  17.7 0.1 collective-permute-start.8
  17.8 0.6 collective-permute-done.4.refs_0_
  18.4 0.1 relay.2
  18.5 0.0 copy-start.4
  18.5 0.0 copy-start.5
  18.5 0.0 copy-start.2
  18.5 0.0 copy-start.3
  18.5 0.0 copy-start
  18.5 0.0 copy-start.1
  18.5 1.1 %collective-permute-start.5 = (bf16[256,384]{1,0:T(8,128)(2,1)S(1)}, bf16[256,384]{1,0:T(8,128)(2,1)S(1)}, u32[]{:S(2)}, u32[]{:S(2)}) collective-permute-start(bf16[256,384]{1,0:T(8,128)(2,1)S(1)} %relay.2), channel_id=1, source_target_pairs={{0,8},{1,9},{2,10},{3,11},{4,12},{5,13},{6,14},{7,15},{8,0},{9,1},... | collective-permute-start | bytes 589832 | tf_op jit(solution)/shard_map/ppermute | solution.py:479
  19.7 1.2 %order_weights.1.weight.refs_4_.refs_5_ = bf16[1024,2048]{1,0:T(8,128)(2,1)S(1)} custom-call(bf16[1024,1024]{1,0:T(8,128)(2,1)S(1)} %get-tuple-element.52.refs_0_.key_weight, bf16[1024,1024]{1,0:T(8,128)(2,1)S(1)} %get-tuple-element.53.refs_1_.refs_0_.value_weight), custom_call_target="tpu_custom_call" | custom-call | bytes 4194304 | tf_op jit(solution)/shard_map/order_weights/pallas_call | solution.py:31
  20.9 1.3 %place.1 = s32[10]{0:T(128)S(1)} custom-call(s32[1,512]{1,0:T(1,128)S(1)} %copy-done.4, s32[1,4]{1,0:T(1,128)S(1)} %copy-done.5), custom_call_target="tpu_custom_call" | custom-call | tf_op jit(solution)/shard_map/place/pallas_call | solution.py:174
  22.2 0.0 collective-permute-done.3.refs_1_
  22.2 0.4 collective-permute-done.8.refs_3_
  22.6 2.1 %collective-permute-done.5.refs_2_ = bf16[256,384]{1,0:T(8,128)(2,1)S(1)} collective-permute-done((bf16[256,384]{1,0:T(8,128)(2,1)S(1)}, bf16[256,384]{1,0:T(8,128)(2,1)S(1)}, u32[]{:S(2)}, u32[]{:S(2)}) %collective-permute-start.5) | collective-permute-done | bytes 196640 | tf_op jit(solution)/shard_map/ppermute | solution.py:479
  24.7 0.7 %finish.1 = (f32[256,256]{1,0:T(8,128)S(1)}, bf16[256,256]{1,0:T(8,128)(2,1)S(1)}) custom-call(s32[10]{0:T(128)S(1)} %place.1, f32[256,256]{1,0:T(8,128)S(1)} %get-tuple-element.65.kept, bf16[256,384]{1,0:T(8,128)(2,1)S(1)} %collective-permute-done.2.refs_0_, bf16[256,384]{1,0:T(8,128)(2,1)S(1)} %collective-permute-done.3.refs_1_, ...), custom_call_target="tpu_custom_call" | custom-call | bytes 1310760 | tf_op jit(solution)/shard_map/finish/pallas_call | solution.py:31
  25.4 3.1 %collective-permute-start.9 = (bf16[256,256]{1,0:T(8,128)(2,1)S(1)}, bf16[256,256]{1,0:T(8,128)(2,1)S(1)}, u32[]{:S(2)}, u32[]{:S(2)}) collective-permute-start(bf16[256,256]{1,0:T(8,128)(2,1)S(1)} %get-tuple-element.70.mine), channel_id=1, source_target_pairs={{0,1},{1,0},{2,3},{3,2},{4,5},{5,4},{6,7},{7,6},{8,9},{9,8},{10,11... | collective-permute-start | bytes 393224 | tf_op jit(solution)/shard_map/ppermute | solution.py:472
  28.5 0.3 collective-permute-start.11
  28.8 0.7 %collective-permute-done.9.other = bf16[256,256]{1,0:T(8,128)(2,1)S(1)} collective-permute-done((bf16[256,256]{1,0:T(8,128)(2,1)S(1)}, bf16[256,256]{1,0:T(8,128)(2,1)S(1)}, u32[]{:S(2)}, u32[]{:S(2)}) %collective-permute-start.9) | collective-permute-done | bytes 131104 | tf_op jit(solution)/shard_map/ppermute | solution.py:472
  29.5 4.6 %attention.1 = (f32[256,256]{1,0:T(8,128)S(1)}, f32[256,256]{1,0:T(8,128)S(1)}) custom-call(s32[10]{0:T(128)S(1)} %place.1, bf16[256,256]{1,0:T(8,128)(2,1)S(1)} %get-tuple-element.70.mine, bf16[256,256]{1,0:T(8,128)(2,1)S(1)} %collective-permute-done.9.other, bf16[512,1024]{1,0:T(8,128)(2,1)S(1)} %copy-done, bf16[512,1024]{1,0:T(8,128)(2,1)S(1)} %copy-done.1), custom_call_target="tpu_custom_call" | custom-call | bytes 2359336 | tf_op jit(solution)/shard_map/attention/pallas_call | solution.py:31
  34.1 0.4 collective-permute-start.10
  34.5 0.8 %tenant_table.1.refs_0_ = f32[32,256]{1,0:T(8,128)S(1)} custom-call(s32[10]{0:T(128)S(1)} %place.1, f32[256,256]{1,0:T(8,128)S(1)} %get-tuple-element.71.keep, f32[256,256]{1,0:T(8,128)S(1)} %get-tuple-element.72.send, f32[256,256]{1,0:T(8,128)S(1)} %get-tuple-element.73.base, f32[256,256]{1,0:T(8,128)S(1)} %collective-permute-done.11.base_other), custom_call_target="tpu_custom_call" | custom-call | bytes 1048616 | tf_op jit(solution)/shard_map/tenant_table/pallas_call | solution.py:31
  35.3 0.4 collective-permute-done.10.recv
  35.7 0.4 collective-permute-start.12
  36.1 0.6 scale_grads.1.mine
  36.7 0.2 collective-permute-done.12.refs_1_
  36.9 1.3 %collective-permute-start.13 = (bf16[256,256]{1,0:T(8,128)(2,1)S(1)}, bf16[256,256]{1,0:T(8,128)(2,1)S(1)}, u32[]{:S(2)}, u32[]{:S(2)}) collective-permute-start(bf16[256,256]{1,0:T(8,128)(2,1)S(1)} %scale_grads.1.mine), channel_id=1, source_target_pairs={{0,2},{1,3},{2,0},{3,1},{4,6},{5,7},{6,4},{7,5},{8,10},{9,11},{10,... | collective-permute-start | bytes 393224 | tf_op jit(solution)/shard_map/ppermute | solution.py:479
  38.2 1.2 %collective-permute-start.15 = (bf16[256,256]{1,0:T(8,128)(2,1)S(1)}, bf16[256,256]{1,0:T(8,128)(2,1)S(1)}, u32[]{:S(2)}, u32[]{:S(2)}) collective-permute-start(bf16[256,256]{1,0:T(8,128)(2,1)S(1)} %scale_grads.1.mine), channel_id=1, source_target_pairs={{0,8},{1,9},{2,10},{3,11},{4,12},{5,13},{6,14},{7,15},{8,0},{9,1},... | collective-permute-start | bytes 393224 | tf_op jit(solution)/shard_map/ppermute | solution.py:479
  39.4 5.3 %collective-permute-start.14 = (f32[32,256]{1,0:T(8,128)S(1)}, f32[32,256]{1,0:T(8,128)S(1)}, u32[]{:S(2)}, u32[]{:S(2)}) collective-permute-start(f32[32,256]{1,0:T(8,128)S(1)} %add_up.2.here), channel_id=1, source_target_pairs={{224,0},{33,1},{226,2},{35,3},{228,4},{37,5},{230,6},{39,7},{232,8... | collective-permute-start | bytes 98312 | tf_op jit(solution)/shard_map/ppermute | solution.py:491
  44.6 1.0 %collective-permute-done.14.direct = f32[32,256]{1,0:T(8,128)S(1)} collective-permute-done((f32[32,256]{1,0:T(8,128)S(1)}, f32[32,256]{1,0:T(8,128)S(1)}, u32[]{:S(2)}, u32[]{:S(2)}) %collective-permute-start.14) | collective-permute-done | bytes 32800 | tf_op jit(solution)/shard_map/ppermute | solution.py:491
  45.7 2.1 %collective-permute-start.21 = (bf16[2,256,256]{2,1,0:T(8,128)(2,1)S(1)}, bf16[2,256,256]{2,1,0:T(8,128)(2,1)S(1)}, u32[]{:S(2)}, u32[]{:S(2)}) collective-permute-start(bf16[2,256,256]{2,1,0:T(8,128)(2,1)S(1)} %pair.1.mine), channel_id=1, source_target_pairs={{0,1},{1,0},{2,3},{3,2},{4,5},{5,4},{6,7},{7,6},{8,9},{9,8},{10,11... | collective-permute-start | bytes 786440 | tf_op jit(solution)/shard_map/ppermute | solution.py:472
  47.8 1.3 %collective-permute-start.16 = (bf16[2,256,256]{2,1,0:T(8,128)(2,1)S(1)}, bf16[2,256,256]{2,1,0:T(8,128)(2,1)S(1)}, u32[]{:S(2)}, u32[]{:S(2)}) collective-permute-start(bf16[2,256,256]{2,1,0:T(8,128)(2,1)S(1)} %pair.1.mine), channel_id=1, source_target_pairs={{0,12},{1,13},{2,14},{3,15},{4,0},{5,1},{6,2},{7,3},{8,4},{9,5},{1... | collective-permute-start | bytes 786440 | tf_op jit(solution)/shard_map/ppermute | solution.py:479
  49.1 0.2 collective-permute-start.17
  49.3 0.6 collective-permute-start.22
  49.9 1.2 %collective-permute-done.19.swapped = f32[32,256]{1,0:T(8,128)S(1)} collective-permute-done((f32[32,256]{1,0:T(8,128)S(1)}, f32[32,256]{1,0:T(8,128)S(1)}, u32[]{:S(2)}, u32[]{:S(2)}) %collective-permute-start.19) | collective-permute-done | bytes 32800 | tf_op jit(solution)/shard_map/ppermute | solution.py:472
  51.1 1.5 %collective-permute-start.18 = (bf16[256,256]{1,0:T(8,128)(2,1)S(1)}, bf16[256,256]{1,0:T(8,128)(2,1)S(1)}, u32[]{:S(2)}, u32[]{:S(2)}) collective-permute-start(bf16[256,256]{1,0:T(8,128)(2,1)S(1)} %collective-permute-done.15), channel_id=1, source_target_pairs={{0,2},{1,3},{2,0},{3,1},{4,6},{5,7},{6,4},{7,5},{8,10},{9,11},{10,... | collective-permute-start | bytes 393224 | tf_op jit(solution)/shard_map/ppermute | solution.py:479
  52.6 1.6 %collective-permute-start.20 = (f32[32,256]{1,0:T(8,128)S(1)}, f32[32,256]{1,0:T(8,128)S(1)}, u32[]{:S(2)}, u32[]{:S(2)}) collective-permute-start(f32[32,256]{1,0:T(8,128)S(1)} %get-tuple-element.82), channel_id=1, source_target_pairs={{96,0},{161,1},{98,2},{163,3},{100,4},{165,5},{102,6},{167,7},{104... | collective-permute-start | bytes 98312 | tf_op jit(solution)/shard_map/ppermute | solution.py:491
  54.3 0.0 collective-permute-done.21.other
  54.3 1.6 %near_grads.1.refs_3_.refs_4_ = f32[512,1024]{1,0:T(8,128)S(1)} custom-call(s32[10]{0:T(128)S(1)} %place.1, bf16[2,256,256]{2,1,0:T(8,128)(2,1)S(1)} %pair.1.mine, bf16[1,256,256]{2,1,0:T(8,128)(2,1)S(1)} %bitcast.3, bf16[2,256,256]{2,1,0:T(8,128)(2,1)S(1)} %collective-permute-done.21.other, bf16[1,256,256]{2,1,0:T(8,128)(2,1)S(1)} %collective-permute-done.22.other_far, ...), custom_call_target="tpu_custom_call" | custom-call | flops 805306368 | bytes 4980776 | tf_op jit(solution)/shard_map/near_grads/pallas_call | solution.py:31
  55.8 2.9 %collective-permute-done.20.recv = f32[32,256]{1,0:T(8,128)S(1)} collective-permute-done((f32[32,256]{1,0:T(8,128)S(1)}, f32[32,256]{1,0:T(8,128)S(1)}, u32[]{:S(2)}, u32[]{:S(2)}) %collective-permute-start.20) | collective-permute-done | bytes 32800 | tf_op jit(solution)/shard_map/ppermute | solution.py:491
  58.7 0.5 collective-permute-start.23
  59.2 0.1 collective-permute-start.24
  59.3 0.4 collective-permute-start.25
  59.7 0.1 collective-permute-start.26
  59.9 1.4 %far_own.1.refs_3_ = bf16[256,1024]{1,0:T(8,128)(2,1)S(1)} custom-call(s32[10]{0:T(128)S(1)} %place.1, bf16[2,256,256]{2,1,0:T(8,128)(2,1)S(1)} %collective-permute-done.16.refs_0_, bf16[2,256,256]{2,1,0:T(8,128)(2,1)S(1)} %collective-permute-done.17.refs_1_, bf16[1,256,256]{2,1,0:T(8,128)(2,1)S(1)} %bitcast.5, f32[512,1024]{1,0:T(8,128)S(1)} %near_grads.1.refs_3_.refs_4_, ...), custom_call_target="tpu_custom_call" | custom-call | flops 671088640 | bytes 6946856 | tf_op jit(solution)/shard_map/far_own/pallas_call | solution.py:31
  61.3 2.8 %collective-permute-start.27 = (f32[32,256]{1,0:T(8,128)S(1)}, f32[32,256]{1,0:T(8,128)S(1)}, u32[]{:S(2)}, u32[]{:S(2)}) collective-permute-start(f32[32,256]{1,0:T(8,128)S(1)} %add_up.3.here), channel_id=1, source_target_pairs={{0,16},{16,0},{32,48},{48,32},{64,80},{80,64},{96,112},{112,96},{1... | collective-permute-start | bytes 98312 | tf_op jit(solution)/shard_map/ppermute | solution.py:553
  64.2 2.2 %far_grads.1 = bf16[512,1024]{1,0:T(8,128)(2,1)} custom-call(s32[10]{0:T(128)S(1)} %place.1, bf16[2,256,256]{2,1,0:T(8,128)(2,1)S(1)} %collective-permute-done.23.refs_0_, bf16[2,256,256]{2,1,0:T(8,128)(2,1)S(1)} %collective-permute-done.24.refs_1_, bf16[1,256,256]{2,1,0:T(8,128)(2,1)S(1)} %collective-permute-done.25.refs_2_, ...), custom_call_target="tpu_custom_call" | custom-call | flops 671088640 | bytes 7471144 | tf_op jit(solution)/shard_map/far_grads/pallas_call | solution.py:31
  66.4 0.7 %tenant_totals.1 = (f32[32,64]{1,0:T(8,128)}, f32[32,64]{1,0:T(8,128)}) custom-call(f32[32,256]{1,0:T(8,128)S(1)} %add_up.3.here, f32[32,256]{1,0:T(8,128)S(1)} %collective-permute-done.27.recv), custom_call_target="tpu_custom_call" | custom-call | tf_op jit(solution)/shard_map/tenant_totals/pallas_call | solution.py:463
  (26 shorter events, 0.1 us)
Async XLA Ops:
  3.6 6.4 %collective-permute-start = (f32[256,1024]{1,0:T(8,128)S(1)}, f32[256,1024]{1,0:T(8,128)S(1)}, u32[]{:S(2)}, u32[]{:S(2)}) collective-permute-start(f32[256,1024]{1,0:T(8,128)S(1)} %get-tuple-element.56), channel_id=1, source_target_pairs={{0,1},{1,0},{2,3},{3,2},{4,5},{5,4},{6,7},{7,6},{8,9},{9,8},{10,11... | collective-permute-start | bytes 3145736 | tf_op jit(solution)/shard_map/ppermute | solution.py:472
  7.7 2.3 %collective-permute-start.1 = (bf16[256,1024]{1,0:T(8,128)(2,1)S(1)}, bf16[256,1024]{1,0:T(8,128)(2,1)S(1)}, u32[]{:S(2)}, u32[]{:S(2)}) collective-permute-start(bf16[256,1024]{1,0:T(8,128)(2,1)S(1)} %project_value.1), channel_id=1, source_target_pairs={{0,1},{1,0},{2,3},{3,2},{4,5},{5,4},{6,7},{7,6},{8,9},{9,8},{10,11... | collective-permute-start | bytes 1572872 | tf_op jit(solution)/shard_map/ppermute | solution.py:472
  10.2 7.4 %collective-permute-start.6 = (bf16[256,384]{1,0:T(8,128)(2,1)S(1)}, bf16[256,384]{1,0:T(8,128)(2,1)S(1)}, u32[]{:S(2)}, u32[]{:S(2)}) collective-permute-start(bf16[256,384]{1,0:T(8,128)(2,1)S(1)} %get-tuple-element.62), channel_id=1, source_target_pairs={{0,4},{1,5},{2,6},{3,7},{4,8},{5,9},{6,10},{7,11},{8,12},{9,13},{1... | collective-permute-start | bytes 589832 | tf_op jit(solution)/shard_map/ppermute | solution.py:479
  10.3 7.3 %collective-permute-start.7 = (bf16[256,384]{1,0:T(8,128)(2,1)S(1)}, bf16[256,384]{1,0:T(8,128)(2,1)S(1)}, u32[]{:S(2)}, u32[]{:S(2)}) collective-permute-start(bf16[256,384]{1,0:T(8,128)(2,1)S(1)} %get-tuple-element.63), channel_id=1, source_target_pairs={{0,12},{1,13},{2,14},{3,15},{4,0},{5,1},{6,2},{7,3},{8,4},{9,5},{1... | collective-permute-start | bytes 589832 | tf_op jit(solution)/shard_map/ppermute | solution.py:479
  12.9 5.5 %collective-permute-start.4 = (bf16[256,384]{1,0:T(8,128)(2,1)S(1)}, bf16[256,384]{1,0:T(8,128)(2,1)S(1)}, u32[]{:S(2)}, u32[]{:S(2)}) collective-permute-start(bf16[256,384]{1,0:T(8,128)(2,1)S(1)} %get-tuple-element.60), channel_id=1, source_target_pairs={{0,2},{1,3},{2,0},{3,1},{4,6},{5,7},{6,4},{7,5},{8,10},{9,11},{10,... | collective-permute-start | bytes 589832 | tf_op jit(solution)/shard_map/ppermute | solution.py:479
  13.3 8.9 %collective-permute-start.2 = (bf16[256,384]{1,0:T(8,128)(2,1)S(1)}, bf16[256,384]{1,0:T(8,128)(2,1)S(1)}, u32[]{:S(2)}, u32[]{:S(2)}) collective-permute-start(bf16[256,384]{1,0:T(8,128)(2,1)S(1)} %get-tuple-element.57), channel_id=1, source_target_pairs={{0,4},{1,5},{2,6},{3,7},{4,8},{5,9},{6,10},{7,11},{8,12},{9,13},{1... | collective-permute-start | bytes 589832 | tf_op jit(solution)/shard_map/ppermute | solution.py:479
  13.4 8.8 %collective-permute-start.3 = (bf16[256,384]{1,0:T(8,128)(2,1)S(1)}, bf16[256,384]{1,0:T(8,128)(2,1)S(1)}, u32[]{:S(2)}, u32[]{:S(2)}) collective-permute-start(bf16[256,384]{1,0:T(8,128)(2,1)S(1)} %get-tuple-element.58), channel_id=1, source_target_pairs={{0,12},{1,13},{2,14},{3,15},{4,0},{5,1},{6,2},{7,3},{8,4},{9,5},{1... | collective-permute-start | bytes 589832 | tf_op jit(solution)/shard_map/ppermute | solution.py:479
  17.7 4.9 %collective-permute-start.8 = (bf16[256,384]{1,0:T(8,128)(2,1)S(1)}, bf16[256,384]{1,0:T(8,128)(2,1)S(1)}, u32[]{:S(2)}, u32[]{:S(2)}) collective-permute-start(bf16[256,384]{1,0:T(8,128)(2,1)S(1)} %relay.3), channel_id=1, source_target_pairs={{0,2},{1,3},{2,0},{3,1},{4,6},{5,7},{6,4},{7,5},{8,10},{9,11},{10,... | collective-permute-start | bytes 589832 | tf_op jit(solution)/shard_map/ppermute | solution.py:479
  18.5 2.4 %copy-start.4 = (s32[1,512]{1,0:T(1,128)S(1)}, s32[1,512]{1,0:T(1,128)}, u32[]{:S(2)}) copy-start(s32[1,512]{1,0:T(1,128)} %segments.1) | copy-start | bytes 6148
  18.5 2.4 %copy-start.5 = (s32[1,4]{1,0:T(1,128)S(1)}, s32[1,4]{1,0:T(1,128)}, u32[]{:S(2)}) copy-start(s32[1,4]{1,0:T(1,128)} %tenants.1) | copy-start | bytes 52
  18.5 6.2 %copy-start.2 = (f32[32,1024]{1,0:T(8,128)S(1)}, f32[32,1024]{1,0:T(8,128)}, u32[]{:S(2)}) copy-start(f32[32,1024]{1,0:T(8,128)} %key_scale.1) | copy-start | bytes 393220
  18.5 6.2 %copy-start.3 = (f32[32,1024]{1,0:T(8,128)S(1)}, f32[32,1024]{1,0:T(8,128)}, u32[]{:S(2)}) copy-start(f32[32,1024]{1,0:T(8,128)} %value_scale.1) | copy-start | bytes 393220
  18.5 11.0 %copy-start = (bf16[512,1024]{1,0:T(8,128)(2,1)S(1)}, bf16[512,1024]{1,0:T(8,128)(2,1)}, u32[]{:S(2)}) copy-start(bf16[512,1024]{1,0:T(8,128)(2,1)} %queries.1) | copy-start | bytes 3145732
  18.5 11.0 %copy-start.1 = (bf16[512,1024]{1,0:T(8,128)(2,1)S(1)}, bf16[512,1024]{1,0:T(8,128)(2,1)}, u32[]{:S(2)}) copy-start(bf16[512,1024]{1,0:T(8,128)(2,1)} %out_grad.1) | copy-start | bytes 3145732
  18.5 6.1 %collective-permute-start.5 = (bf16[256,384]{1,0:T(8,128)(2,1)S(1)}, bf16[256,384]{1,0:T(8,128)(2,1)S(1)}, u32[]{:S(2)}, u32[]{:S(2)}) collective-permute-start(bf16[256,384]{1,0:T(8,128)(2,1)S(1)} %relay.2), channel_id=1, source_target_pairs={{0,8},{1,9},{2,10},{3,11},{4,12},{5,13},{6,14},{7,15},{8,0},{9,1},... | collective-permute-start | bytes 589832 | tf_op jit(solution)/shard_map/ppermute | solution.py:479
  25.4 4.1 %collective-permute-start.9 = (bf16[256,256]{1,0:T(8,128)(2,1)S(1)}, bf16[256,256]{1,0:T(8,128)(2,1)S(1)}, u32[]{:S(2)}, u32[]{:S(2)}) collective-permute-start(bf16[256,256]{1,0:T(8,128)(2,1)S(1)} %get-tuple-element.70.mine), channel_id=1, source_target_pairs={{0,1},{1,0},{2,3},{3,2},{4,5},{5,4},{6,7},{7,6},{8,9},{9,8},{10,11... | collective-permute-start | bytes 393224 | tf_op jit(solution)/shard_map/ppermute | solution.py:472
  28.5 6.0 %collective-permute-start.11 = (f32[256,256]{1,0:T(8,128)S(1)}, f32[256,256]{1,0:T(8,128)S(1)}, u32[]{:S(2)}, u32[]{:S(2)}) collective-permute-start(f32[256,256]{1,0:T(8,128)S(1)} %get-tuple-element.73.base), channel_id=1, source_target_pairs={{0,1},{1,0},{2,3},{3,2},{4,5},{5,4},{6,7},{7,6},{8,9},{9,8},{10,11... | collective-permute-start | bytes 786440 | tf_op jit(solution)/shard_map/ppermute | solution.py:472
  34.1 1.6 %collective-permute-start.10 = (f32[256,256]{1,0:T(8,128)S(1)}, f32[256,256]{1,0:T(8,128)S(1)}, u32[]{:S(2)}, u32[]{:S(2)}) collective-permute-start(f32[256,256]{1,0:T(8,128)S(1)} %get-tuple-element.72.send), channel_id=1, source_target_pairs={{0,1},{1,0},{2,3},{3,2},{4,5},{5,4},{6,7},{7,6},{8,9},{9,8},{10,11... | collective-permute-start | bytes 786440 | tf_op jit(solution)/shard_map/ppermute | solution.py:472
  35.7 1.2 %collective-permute-start.12 = (f32[32,256]{1,0:T(8,128)S(1)}, f32[32,256]{1,0:T(8,128)S(1)}, u32[]{:S(2)}, u32[]{:S(2)}) collective-permute-start(f32[32,256]{1,0:T(8,128)S(1)} %tenant_table.1.refs_0_), channel_id=1, source_target_pairs={{0,1},{1,0},{2,3},{3,2},{4,5},{5,4},{6,7},{7,6},{8,9},{9,8},{10,11... | collective-permute-start | bytes 98312 | tf_op jit(solution)/shard_map/ppermute | solution.py:472
  36.9 8.7 %collective-permute-start.13 = (bf16[256,256]{1,0:T(8,128)(2,1)S(1)}, bf16[256,256]{1,0:T(8,128)(2,1)S(1)}, u32[]{:S(2)}, u32[]{:S(2)}) collective-permute-start(bf16[256,256]{1,0:T(8,128)(2,1)S(1)} %scale_grads.1.mine), channel_id=1, source_target_pairs={{0,2},{1,3},{2,0},{3,1},{4,6},{5,7},{6,4},{7,5},{8,10},{9,11},{10,... | collective-permute-start | bytes 393224 | tf_op jit(solution)/shard_map/ppermute | solution.py:479
  38.2 7.5 %collective-permute-start.15 = (bf16[256,256]{1,0:T(8,128)(2,1)S(1)}, bf16[256,256]{1,0:T(8,128)(2,1)S(1)}, u32[]{:S(2)}, u32[]{:S(2)}) collective-permute-start(bf16[256,256]{1,0:T(8,128)(2,1)S(1)} %scale_grads.1.mine), channel_id=1, source_target_pairs={{0,8},{1,9},{2,10},{3,11},{4,12},{5,13},{6,14},{7,15},{8,0},{9,1},... | collective-permute-start | bytes 393224 | tf_op jit(solution)/shard_map/ppermute | solution.py:479
  39.4 6.3 %collective-permute-start.14 = (f32[32,256]{1,0:T(8,128)S(1)}, f32[32,256]{1,0:T(8,128)S(1)}, u32[]{:S(2)}, u32[]{:S(2)}) collective-permute-start(f32[32,256]{1,0:T(8,128)S(1)} %add_up.2.here), channel_id=1, source_target_pairs={{224,0},{33,1},{226,2},{35,3},{228,4},{37,5},{230,6},{39,7},{232,8... | collective-permute-start | bytes 98312 | tf_op jit(solution)/shard_map/ppermute | solution.py:491
  45.7 8.6 %collective-permute-start.21 = (bf16[2,256,256]{2,1,0:T(8,128)(2,1)S(1)}, bf16[2,256,256]{2,1,0:T(8,128)(2,1)S(1)}, u32[]{:S(2)}, u32[]{:S(2)}) collective-permute-start(bf16[2,256,256]{2,1,0:T(8,128)(2,1)S(1)} %pair.1.mine), channel_id=1, source_target_pairs={{0,1},{1,0},{2,3},{3,2},{4,5},{5,4},{6,7},{7,6},{8,9},{9,8},{10,11... | collective-permute-start | bytes 786440 | tf_op jit(solution)/shard_map/ppermute | solution.py:472
  47.8 10.9 %collective-permute-start.16 = (bf16[2,256,256]{2,1,0:T(8,128)(2,1)S(1)}, bf16[2,256,256]{2,1,0:T(8,128)(2,1)S(1)}, u32[]{:S(2)}, u32[]{:S(2)}) collective-permute-start(bf16[2,256,256]{2,1,0:T(8,128)(2,1)S(1)} %pair.1.mine), channel_id=1, source_target_pairs={{0,12},{1,13},{2,14},{3,15},{4,0},{5,1},{6,2},{7,3},{8,4},{9,5},{1... | collective-permute-start | bytes 786440 | tf_op jit(solution)/shard_map/ppermute | solution.py:479
  49.1 9.6 %collective-permute-start.17 = (bf16[2,256,256]{2,1,0:T(8,128)(2,1)S(1)}, bf16[2,256,256]{2,1,0:T(8,128)(2,1)S(1)}, u32[]{:S(2)}, u32[]{:S(2)}) collective-permute-start(bf16[2,256,256]{2,1,0:T(8,128)(2,1)S(1)} %pair.1.mine), channel_id=1, source_target_pairs={{0,4},{1,5},{2,6},{3,7},{4,8},{5,9},{6,10},{7,11},{8,12},{9,13},{1... | collective-permute-start | bytes 786440 | tf_op jit(solution)/shard_map/ppermute | solution.py:479
  49.3 3.3 %collective-permute-start.22 = (bf16[1,256,256]{2,1,0:T(8,128)(2,1)S(1)}, bf16[1,256,256]{2,1,0:T(8,128)(2,1)S(1)}, u32[]{:S(2)}, u32[]{:S(2)}) collective-permute-start(bf16[1,256,256]{2,1,0:T(8,128)(2,1)S(1)} %bitcast.2), channel_id=1, source_target_pairs={{0,1},{1,0},{2,3},{3,2},{4,5},{5,4},{6,7},{7,6},{8,9},{9,8},{10,11... | collective-permute-start | bytes 393224 | tf_op jit(solution)/shard_map/ppermute | solution.py:472
  49.9 1.2 %collective-permute-start.19 = (f32[32,256]{1,0:T(8,128)S(1)}, f32[32,256]{1,0:T(8,128)S(1)}, u32[]{:S(2)}, u32[]{:S(2)}) collective-permute-start(f32[32,256]{1,0:T(8,128)S(1)} %collective-permute-done.14.direct), channel_id=1, source_target_pairs={{0,1},{1,0},{2,3},{3,2},{4,5},{5,4},{6,7},{7,6},{8,9},{9,8},{10,11... | collective-permute-start | bytes 98312 | tf_op jit(solution)/shard_map/ppermute | solution.py:472
  51.1 7.6 %collective-permute-start.18 = (bf16[256,256]{1,0:T(8,128)(2,1)S(1)}, bf16[256,256]{1,0:T(8,128)(2,1)S(1)}, u32[]{:S(2)}, u32[]{:S(2)}) collective-permute-start(bf16[256,256]{1,0:T(8,128)(2,1)S(1)} %collective-permute-done.15), channel_id=1, source_target_pairs={{0,2},{1,3},{2,0},{3,1},{4,6},{5,7},{6,4},{7,5},{8,10},{9,11},{10,... | collective-permute-start | bytes 393224 | tf_op jit(solution)/shard_map/ppermute | solution.py:479
  52.6 6.1 %collective-permute-start.20 = (f32[32,256]{1,0:T(8,128)S(1)}, f32[32,256]{1,0:T(8,128)S(1)}, u32[]{:S(2)}, u32[]{:S(2)}) collective-permute-start(f32[32,256]{1,0:T(8,128)S(1)} %get-tuple-element.82), channel_id=1, source_target_pairs={{96,0},{161,1},{98,2},{163,3},{100,4},{165,5},{102,6},{167,7},{104... | collective-permute-start | bytes 98312 | tf_op jit(solution)/shard_map/ppermute | solution.py:491
  58.7 2.6 %collective-permute-start.23 = (bf16[2,256,256]{2,1,0:T(8,128)(2,1)S(1)}, bf16[2,256,256]{2,1,0:T(8,128)(2,1)S(1)}, u32[]{:S(2)}, u32[]{:S(2)}) collective-permute-start(bf16[2,256,256]{2,1,0:T(8,128)(2,1)S(1)} %collective-permute-done.16.refs_0_), channel_id=1, source_target_pairs={{0,1},{1,0},{2,3},{3,2},{4,5},{5,4},{6,7},{7,6},{8,9},{9,8},{10,11... | collective-permute-start | bytes 786440 | tf_op jit(solution)/shard_map/ppermute | solution.py:472
  59.2 2.1 %collective-permute-start.24 = (bf16[2,256,256]{2,1,0:T(8,128)(2,1)S(1)}, bf16[2,256,256]{2,1,0:T(8,128)(2,1)S(1)}, u32[]{:S(2)}, u32[]{:S(2)}) collective-permute-start(bf16[2,256,256]{2,1,0:T(8,128)(2,1)S(1)} %collective-permute-done.17.refs_1_), channel_id=1, source_target_pairs={{0,1},{1,0},{2,3},{3,2},{4,5},{5,4},{6,7},{7,6},{8,9},{9,8},{10,11... | collective-permute-start | bytes 786440 | tf_op jit(solution)/shard_map/ppermute | solution.py:472
  59.3 2.0 %collective-permute-start.25 = (bf16[1,256,256]{2,1,0:T(8,128)(2,1)S(1)}, bf16[1,256,256]{2,1,0:T(8,128)(2,1)S(1)}, u32[]{:S(2)}, u32[]{:S(2)}) collective-permute-start(bf16[1,256,256]{2,1,0:T(8,128)(2,1)S(1)} %bitcast.4), channel_id=1, source_target_pairs={{0,1},{1,0},{2,3},{3,2},{4,5},{5,4},{6,7},{7,6},{8,9},{9,8},{10,11... | collective-permute-start | bytes 393224 | tf_op jit(solution)/shard_map/ppermute | solution.py:472
  59.7 1.6 %collective-permute-start.26 = (f32[32,256]{1,0:T(8,128)S(1)}, f32[32,256]{1,0:T(8,128)S(1)}, u32[]{:S(2)}, u32[]{:S(2)}) collective-permute-start(f32[32,256]{1,0:T(8,128)S(1)} %ring_end.1.refs_0_), channel_id=1, source_target_pairs={{0,1},{1,0},{2,3},{3,2},{4,5},{5,4},{6,7},{7,6},{8,9},{9,8},{10,11... | collective-permute-start | bytes 98312 | tf_op jit(solution)/shard_map/ppermute | solution.py:472
  61.3 5.0 %collective-permute-start.27 = (f32[32,256]{1,0:T(8,128)S(1)}, f32[32,256]{1,0:T(8,128)S(1)}, u32[]{:S(2)}, u32[]{:S(2)}) collective-permute-start(f32[32,256]{1,0:T(8,128)S(1)} %add_up.3.here), channel_id=1, source_target_pairs={{0,16},{16,0},{32,48},{48,32},{64,80},{80,64},{96,112},{112,96},{1... | collective-permute-start | bytes 98312 | tf_op jit(solution)/shard_map/ppermute | solution.py:553

commit v8 on v7

--- a/solution.py
+++ b/solution.py
@@ -229,7 +229,6 @@
     other_rows = pl.ds(pl.multiple_of((1 - core) * HALF, HALF), HALF)
     tile[own_rows, :] = mine[...]
     tile[other_rows, :] = other[...]
-    grads[...] = jnp.zeros_like(grads)
     heads = queries.shape[1] // HEAD
     for block in range(TOK // BLOCK):
         first = max(0, block - 2) * BLOCK
@@ -237,8 +236,8 @@
         rows = slice(block * BLOCK, (block + 1) * BLOCK)
         visible = slice(first, first + reach)
         key_row = lax.broadcasted_iota(jnp.int32, (reach, BLOCK), 0) + first
-        query_row = lax.broadcasted_iota(jnp.int32, (reach, BLOCK), 1) + block * BLOCK
-        start = jnp.zeros((reach, BLOCK), jnp.int32)
+        query_row = lax.broadcasted_iota(jnp.int32, (1, BLOCK), 1) + block * BLOCK
+        start = jnp.zeros((1, BLOCK), jnp.int32)
         for seq in range(1, SEQS):
             start = jnp.where(query_row >= place[1 + seq], place[1 + seq], start)
         allowed = (key_row >= start) & (key_row <= query_row)
@@ -267,7 +266,10 @@
             (slice(HEAD, 2 * HEAD), probs_parts, out_parts),
         ):
             left, right = jnp.concatenate(left, axis=1), jnp.concatenate(right, axis=0)
-            grads[visible, part] += jnp.dot(left, right, preferred_element_type=F32)
+            total = jnp.dot(left, right, preferred_element_type=F32)
+            if reach > BLOCK:
+                grads[first : first + reach - BLOCK, part] += total[: reach - BLOCK]
+            grads[rows, part] = total[reach - BLOCK :]
     for rows, target in ((other_rows, send), (own_rows, keep)):
         target[:, :HEAD] = grads[rows, :HEAD] * SCALE
         target[:, HEAD:] = grads[rows, HEAD:]

time: 67.1 us -> 67.1 us (level)
  no operation moved by 1% of the time
where the time goes in v8:
time: 67.1 us
  starting transfers between devices  33.3 us (50%)
  Pallas kernels  20.8 us (31%)
  waiting for transfers between devices  12 us (18%)
  between operations  0.93 us (1%)
    pallas_call x19, Pallas kernels, call(): pl.pallas_call(body, in_specs=[pl.BlockSpec(memory_space=space) for space...  15.8 us
    ppermute x12, starting transfers between devices, chip_from(): return lax.ppermute(array, 'tensor', pairs)  12.1 us
    ppermute x13, starting transfers between devices, core_swap(): return lax.ppermute(array, 'tensor', CORE_SWAP)  11.5 us
    ppermute x2, starting transfers between devices, depth_from(): return lax.ppermute(array, ('dp', 'tensor'), pairs)  6.88 us
    ppermute x12, waiting for transfers between devices, chip_from(): return lax.ppermute(array, 'tensor', pairs)  4.65 us
    ppermute x2, waiting for transfers between devices, depth_from(): return lax.ppermute(array, ('dp', 'tensor'), pairs)  3.89 us
    ppermute x13, waiting for transfers between devices, core_swap(): return lax.ppermute(array, 'tensor', CORE_SWAP)  3.46 us
    pallas_call x1, Pallas kernels, load_project(): pl.pallas_call(load_body, in_specs=[pl.BlockSpec(memory_space=pltpu.HBM)]...  2.97 us
  transfers between devices with their start and end apart: 28, of which 11 were waited for; matrix products, arithmetic and copies ran while one was open for 0% of the time, Pallas kernels for 24%

profile of v8, /device:TPU:1, one launch (start us, length us, event | category | flops | bytes accessed | tf_op | source)
XLA Modules:
  0.0 67.1 jit_solution(4421802076110565561)
XLA Ops:
  0.6 3.0 %project_key.1 = (f32[256,1024]{1,0:T(8,128)S(1)}, bf16[512,1024]{1,0:T(8,128)(2,1)S(1)}, bf16[1024,1024]{1,0:T(8,128)(2,1)S(1)}, bf16[1024,1024]{1,0:T(8,128)(2,1)S(1)}) custom-call(bf16[512,1024]{1,0:T(8,128)(2,1)} %tokens.1, bf16[1024,1024]{1,0:T(8,128)(2,1)} %key_weight.1, bf16[1024,1024]{1,0:T(8,128)(2,1)} %value_weight.1), custom_call_target="tpu_custom_call" | custom-call | tf_op jit(solution)/shard_map/project_key/pallas_call | solution.py:83
  3.6 3.3 %collective-permute-start = (f32[256,1024]{1,0:T(8,128)S(1)}, f32[256,1024]{1,0:T(8,128)S(1)}, u32[]{:S(2)}, u32[]{:S(2)}) collective-permute-start(f32[256,1024]{1,0:T(8,128)S(1)} %get-tuple-element.56), channel_id=1, source_target_pairs={{0,1},{1,0},{2,3},{3,2},{4,5},{5,4},{6,7},{7,6},{8,9},{9,8},{10,11... | collective-permute-start | bytes 3145736 | tf_op jit(solution)/shard_map/ppermute | solution.py:474
  6.9 0.7 %project_value.1 = bf16[256,1024]{1,0:T(8,128)(2,1)S(1)} custom-call(bf16[512,1024]{1,0:T(8,128)(2,1)S(1)} %get-tuple-element.51.tokens, bf16[1024,1024]{1,0:T(8,128)(2,1)S(1)} %get-tuple-element.53.refs_1_.refs_0_.value_weight), custom_call_target="tpu_custom_call" | custom-call | flops 536870912 | bytes 3145728 | tf_op jit(solution)/shard_map/project_value/pallas_call | solution.py:31
  7.7 0.1 collective-permute-start.1
  7.8 1.3 %project_keep.1 = (f32[256,1024]{1,0:T(8,128)S(1)}, f32[256,1024]{1,0:T(8,128)S(1)}) custom-call(bf16[512,1024]{1,0:T(8,128)(2,1)S(1)} %get-tuple-element.51.tokens, bf16[1024,1024]{1,0:T(8,128)(2,1)S(1)} %get-tuple-element.52.refs_0_.key_weight, bf16[1024,1024]{1,0:T(8,128)(2,1)S(1)} %get-tuple-element.53.refs_1_.refs_0_.value_weight), custom_call_target="tpu_custom_call" | custom-call | flops 1073741824 | bytes 5242880 | tf_op jit(solution)/shard_map/project_keep/pallas_call | solution.py:31
  9.0 0.9 %collective-permute-done.1.value_recv = bf16[256,1024]{1,0:T(8,128)(2,1)S(1)} collective-permute-done((bf16[256,1024]{1,0:T(8,128)(2,1)S(1)}, bf16[256,1024]{1,0:T(8,128)(2,1)S(1)}, u32[]{:S(2)}, u32[]{:S(2)}) %collective-permute-start.1) | collective-permute-done | bytes 524320 | tf_op jit(solution)/shard_map/ppermute | solution.py:474
  10.0 0.0 collective-permute-done.key_recv
  10.0 0.2 pack_relayed.1
  10.2 0.1 collective-permute-start.6
  10.3 2.7 %collective-permute-start.7 = (bf16[256,384]{1,0:T(8,128)(2,1)S(1)}, bf16[256,384]{1,0:T(8,128)(2,1)S(1)}, u32[]{:S(2)}, u32[]{:S(2)}) collective-permute-start(bf16[256,384]{1,0:T(8,128)(2,1)S(1)} %get-tuple-element.63), channel_id=1, source_target_pairs={{0,12},{1,13},{2,14},{3,15},{4,0},{5,1},{6,2},{7,3},{8,4},{9,5},{1... | collective-permute-start | bytes 589832 | tf_op jit(solution)/shard_map/ppermute | solution.py:481
  12.9 0.0 collective-permute-start.4
  13.0 0.3 pack_rest.1
  13.3 0.1 collective-permute-start.2
  13.4 2.7 %collective-permute-start.3 = (bf16[256,384]{1,0:T(8,128)(2,1)S(1)}, bf16[256,384]{1,0:T(8,128)(2,1)S(1)}, u32[]{:S(2)}, u32[]{:S(2)}) collective-permute-start(bf16[256,384]{1,0:T(8,128)(2,1)S(1)} %get-tuple-element.58), channel_id=1, source_target_pairs={{0,12},{1,13},{2,14},{3,15},{4,0},{5,1},{6,2},{7,3},{8,4},{9,5},{1... | collective-permute-start | bytes 589832 | tf_op jit(solution)/shard_map/ppermute | solution.py:481
  16.1 1.5 %collective-permute-done.6.refs_0_ = bf16[256,384]{1,0:T(8,128)(2,1)S(1)} collective-permute-done((bf16[256,384]{1,0:T(8,128)(2,1)S(1)}, bf16[256,384]{1,0:T(8,128)(2,1)S(1)}, u32[]{:S(2)}, u32[]{:S(2)}) %collective-permute-start.6) | collective-permute-done | bytes 196640 | tf_op jit(solution)/shard_map/ppermute | solution.py:481
  17.6 0.1 relay.3
  17.7 0.1 collective-permute-start.8
  17.8 0.6 collective-permute-done.4.refs_0_
  18.4 0.1 relay.2
  18.5 0.0 copy-start.4
  18.5 0.0 copy-start.5
  18.5 0.0 copy-start.2
  18.5 0.0 copy-start.3
  18.5 0.0 copy-start
  18.5 0.0 copy-start.1
  18.5 1.1 %collective-permute-start.5 = (bf16[256,384]{1,0:T(8,128)(2,1)S(1)}, bf16[256,384]{1,0:T(8,128)(2,1)S(1)}, u32[]{:S(2)}, u32[]{:S(2)}) collective-permute-start(bf16[256,384]{1,0:T(8,128)(2,1)S(1)} %relay.2), channel_id=1, source_target_pairs={{0,8},{1,9},{2,10},{3,11},{4,12},{5,13},{6,14},{7,15},{8,0},{9,1},... | collective-permute-start | bytes 589832 | tf_op jit(solution)/shard_map/ppermute | solution.py:481
  19.7 1.2 %order_weights.1.weight.refs_4_.refs_5_ = bf16[1024,2048]{1,0:T(8,128)(2,1)S(1)} custom-call(bf16[1024,1024]{1,0:T(8,128)(2,1)S(1)} %get-tuple-element.52.refs_0_.key_weight, bf16[1024,1024]{1,0:T(8,128)(2,1)S(1)} %get-tuple-element.53.refs_1_.refs_0_.value_weight), custom_call_target="tpu_custom_call" | custom-call | bytes 4194304 | tf_op jit(solution)/shard_map/order_weights/pallas_call | solution.py:31
  20.9 1.3 %place.1 = s32[10]{0:T(128)S(1)} custom-call(s32[1,512]{1,0:T(1,128)S(1)} %copy-done.4, s32[1,4]{1,0:T(1,128)S(1)} %copy-done.5), custom_call_target="tpu_custom_call" | custom-call | tf_op jit(solution)/shard_map/place/pallas_call | solution.py:174
  22.2 0.0 collective-permute-done.2.refs_0_
  22.2 0.0 collective-permute-done.3.refs_1_
  22.2 0.4 collective-permute-done.8.refs_3_
  22.6 2.1 %collective-permute-done.5.refs_2_ = bf16[256,384]{1,0:T(8,128)(2,1)S(1)} collective-permute-done((bf16[256,384]{1,0:T(8,128)(2,1)S(1)}, bf16[256,384]{1,0:T(8,128)(2,1)S(1)}, u32[]{:S(2)}, u32[]{:S(2)}) %collective-permute-start.5) | collective-permute-done | bytes 196640 | tf_op jit(solution)/shard_map/ppermute | solution.py:481
  24.7 0.7 %finish.1 = (f32[256,256]{1,0:T(8,128)S(1)}, bf16[256,256]{1,0:T(8,128)(2,1)S(1)}) custom-call(s32[10]{0:T(128)S(1)} %place.1, f32[256,256]{1,0:T(8,128)S(1)} %get-tuple-element.65.kept, bf16[256,384]{1,0:T(8,128)(2,1)S(1)} %collective-permute-done.2.refs_0_, bf16[256,384]{1,0:T(8,128)(2,1)S(1)} %collective-permute-done.3.refs_1_, ...), custom_call_target="tpu_custom_call" | custom-call | bytes 1310760 | tf_op jit(solution)/shard_map/finish/pallas_call | solution.py:31
  25.4 3.1 %collective-permute-start.9 = (bf16[256,256]{1,0:T(8,128)(2,1)S(1)}, bf16[256,256]{1,0:T(8,128)(2,1)S(1)}, u32[]{:S(2)}, u32[]{:S(2)}) collective-permute-start(bf16[256,256]{1,0:T(8,128)(2,1)S(1)} %get-tuple-element.70.mine), channel_id=1, source_target_pairs={{0,1},{1,0},{2,3},{3,2},{4,5},{5,4},{6,7},{7,6},{8,9},{9,8},{10,11... | collective-permute-start | bytes 393224 | tf_op jit(solution)/shard_map/ppermute | solution.py:474
  28.5 0.3 collective-permute-start.11
  28.8 0.7 %collective-permute-done.9.other = bf16[256,256]{1,0:T(8,128)(2,1)S(1)} collective-permute-done((bf16[256,256]{1,0:T(8,128)(2,1)S(1)}, bf16[256,256]{1,0:T(8,128)(2,1)S(1)}, u32[]{:S(2)}, u32[]{:S(2)}) %collective-permute-start.9) | collective-permute-done | bytes 131104 | tf_op jit(solution)/shard_map/ppermute | solution.py:474
  29.5 4.6 %attention.1 = (f32[256,256]{1,0:T(8,128)S(1)}, f32[256,256]{1,0:T(8,128)S(1)}) custom-call(s32[10]{0:T(128)S(1)} %place.1, bf16[256,256]{1,0:T(8,128)(2,1)S(1)} %get-tuple-element.70.mine, bf16[256,256]{1,0:T(8,128)(2,1)S(1)} %collective-permute-done.9.other, bf16[512,1024]{1,0:T(8,128)(2,1)S(1)} %copy-done, bf16[512,1024]{1,0:T(8,128)(2,1)S(1)} %copy-done.1), custom_call_target="tpu_custom_call" | custom-call | bytes 2359336 | tf_op jit(solution)/shard_map/attention/pallas_call | solution.py:31
  34.1 0.4 collective-permute-start.10
  34.5 0.8 %tenant_table.1.refs_0_ = f32[32,256]{1,0:T(8,128)S(1)} custom-call(s32[10]{0:T(128)S(1)} %place.1, f32[256,256]{1,0:T(8,128)S(1)} %get-tuple-element.71.keep, f32[256,256]{1,0:T(8,128)S(1)} %get-tuple-element.72.send, f32[256,256]{1,0:T(8,128)S(1)} %get-tuple-element.73.base, f32[256,256]{1,0:T(8,128)S(1)} %collective-permute-done.11.base_other), custom_call_target="tpu_custom_call" | custom-call | bytes 1048616 | tf_op jit(solution)/shard_map/tenant_table/pallas_call | solution.py:31
  35.3 0.4 collective-permute-done.10.recv
  35.7 0.4 collective-permute-start.12
  36.1 0.6 scale_grads.1.mine
  36.7 0.2 collective-permute-done.12.refs_1_
  36.9 1.3 %collective-permute-start.13 = (bf16[256,256]{1,0:T(8,128)(2,1)S(1)}, bf16[256,256]{1,0:T(8,128)(2,1)S(1)}, u32[]{:S(2)}, u32[]{:S(2)}) collective-permute-start(bf16[256,256]{1,0:T(8,128)(2,1)S(1)} %scale_grads.1.mine), channel_id=1, source_target_pairs={{0,2},{1,3},{2,0},{3,1},{4,6},{5,7},{6,4},{7,5},{8,10},{9,11},{10,... | collective-permute-start | bytes 393224 | tf_op jit(solution)/shard_map/ppermute | solution.py:481
  38.2 1.2 %collective-permute-start.15 = (bf16[256,256]{1,0:T(8,128)(2,1)S(1)}, bf16[256,256]{1,0:T(8,128)(2,1)S(1)}, u32[]{:S(2)}, u32[]{:S(2)}) collective-permute-start(bf16[256,256]{1,0:T(8,128)(2,1)S(1)} %scale_grads.1.mine), channel_id=1, source_target_pairs={{0,8},{1,9},{2,10},{3,11},{4,12},{5,13},{6,14},{7,15},{8,0},{9,1},... | collective-permute-start | bytes 393224 | tf_op jit(solution)/shard_map/ppermute | solution.py:481
  39.4 5.3 %collective-permute-start.14 = (f32[32,256]{1,0:T(8,128)S(1)}, f32[32,256]{1,0:T(8,128)S(1)}, u32[]{:S(2)}, u32[]{:S(2)}) collective-permute-start(f32[32,256]{1,0:T(8,128)S(1)} %add_up.2.here), channel_id=1, source_target_pairs={{224,0},{33,1},{226,2},{35,3},{228,4},{37,5},{230,6},{39,7},{232,8... | collective-permute-start | bytes 98312 | tf_op jit(solution)/shard_map/ppermute | solution.py:493
  44.6 1.0 %collective-permute-done.14.direct = f32[32,256]{1,0:T(8,128)S(1)} collective-permute-done((f32[32,256]{1,0:T(8,128)S(1)}, f32[32,256]{1,0:T(8,128)S(1)}, u32[]{:S(2)}, u32[]{:S(2)}) %collective-permute-start.14) | collective-permute-done | bytes 32800 | tf_op jit(solution)/shard_map/ppermute | solution.py:493
  45.7 2.1 %collective-permute-start.21 = (bf16[2,256,256]{2,1,0:T(8,128)(2,1)S(1)}, bf16[2,256,256]{2,1,0:T(8,128)(2,1)S(1)}, u32[]{:S(2)}, u32[]{:S(2)}) collective-permute-start(bf16[2,256,256]{2,1,0:T(8,128)(2,1)S(1)} %pair.1.mine), channel_id=1, source_target_pairs={{0,1},{1,0},{2,3},{3,2},{4,5},{5,4},{6,7},{7,6},{8,9},{9,8},{10,11... | collective-permute-start | bytes 786440 | tf_op jit(solution)/shard_map/ppermute | solution.py:474
  47.8 1.3 %collective-permute-start.16 = (bf16[2,256,256]{2,1,0:T(8,128)(2,1)S(1)}, bf16[2,256,256]{2,1,0:T(8,128)(2,1)S(1)}, u32[]{:S(2)}, u32[]{:S(2)}) collective-permute-start(bf16[2,256,256]{2,1,0:T(8,128)(2,1)S(1)} %pair.1.mine), channel_id=1, source_target_pairs={{0,12},{1,13},{2,14},{3,15},{4,0},{5,1},{6,2},{7,3},{8,4},{9,5},{1... | collective-permute-start | bytes 786440 | tf_op jit(solution)/shard_map/ppermute | solution.py:481
  49.1 0.2 collective-permute-start.17
  49.3 0.6 collective-permute-start.22
  50.0 1.2 %collective-permute-done.19.swapped = f32[32,256]{1,0:T(8,128)S(1)} collective-permute-done((f32[32,256]{1,0:T(8,128)S(1)}, f32[32,256]{1,0:T(8,128)S(1)}, u32[]{:S(2)}, u32[]{:S(2)}) %collective-permute-start.19) | collective-permute-done | bytes 32800 | tf_op jit(solution)/shard_map/ppermute | solution.py:474
  51.2 1.5 %collective-permute-start.18 = (bf16[256,256]{1,0:T(8,128)(2,1)S(1)}, bf16[256,256]{1,0:T(8,128)(2,1)S(1)}, u32[]{:S(2)}, u32[]{:S(2)}) collective-permute-start(bf16[256,256]{1,0:T(8,128)(2,1)S(1)} %collective-permute-done.15), channel_id=1, source_target_pairs={{0,2},{1,3},{2,0},{3,1},{4,6},{5,7},{6,4},{7,5},{8,10},{9,11},{10,... | collective-permute-start | bytes 393224 | tf_op jit(solution)/shard_map/ppermute | solution.py:481
  52.6 1.6 %collective-permute-start.20 = (f32[32,256]{1,0:T(8,128)S(1)}, f32[32,256]{1,0:T(8,128)S(1)}, u32[]{:S(2)}, u32[]{:S(2)}) collective-permute-start(f32[32,256]{1,0:T(8,128)S(1)} %get-tuple-element.82), channel_id=1, source_target_pairs={{96,0},{161,1},{98,2},{163,3},{100,4},{165,5},{102,6},{167,7},{104... | collective-permute-start | bytes 98312 | tf_op jit(solution)/shard_map/ppermute | solution.py:493
  54.3 1.6 %near_grads.1.refs_3_.refs_4_ = f32[512,1024]{1,0:T(8,128)S(1)} custom-call(s32[10]{0:T(128)S(1)} %place.1, bf16[2,256,256]{2,1,0:T(8,128)(2,1)S(1)} %pair.1.mine, bf16[1,256,256]{2,1,0:T(8,128)(2,1)S(1)} %bitcast.3, bf16[2,256,256]{2,1,0:T(8,128)(2,1)S(1)} %collective-permute-done.21.other, bf16[1,256,256]{2,1,0:T(8,128)(2,1)S(1)} %collective-permute-done.22.other_far, ...), custom_call_target="tpu_custom_call" | custom-call | flops 805306368 | bytes 4980776 | tf_op jit(solution)/shard_map/near_grads/pallas_call | solution.py:31
  55.8 2.9 %collective-permute-done.20.recv = f32[32,256]{1,0:T(8,128)S(1)} collective-permute-done((f32[32,256]{1,0:T(8,128)S(1)}, f32[32,256]{1,0:T(8,128)S(1)}, u32[]{:S(2)}, u32[]{:S(2)}) %collective-permute-start.20) | collective-permute-done | bytes 32800 | tf_op jit(solution)/shard_map/ppermute | solution.py:493
  58.7 0.5 collective-permute-start.23
  59.2 0.1 collective-permute-start.24
  59.3 0.4 collective-permute-start.25
  59.7 0.1 collective-permute-start.26
  59.9 1.4 %far_own.1.refs_3_ = bf16[256,1024]{1,0:T(8,128)(2,1)S(1)} custom-call(s32[10]{0:T(128)S(1)} %place.1, bf16[2,256,256]{2,1,0:T(8,128)(2,1)S(1)} %collective-permute-done.16.refs_0_, bf16[2,256,256]{2,1,0:T(8,128)(2,1)S(1)} %collective-permute-done.17.refs_1_, bf16[1,256,256]{2,1,0:T(8,128)(2,1)S(1)} %bitcast.5, f32[512,1024]{1,0:T(8,128)S(1)} %near_grads.1.refs_3_.refs_4_, ...), custom_call_target="tpu_custom_call" | custom-call | flops 671088640 | bytes 6946856 | tf_op jit(solution)/shard_map/far_own/pallas_call | solution.py:31
  61.4 2.8 %collective-permute-start.27 = (f32[32,256]{1,0:T(8,128)S(1)}, f32[32,256]{1,0:T(8,128)S(1)}, u32[]{:S(2)}, u32[]{:S(2)}) collective-permute-start(f32[32,256]{1,0:T(8,128)S(1)} %add_up.3.here), channel_id=1, source_target_pairs={{0,16},{16,0},{32,48},{48,32},{64,80},{80,64},{96,112},{112,96},{1... | collective-permute-start | bytes 98312 | tf_op jit(solution)/shard_map/ppermute | solution.py:555
  64.2 2.2 %far_grads.1 = bf16[512,1024]{1,0:T(8,128)(2,1)} custom-call(s32[10]{0:T(128)S(1)} %place.1, bf16[2,256,256]{2,1,0:T(8,128)(2,1)S(1)} %collective-permute-done.23.refs_0_, bf16[2,256,256]{2,1,0:T(8,128)(2,1)S(1)} %collective-permute-done.24.refs_1_, bf16[1,256,256]{2,1,0:T(8,128)(2,1)S(1)} %collective-permute-done.25.refs_2_, ...), custom_call_target="tpu_custom_call" | custom-call | flops 671088640 | bytes 7471144 | tf_op jit(solution)/shard_map/far_grads/pallas_call | solution.py:31
  66.4 0.7 %tenant_totals.1 = (f32[32,64]{1,0:T(8,128)}, f32[32,64]{1,0:T(8,128)}) custom-call(f32[32,256]{1,0:T(8,128)S(1)} %add_up.3.here, f32[32,256]{1,0:T(8,128)S(1)} %collective-permute-done.27.recv), custom_call_target="tpu_custom_call" | custom-call | tf_op jit(solution)/shard_map/tenant_totals/pallas_call | solution.py:465
  (26 shorter events, 0.1 us)
Async XLA Ops:
  3.6 6.4 %collective-permute-start = (f32[256,1024]{1,0:T(8,128)S(1)}, f32[256,1024]{1,0:T(8,128)S(1)}, u32[]{:S(2)}, u32[]{:S(2)}) collective-permute-start(f32[256,1024]{1,0:T(8,128)S(1)} %get-tuple-element.56), channel_id=1, source_target_pairs={{0,1},{1,0},{2,3},{3,2},{4,5},{5,4},{6,7},{7,6},{8,9},{9,8},{10,11... | collective-permute-start | bytes 3145736 | tf_op jit(solution)/shard_map/ppermute | solution.py:474
  7.7 2.3 %collective-permute-start.1 = (bf16[256,1024]{1,0:T(8,128)(2,1)S(1)}, bf16[256,1024]{1,0:T(8,128)(2,1)S(1)}, u32[]{:S(2)}, u32[]{:S(2)}) collective-permute-start(bf16[256,1024]{1,0:T(8,128)(2,1)S(1)} %project_value.1), channel_id=1, source_target_pairs={{0,1},{1,0},{2,3},{3,2},{4,5},{5,4},{6,7},{7,6},{8,9},{9,8},{10,11... | collective-permute-start | bytes 1572872 | tf_op jit(solution)/shard_map/ppermute | solution.py:474
  10.2 7.4 %collective-permute-start.6 = (bf16[256,384]{1,0:T(8,128)(2,1)S(1)}, bf16[256,384]{1,0:T(8,128)(2,1)S(1)}, u32[]{:S(2)}, u32[]{:S(2)}) collective-permute-start(bf16[256,384]{1,0:T(8,128)(2,1)S(1)} %get-tuple-element.62), channel_id=1, source_target_pairs={{0,4},{1,5},{2,6},{3,7},{4,8},{5,9},{6,10},{7,11},{8,12},{9,13},{1... | collective-permute-start | bytes 589832 | tf_op jit(solution)/shard_map/ppermute | solution.py:481
  10.3 7.3 %collective-permute-start.7 = (bf16[256,384]{1,0:T(8,128)(2,1)S(1)}, bf16[256,384]{1,0:T(8,128)(2,1)S(1)}, u32[]{:S(2)}, u32[]{:S(2)}) collective-permute-start(bf16[256,384]{1,0:T(8,128)(2,1)S(1)} %get-tuple-element.63), channel_id=1, source_target_pairs={{0,12},{1,13},{2,14},{3,15},{4,0},{5,1},{6,2},{7,3},{8,4},{9,5},{1... | collective-permute-start | bytes 589832 | tf_op jit(solution)/shard_map/ppermute | solution.py:481
  12.9 5.5 %collective-permute-start.4 = (bf16[256,384]{1,0:T(8,128)(2,1)S(1)}, bf16[256,384]{1,0:T(8,128)(2,1)S(1)}, u32[]{:S(2)}, u32[]{:S(2)}) collective-permute-start(bf16[256,384]{1,0:T(8,128)(2,1)S(1)} %get-tuple-element.60), channel_id=1, source_target_pairs={{0,2},{1,3},{2,0},{3,1},{4,6},{5,7},{6,4},{7,5},{8,10},{9,11},{10,... | collective-permute-start | bytes 589832 | tf_op jit(solution)/shard_map/ppermute | solution.py:481
  13.3 8.9 %collective-permute-start.2 = (bf16[256,384]{1,0:T(8,128)(2,1)S(1)}, bf16[256,384]{1,0:T(8,128)(2,1)S(1)}, u32[]{:S(2)}, u32[]{:S(2)}) collective-permute-start(bf16[256,384]{1,0:T(8,128)(2,1)S(1)} %get-tuple-element.57), channel_id=1, source_target_pairs={{0,4},{1,5},{2,6},{3,7},{4,8},{5,9},{6,10},{7,11},{8,12},{9,13},{1... | collective-permute-start | bytes 589832 | tf_op jit(solution)/shard_map/ppermute | solution.py:481
  13.4 8.8 %collective-permute-start.3 = (bf16[256,384]{1,0:T(8,128)(2,1)S(1)}, bf16[256,384]{1,0:T(8,128)(2,1)S(1)}, u32[]{:S(2)}, u32[]{:S(2)}) collective-permute-start(bf16[256,384]{1,0:T(8,128)(2,1)S(1)} %get-tuple-element.58), channel_id=1, source_target_pairs={{0,12},{1,13},{2,14},{3,15},{4,0},{5,1},{6,2},{7,3},{8,4},{9,5},{1... | collective-permute-start | bytes 589832 | tf_op jit(solution)/shard_map/ppermute | solution.py:481
  17.7 4.9 %collective-permute-start.8 = (bf16[256,384]{1,0:T(8,128)(2,1)S(1)}, bf16[256,384]{1,0:T(8,128)(2,1)S(1)}, u32[]{:S(2)}, u32[]{:S(2)}) collective-permute-start(bf16[256,384]{1,0:T(8,128)(2,1)S(1)} %relay.3), channel_id=1, source_target_pairs={{0,2},{1,3},{2,0},{3,1},{4,6},{5,7},{6,4},{7,5},{8,10},{9,11},{10,... | collective-permute-start | bytes 589832 | tf_op jit(solution)/shard_map/ppermute | solution.py:481
  18.5 2.4 %copy-start.4 = (s32[1,512]{1,0:T(1,128)S(1)}, s32[1,512]{1,0:T(1,128)}, u32[]{:S(2)}) copy-start(s32[1,512]{1,0:T(1,128)} %segments.1) | copy-start | bytes 6148
  18.5 2.4 %copy-start.5 = (s32[1,4]{1,0:T(1,128)S(1)}, s32[1,4]{1,0:T(1,128)}, u32[]{:S(2)}) copy-start(s32[1,4]{1,0:T(1,128)} %tenants.1) | copy-start | bytes 52
  18.5 6.2 %copy-start.2 = (f32[32,1024]{1,0:T(8,128)S(1)}, f32[32,1024]{1,0:T(8,128)}, u32[]{:S(2)}) copy-start(f32[32,1024]{1,0:T(8,128)} %key_scale.1) | copy-start | bytes 393220
  18.5 6.2 %copy-start.3 = (f32[32,1024]{1,0:T(8,128)S(1)}, f32[32,1024]{1,0:T(8,128)}, u32[]{:S(2)}) copy-start(f32[32,1024]{1,0:T(8,128)} %value_scale.1) | copy-start | bytes 393220
  18.5 11.0 %copy-start = (bf16[512,1024]{1,0:T(8,128)(2,1)S(1)}, bf16[512,1024]{1,0:T(8,128)(2,1)}, u32[]{:S(2)}) copy-start(bf16[512,1024]{1,0:T(8,128)(2,1)} %queries.1) | copy-start | bytes 3145732
  18.5 11.0 %copy-start.1 = (bf16[512,1024]{1,0:T(8,128)(2,1)S(1)}, bf16[512,1024]{1,0:T(8,128)(2,1)}, u32[]{:S(2)}) copy-start(bf16[512,1024]{1,0:T(8,128)(2,1)} %out_grad.1) | copy-start | bytes 3145732
  18.5 6.1 %collective-permute-start.5 = (bf16[256,384]{1,0:T(8,128)(2,1)S(1)}, bf16[256,384]{1,0:T(8,128)(2,1)S(1)}, u32[]{:S(2)}, u32[]{:S(2)}) collective-permute-start(bf16[256,384]{1,0:T(8,128)(2,1)S(1)} %relay.2), channel_id=1, source_target_pairs={{0,8},{1,9},{2,10},{3,11},{4,12},{5,13},{6,14},{7,15},{8,0},{9,1},... | collective-permute-start | bytes 589832 | tf_op jit(solution)/shard_map/ppermute | solution.py:481
  25.4 4.1 %collective-permute-start.9 = (bf16[256,256]{1,0:T(8,128)(2,1)S(1)}, bf16[256,256]{1,0:T(8,128)(2,1)S(1)}, u32[]{:S(2)}, u32[]{:S(2)}) collective-permute-start(bf16[256,256]{1,0:T(8,128)(2,1)S(1)} %get-tuple-element.70.mine), channel_id=1, source_target_pairs={{0,1},{1,0},{2,3},{3,2},{4,5},{5,4},{6,7},{7,6},{8,9},{9,8},{10,11... | collective-permute-start | bytes 393224 | tf_op jit(solution)/shard_map/ppermute | solution.py:474
  28.5 6.0 %collective-permute-start.11 = (f32[256,256]{1,0:T(8,128)S(1)}, f32[256,256]{1,0:T(8,128)S(1)}, u32[]{:S(2)}, u32[]{:S(2)}) collective-permute-start(f32[256,256]{1,0:T(8,128)S(1)} %get-tuple-element.73.base), channel_id=1, source_target_pairs={{0,1},{1,0},{2,3},{3,2},{4,5},{5,4},{6,7},{7,6},{8,9},{9,8},{10,11... | collective-permute-start | bytes 786440 | tf_op jit(solution)/shard_map/ppermute | solution.py:474
  34.1 1.6 %collective-permute-start.10 = (f32[256,256]{1,0:T(8,128)S(1)}, f32[256,256]{1,0:T(8,128)S(1)}, u32[]{:S(2)}, u32[]{:S(2)}) collective-permute-start(f32[256,256]{1,0:T(8,128)S(1)} %get-tuple-element.72.send), channel_id=1, source_target_pairs={{0,1},{1,0},{2,3},{3,2},{4,5},{5,4},{6,7},{7,6},{8,9},{9,8},{10,11... | collective-permute-start | bytes 786440 | tf_op jit(solution)/shard_map/ppermute | solution.py:474
  35.7 1.2 %collective-permute-start.12 = (f32[32,256]{1,0:T(8,128)S(1)}, f32[32,256]{1,0:T(8,128)S(1)}, u32[]{:S(2)}, u32[]{:S(2)}) collective-permute-start(f32[32,256]{1,0:T(8,128)S(1)} %tenant_table.1.refs_0_), channel_id=1, source_target_pairs={{0,1},{1,0},{2,3},{3,2},{4,5},{5,4},{6,7},{7,6},{8,9},{9,8},{10,11... | collective-permute-start | bytes 98312 | tf_op jit(solution)/shard_map/ppermute | solution.py:474
  36.9 8.7 %collective-permute-start.13 = (bf16[256,256]{1,0:T(8,128)(2,1)S(1)}, bf16[256,256]{1,0:T(8,128)(2,1)S(1)}, u32[]{:S(2)}, u32[]{:S(2)}) collective-permute-start(bf16[256,256]{1,0:T(8,128)(2,1)S(1)} %scale_grads.1.mine), channel_id=1, source_target_pairs={{0,2},{1,3},{2,0},{3,1},{4,6},{5,7},{6,4},{7,5},{8,10},{9,11},{10,... | collective-permute-start | bytes 393224 | tf_op jit(solution)/shard_map/ppermute | solution.py:481
  38.2 7.5 %collective-permute-start.15 = (bf16[256,256]{1,0:T(8,128)(2,1)S(1)}, bf16[256,256]{1,0:T(8,128)(2,1)S(1)}, u32[]{:S(2)}, u32[]{:S(2)}) collective-permute-start(bf16[256,256]{1,0:T(8,128)(2,1)S(1)} %scale_grads.1.mine), channel_id=1, source_target_pairs={{0,8},{1,9},{2,10},{3,11},{4,12},{5,13},{6,14},{7,15},{8,0},{9,1},... | collective-permute-start | bytes 393224 | tf_op jit(solution)/shard_map/ppermute | solution.py:481
  39.4 6.3 %collective-permute-start.14 = (f32[32,256]{1,0:T(8,128)S(1)}, f32[32,256]{1,0:T(8,128)S(1)}, u32[]{:S(2)}, u32[]{:S(2)}) collective-permute-start(f32[32,256]{1,0:T(8,128)S(1)} %add_up.2.here), channel_id=1, source_target_pairs={{224,0},{33,1},{226,2},{35,3},{228,4},{37,5},{230,6},{39,7},{232,8... | collective-permute-start | bytes 98312 | tf_op jit(solution)/shard_map/ppermute | solution.py:493
  45.7 8.6 %collective-permute-start.21 = (bf16[2,256,256]{2,1,0:T(8,128)(2,1)S(1)}, bf16[2,256,256]{2,1,0:T(8,128)(2,1)S(1)}, u32[]{:S(2)}, u32[]{:S(2)}) collective-permute-start(bf16[2,256,256]{2,1,0:T(8,128)(2,1)S(1)} %pair.1.mine), channel_id=1, source_target_pairs={{0,1},{1,0},{2,3},{3,2},{4,5},{5,4},{6,7},{7,6},{8,9},{9,8},{10,11... | collective-permute-start | bytes 786440 | tf_op jit(solution)/shard_map/ppermute | solution.py:474
  47.8 10.9 %collective-permute-start.16 = (bf16[2,256,256]{2,1,0:T(8,128)(2,1)S(1)}, bf16[2,256,256]{2,1,0:T(8,128)(2,1)S(1)}, u32[]{:S(2)}, u32[]{:S(2)}) collective-permute-start(bf16[2,256,256]{2,1,0:T(8,128)(2,1)S(1)} %pair.1.mine), channel_id=1, source_target_pairs={{0,12},{1,13},{2,14},{3,15},{4,0},{5,1},{6,2},{7,3},{8,4},{9,5},{1... | collective-permute-start | bytes 786440 | tf_op jit(solution)/shard_map/ppermute | solution.py:481
  49.1 9.6 %collective-permute-start.17 = (bf16[2,256,256]{2,1,0:T(8,128)(2,1)S(1)}, bf16[2,256,256]{2,1,0:T(8,128)(2,1)S(1)}, u32[]{:S(2)}, u32[]{:S(2)}) collective-permute-start(bf16[2,256,256]{2,1,0:T(8,128)(2,1)S(1)} %pair.1.mine), channel_id=1, source_target_pairs={{0,4},{1,5},{2,6},{3,7},{4,8},{5,9},{6,10},{7,11},{8,12},{9,13},{1... | collective-permute-start | bytes 786440 | tf_op jit(solution)/shard_map/ppermute | solution.py:481
  49.3 3.3 %collective-permute-start.22 = (bf16[1,256,256]{2,1,0:T(8,128)(2,1)S(1)}, bf16[1,256,256]{2,1,0:T(8,128)(2,1)S(1)}, u32[]{:S(2)}, u32[]{:S(2)}) collective-permute-start(bf16[1,256,256]{2,1,0:T(8,128)(2,1)S(1)} %bitcast.2), channel_id=1, source_target_pairs={{0,1},{1,0},{2,3},{3,2},{4,5},{5,4},{6,7},{7,6},{8,9},{9,8},{10,11... | collective-permute-start | bytes 393224 | tf_op jit(solution)/shard_map/ppermute | solution.py:474
  49.9 1.2 %collective-permute-start.19 = (f32[32,256]{1,0:T(8,128)S(1)}, f32[32,256]{1,0:T(8,128)S(1)}, u32[]{:S(2)}, u32[]{:S(2)}) collective-permute-start(f32[32,256]{1,0:T(8,128)S(1)} %collective-permute-done.14.direct), channel_id=1, source_target_pairs={{0,1},{1,0},{2,3},{3,2},{4,5},{5,4},{6,7},{7,6},{8,9},{9,8},{10,11... | collective-permute-start | bytes 98312 | tf_op jit(solution)/shard_map/ppermute | solution.py:474
  51.2 7.6 %collective-permute-start.18 = (bf16[256,256]{1,0:T(8,128)(2,1)S(1)}, bf16[256,256]{1,0:T(8,128)(2,1)S(1)}, u32[]{:S(2)}, u32[]{:S(2)}) collective-permute-start(bf16[256,256]{1,0:T(8,128)(2,1)S(1)} %collective-permute-done.15), channel_id=1, source_target_pairs={{0,2},{1,3},{2,0},{3,1},{4,6},{5,7},{6,4},{7,5},{8,10},{9,11},{10,... | collective-permute-start | bytes 393224 | tf_op jit(solution)/shard_map/ppermute | solution.py:481
  52.6 6.1 %collective-permute-start.20 = (f32[32,256]{1,0:T(8,128)S(1)}, f32[32,256]{1,0:T(8,128)S(1)}, u32[]{:S(2)}, u32[]{:S(2)}) collective-permute-start(f32[32,256]{1,0:T(8,128)S(1)} %get-tuple-element.82), channel_id=1, source_target_pairs={{96,0},{161,1},{98,2},{163,3},{100,4},{165,5},{102,6},{167,7},{104... | collective-permute-start | bytes 98312 | tf_op jit(solution)/shard_map/ppermute | solution.py:493
  58.7 2.6 %collective-permute-start.23 = (bf16[2,256,256]{2,1,0:T(8,128)(2,1)S(1)}, bf16[2,256,256]{2,1,0:T(8,128)(2,1)S(1)}, u32[]{:S(2)}, u32[]{:S(2)}) collective-permute-start(bf16[2,256,256]{2,1,0:T(8,128)(2,1)S(1)} %collective-permute-done.16.refs_0_), channel_id=1, source_target_pairs={{0,1},{1,0},{2,3},{3,2},{4,5},{5,4},{6,7},{7,6},{8,9},{9,8},{10,11... | collective-permute-start | bytes 786440 | tf_op jit(solution)/shard_map/ppermute | solution.py:474
  59.2 2.1 %collective-permute-start.24 = (bf16[2,256,256]{2,1,0:T(8,128)(2,1)S(1)}, bf16[2,256,256]{2,1,0:T(8,128)(2,1)S(1)}, u32[]{:S(2)}, u32[]{:S(2)}) collective-permute-start(bf16[2,256,256]{2,1,0:T(8,128)(2,1)S(1)} %collective-permute-done.17.refs_1_), channel_id=1, source_target_pairs={{0,1},{1,0},{2,3},{3,2},{4,5},{5,4},{6,7},{7,6},{8,9},{9,8},{10,11... | collective-permute-start | bytes 786440 | tf_op jit(solution)/shard_map/ppermute | solution.py:474
  59.3 2.0 %collective-permute-start.25 = (bf16[1,256,256]{2,1,0:T(8,128)(2,1)S(1)}, bf16[1,256,256]{2,1,0:T(8,128)(2,1)S(1)}, u32[]{:S(2)}, u32[]{:S(2)}) collective-permute-start(bf16[1,256,256]{2,1,0:T(8,128)(2,1)S(1)} %bitcast.4), channel_id=1, source_target_pairs={{0,1},{1,0},{2,3},{3,2},{4,5},{5,4},{6,7},{7,6},{8,9},{9,8},{10,11... | collective-permute-start | bytes 393224 | tf_op jit(solution)/shard_map/ppermute | solution.py:474
  59.7 1.6 %collective-permute-start.26 = (f32[32,256]{1,0:T(8,128)S(1)}, f32[32,256]{1,0:T(8,128)S(1)}, u32[]{:S(2)}, u32[]{:S(2)}) collective-permute-start(f32[32,256]{1,0:T(8,128)S(1)} %ring_end.1.refs_0_), channel_id=1, source_target_pairs={{0,1},{1,0},{2,3},{3,2},{4,5},{5,4},{6,7},{7,6},{8,9},{9,8},{10,11... | collective-permute-start | bytes 98312 | tf_op jit(solution)/shard_map/ppermute | solution.py:474
  61.4 5.0 %collective-permute-start.27 = (f32[32,256]{1,0:T(8,128)S(1)}, f32[32,256]{1,0:T(8,128)S(1)}, u32[]{:S(2)}, u32[]{:S(2)}) collective-permute-start(f32[32,256]{1,0:T(8,128)S(1)} %add_up.3.here), channel_id=1, source_target_pairs={{0,16},{16,0},{32,48},{48,32},{64,80},{80,64},{96,112},{112,96},{1... | collective-permute-start | bytes 98312 | tf_op jit(solution)/shard_map/ppermute | solution.py:555
